TPU v7x, 32 devices: a whole 2x2x4 slice. The times are simulated.
32 devices in a mesh: shots: 2 (over y), depth: 4 (over z), row: 4 (over x, core).
Axes of the slice: x: 2, y: 2, z: 4, core: 2. Of those that a mesh axis runs over, the one named last changes fastest.
Arguments:
- waves: float32 [8, 2, 512, 2, 1, 512], P(('shots', 'depth'), None, 'row'), parts along dimension 0, may hold values from -6 to 6
- slab_freq: float32 [8, 1], P(('shots', 'depth')), parts along dimension 0, may hold values from 1.2 to 2.4
- slowness: float32 [4, 512, 512], P('depth', 'row'), may hold values from 0.8 to 1.25
- ref_slow: float32 [4], P('depth'), may hold values from 0.9 to 1.1
- inj_freq: float32 [2, 1], P('shots'), parts along dimension 0, may hold values from 1.2 to 2.4
- wavelet: float32 [2, 1, 2], P('shots'), parts along dimension 0, may hold values from -64 to 64
- records: float32 [2, 1, 2, 4096], P('shots'), parts along dimension 0, may hold values from -6 to 6
- src_pos: int32 [4], P('shots'), parts along dimension 0, may hold values from 0 to 511
- rcv_pos: int32 [8192, 2], P('shots'), parts along dimension 0, may hold values from 0 to 511
Outputs:
- wave_out: float32 [8, 2, 512, 2, 1, 512], P(('shots', 'depth'), None, 'row'), parts along dimension 0
- image: float32 [8, 16, 512, 512], P(('shots', 'depth'), None, 'row'), parts along dimension 0
There are 2 independent parts, one for each index of `shots`. A program takes and returns all parts, laid end to end along the dimension named above; an argument that names none is the same for every part. Nothing has to cross between parts.
All inputs are finite; a program needn't handle non-finite values.
Results may differ from a plain program's by a relative error of at most 0.0003.
Values sent between devices are 32-bit elements; how exact they have to be, the bound alone decides.
No kernel may reach another device: no remote copies, remote signals or barrier semaphores. Data moves between devices by JAX's collectives and lax.ppermute only.
A program may use at most 128 MiB of HBM per device.

v0:
```python
import functools
import math

import jax
import jax.numpy as jnp
import ml_dtypes
import numpy as np
from jax import lax
from jax.experimental import pallas as pl
from jax.experimental.pallas import tpu as pltpu
from jax.sharding import PartitionSpec as P

OFF = 16
HALF = OFF // 2
DZ = 4
LANES = 128
MIB = 1024 * 1024

F32 = jnp.float32
BF16 = jnp.bfloat16


def wave_order(length):
    place = np.arange(length)
    half = length // 2
    return np.where(place < half, 2 * place, 2 * (place - half) + 1)


def two_parts(table):
    high = table.astype(ml_dtypes.bfloat16)
    low = (table - high.astype(np.float64)).astype(ml_dtypes.bfloat16)
    return np.stack([high, low])


@functools.lru_cache(maxsize=None)
def tables(length, slices):
    half, cols = length // 2, length // slices
    product = wave_order(length)[:, None] * np.arange(half)[None, :] % length
    angle = product * (2.0 * math.pi / length)
    pair = np.stack([np.cos(angle), np.sin(angle)])
    by_parity = pair.reshape(2, 2, half, half)
    x_forward = by_parity.transpose(1, 0, 2, 3).reshape(2, 2 * half, half)
    x_inverse = by_parity.transpose(1, 0, 3, 2).reshape(2, 2 * half, half)
    y_inverse = pair.reshape(2, slices, cols, half)
    y_forward = y_inverse.transpose(0, 1, 3, 2)
    return tuple(two_parts(t) for t in (x_forward, x_inverse, y_forward, y_inverse))


def parts_of(value):
    high = value.astype(BF16)
    return high, (value - high.astype(F32)).astype(BF16)


def dot(a, b):
    return jnp.dot(a, b, preferred_element_type=F32)


def sin_cos(angle):
    turns = jnp.floor(angle * (2.0 / math.pi) + 0.5)
    rest = angle - turns * 1.5703125
    rest = rest - turns * 4.837512969970703125e-4
    rest = rest - turns * 7.54978995489188216e-8
    square = rest * rest
    sine = rest + rest * square * (
        -1.6666654611e-1 + square * (8.3321608736e-3 - square * 1.9515295891e-4)
    )
    cosine = 1.0 + square * (
        -0.5
        + square * (4.166664568298827e-2 + square * (-1.388731625493765e-3 + square * 2.443315711809948e-5))
    )
    quarter = turns.astype(jnp.int32)
    swap = (quarter & 1) == 1
    sine_out = jnp.where(swap, cosine, sine)
    cosine_out = jnp.where(swap, sine, cosine)
    sine_out = jnp.where((quarter & 2) == 2, -sine_out, sine_out)
    cosine_out = jnp.where(((quarter + 1) & 2) == 2, -cosine_out, cosine_out)
    return sine_out, cosine_out


def along_y(real, imag, table, index, inverse):
    rows = real.shape[0]
    real_high, real_low = parts_of(real)
    imag_high, imag_low = parts_of(imag)
    stacked = jnp.concatenate([real_high, imag_high, real_low, imag_low], axis=0)
    products = []
    for which in range(2):
        both = dot(stacked, table[0, which, index])
        products.append(
            both[: 2 * rows] + (both[2 * rows :] + dot(stacked[: 2 * rows], table[1, which, index]))
        )
    cosines, sines = products
    if inverse:
        return cosines[:rows] - sines[rows:], cosines[rows:] + sines[:rows]
    return cosines[:rows] + sines[rows:], cosines[rows:] - sines[:rows]


def along_x(real, imag, table, parity, inverse):
    half = real.shape[0]
    products = []
    for value in (real, imag):
        high, low = parts_of(value)
        products.append(
            dot(table[0, parity], high)
            + (dot(table[0, parity], low) + dot(table[1, parity], high))
        )
    by_real, by_imag = products
    if inverse:
        return by_real[:half] - by_imag[half:], by_imag[:half] + by_real[half:]
    return by_real[:half] + by_imag[half:], by_imag[:half] - by_real[half:]


class Layout:
    def __init__(self, ranks, groups, rows, lateral):
        self.ranks, self.groups, self.rows, self.lateral = ranks, groups, rows, lateral
        self.slices = ranks // 2
        self.half = lateral // 2
        self.cols = lateral // self.slices
        self.chunks = lateral // LANES

    def place(self):
        rank = lax.axis_index("row")
        return rank % self.slices, rank // self.slices


def first_kernel(lay, *refs):
    waves, y_forward = refs[:2]
    pieces = refs[2 : 2 + lay.ranks]
    parity_parts = refs[-1]
    index, side = lay.place()
    middle = lay.chunks // 2
    for field in range(2):
        for part in range(2):
            chunks = [
                waves[
                    pl.ds(
                        (part * lay.rows * 2 + field) * lay.chunks + chunk,
                        lay.rows,
                        stride=2 * lay.chunks,
                    ),
                    :,
                ]
                for chunk in range(lay.chunks)
            ]
            low = jnp.concatenate(chunks[:middle], axis=1)
            high = jnp.concatenate(chunks[middle:], axis=1)
            parity_parts[2 * field, part] = low + high
            parity_parts[2 * field + 1, part] = low - high
    for step in reversed(range(lay.ranks)):
        piece_slice = index ^ (step % lay.slices)
        field = side ^ (step // lay.slices)
        at = 2 * field + piece_slice // (lay.slices // 2)
        real, imag = along_y(
            parity_parts[at, 0], parity_parts[at, 1], y_forward, piece_slice, False
        )
        pieces[step][0] = real
        pieces[step][1] = imag


def column_kernel(lay, first, *refs):
    count_in = lay.ranks if first else lay.slices
    count_out = lay.slices if first else lay.ranks
    pieces = refs[:count_in]
    phase, x_forward, x_inverse = refs[count_in : count_in + 3]
    results = refs[count_in + 3 : count_in + 3 + count_out]
    parity_parts, halves = refs[-2:]
    index, side = lay.place()
    sign = (1 - 2 * side).astype(F32)
    for step in range(lay.slices):
        at = pl.ds(pl.multiple_of((index ^ step) * lay.rows, lay.rows), lay.rows)
        for part in range(2):
            if first:
                low, high = pieces[step][part], pieces[step + lay.slices][part]
                difference = (low - high) * sign
            else:
                low, high = pieces[step][0, part], pieces[step][1, part]
                difference = low - high
            parity_parts[0, part, at, :] = low + high
            parity_parts[1, part, at, :] = difference
    sums = []
    for parity in range(2):
        real, imag = along_x(
            parity_parts[parity, 0], parity_parts[parity, 1], x_forward, parity, False
        )
        phase_real, phase_imag = phase[0, parity], phase[1, parity]
        sums.append(
            along_x(
                real * phase_real - imag * phase_imag,
                real * phase_imag + imag * phase_real,
                x_inverse,
                parity,
                True,
            )
        )
    for part in range(2):
        halves[0, part] = sums[0][part] + sums[1][part]
        halves[1, part] = sums[0][part] - sums[1][part]
    for step in range(count_out):
        block = (index ^ (step % lay.slices)) * lay.rows
        at = pl.ds(pl.multiple_of(block, lay.rows), lay.rows)
        for part in range(2):
            if first:
                for upper in range(2):
                    results[step][upper, part] = halves[upper, part, at, :]
            else:
                results[step][part] = halves[side ^ (step // lay.slices), part, at, :]


def rows_from(lay, pieces, y_inverse, index):
    low, high = None, None
    for step, (real, imag) in enumerate(pieces):
        piece_slice = index ^ step
        sign = (1 - 2 * (piece_slice // (lay.slices // 2))).astype(F32)
        part = along_y(real, imag, y_inverse, piece_slice, True)
        turned = [value * sign for value in part]
        low = part if low is None else [a + b for a, b in zip(low, part)]
        high = turned if high is None else [a + b for a, b in zip(high, turned)]
    return low, high


def middle_kernel(lay, *refs):
    pieces = refs[: lay.slices]
    lens, injected, y_inverse, y_forward = refs[lay.slices : lay.slices + 4]
    own, other = refs[lay.slices + 4 : lay.slices + 6]
    results = refs[lay.slices + 6 : 2 * lay.slices + 6]
    fields, parity_parts = refs[-2:]
    index, side = lay.place()
    last = lax.axis_index("depth") == lay.groups - 1
    both = 2 * lay.rows
    low, high = rows_from(
        lay,
        [[piece[:, part].reshape(both, lay.cols) for part in range(2)] for piece in pieces],
        y_inverse,
        index,
    )
    for end, (real, imag) in enumerate((low, high)):
        lanes = pl.ds(end * lay.half, lay.half)
        cosine = lens[0, :, :, lanes].reshape(both, lay.half)
        sine = lens[1, :, :, lanes].reshape(both, lay.half)
        shape = (2, lay.rows, lay.half)
        fields[:, 0, :, lanes] = (real * cosine - imag * sine).reshape(shape)
        fields[:, 1, :, lanes] = (real * sine + imag * cosine).reshape(shape)
    for part in range(2):
        own[part] = fields[side, part]
        other[part] = fields[1 - side, part]
    for part in range(2):
        ends = []
        for end in range(2):
            lanes = pl.ds(end * lay.half, lay.half)
            value = jnp.where(last, injected[part, :, :, lanes], fields[:, part, :, lanes])
            ends.append(value.reshape(both, lay.half))
        parity_parts[0, part] = ends[0] + ends[1]
        parity_parts[1, part] = ends[0] - ends[1]
    for step in range(lay.slices):
        piece_slice = index ^ step
        at = piece_slice // (lay.slices // 2)
        pair = along_y(parity_parts[at, 0], parity_parts[at, 1], y_forward, piece_slice, False)
        for part in range(2):
            results[step][:, part] = pair[part].reshape(2, lay.rows, lay.cols)


def last_kernel(lay, *refs):
    pieces = refs[: lay.ranks]
    lens, y_inverse = refs[lay.ranks : lay.ranks + 2]
    wave_out, own, other, leading, trailing = refs[lay.ranks + 2 : lay.ranks + 7]
    fields = refs[-1]
    index, side = lay.place()
    for turn, result in enumerate((own, other)):
        field = side ^ turn
        low, high = rows_from(
            lay,
            [
                [piece[0], piece[1]]
                for piece in pieces[turn * lay.slices : (turn + 1) * lay.slices]
            ],
            y_inverse,
            index,
        )
        sign = (1 - 2 * field).astype(F32)
        for end, (real, imag) in enumerate((low, high)):
            lanes = pl.ds(end * lay.half, lay.half)
            cosine, sine = lens[0, :, lanes], lens[1, :, lanes] * sign
            result[0, :, lanes] = real * cosine - imag * sine
            result[1, :, lanes] = real * sine + imag * cosine
        for part in range(2):
            fields[field, part] = result[part]
            leading[turn, part] = result[part, :HALF]
            trailing[turn, part] = result[part, lay.rows - HALF :]
    for field in range(2):
        for part in range(2):
            for chunk in range(lay.chunks):
                start = (part * lay.rows * 2 + field) * lay.chunks + chunk
                wave_out[pl.ds(start, lay.rows, stride=2 * lay.chunks), :] = fields[
                    field, part, :, pl.ds(chunk * LANES, LANES)
                ]


def image_kernel(lay, adds, *refs):
    own, other, before, after = refs[:4]
    result, padded = refs[-2:]
    rank = lax.axis_index("row")
    side = rank // lay.slices
    side_before = (rank + lay.ranks - 1) % lay.ranks // lay.slices
    side_after = (rank + 1) % lay.ranks // lay.slices
    end = HALF + lay.rows
    for part in range(2):
        padded[side, part, HALF:end] = own[part]
        padded[1 - side, part, HALF:end] = other[part]
        for field in range(2):
            padded[field, part, :HALF] = before[field ^ side_before, part]
            padded[field, part, end:] = after[field ^ side_after, part]
    for offset in range(OFF):
        lag = offset - HALF
        source = pl.ds(HALF - lag, lay.rows)
        receiver = pl.ds(HALF + lag, lay.rows)
        value = (
            padded[0, 0, source] * padded[1, 0, receiver]
            + padded[0, 1, source] * padded[1, 1, receiver]
        )
        result[offset] = refs[4][offset] + value if adds else value


def prepare_kernel(lay, freq, freq_injected, ref_own, ref_next, source_at, wavelet, records, receivers, phase_a, phase_b, injected, sums):
    index, side = lay.place()
    last = lax.axis_index("depth") == lay.groups - 1
    shape = (lay.half, lay.cols)
    spacing = 2.0 * math.pi / lay.lateral

    def squares(even_odd):
        signed = jnp.where(even_odd < lay.half, even_odd, even_odd - lay.lateral)
        number = signed.astype(F32) * spacing
        return number * number

    place = lax.broadcasted_iota(jnp.int32, shape, 1) + index * lay.cols
    y_squares = squares(jnp.where(place < lay.half, 2 * place, 2 * (place - lay.half) + 1))
    scale = 1.0 / (lay.lateral * lay.lateral)
    sign = (1 - 2 * side).astype(F32) * scale
    wave_numbers = (
        freq[0, 0] * ref_own[0],
        jnp.where(last, freq_injected[0, 0], freq[0, 0]) * ref_next[0],
    )
    for parity in range(2):
        x_squares = squares(2 * lax.broadcasted_iota(jnp.int32, shape, 0) + parity)
        lateral_squares = x_squares + y_squares
        for number, phase in zip(wave_numbers, (phase_a, phase_b)):
            vertical = number * number - lateral_squares
            argument = jnp.sqrt(jnp.abs(vertical)) * DZ
            sine, cosine = sin_cos(argument)
            runs = vertical > 0
            phase[0, parity] = jnp.where(runs, cosine, jnp.exp(-argument)) * scale
            phase[1, parity] = jnp.where(runs, sine, 0.0) * sign

    count = receivers.shape[1]
    width = next((w for w in (1024, 512, 256, 128) if count % w == 0), count)
    both = 2 * lay.rows
    is_source = side == 0
    row = lax.broadcasted_iota(jnp.int32, (both, width), 0)
    row = row + index * lay.rows + jnp.where(row >= lay.rows, (lay.slices - 1) * lay.rows, 0)
    column = lax.broadcasted_iota(jnp.int32, (lay.lateral, width), 0)
    for start in range(0, count, width):
        lanes = pl.ds(start, width)
        is_first = lax.broadcasted_iota(jnp.int32, (1, width), 1) + start == 0
        at_row = jnp.where(
            is_source, jnp.where(is_first, source_at[0], -1), receivers[0:1, lanes]
        )
        at_column = jnp.where(is_source, source_at[1], receivers[1:2, lanes])
        hit = row == at_row
        stacked = []
        for part in range(2):
            value = jnp.where(is_source, wavelet[0, part], records[part : part + 1, lanes])
            high = value.astype(BF16).astype(F32)
            for piece in (high, value - high):
                stacked.append(jnp.where(hit, piece, 0.0).astype(BF16))
        picked = jnp.where(column == at_column, 1.0, 0.0).astype(BF16)
        found = lax.dot_general(
            jnp.concatenate(stacked, axis=0),
            picked,
            (((1,), (1,)), ((), ())),
            preferred_element_type=F32,
        )
        sums[...] = found if start == 0 else sums[...] + found
    for part in range(2):
        at = 2 * part * both
        value = sums[at : at + both] + sums[at + both : at + 2 * both]
        injected[part] = value.reshape(2, lay.rows, lay.lateral)


def lens_kernel(lay, freq, ref_own, slow_own, slow_other, lens):
    index, side = lay.place()
    sign = (1 - 2 * side).astype(F32)
    for turn, slow in enumerate((slow_own, slow_other)):
        at = side ^ turn
        sine, cosine = sin_cos(sign * freq[0, 0] * (slow[...] - ref_own[0]) * DZ)
        lens[0, at] = cosine
        lens[1, at] = sine


def last_lens_kernel(lay, freq_before, freq_injected, ref_own, slow, lens):
    top = lax.axis_index("depth") == 0
    freq = jnp.where(top, freq_injected[0, 0], freq_before[0, 0])
    sine, cosine = sin_cos(freq * (slow[...] - ref_own[0]) * DZ)
    lens[0] = cosine
    lens[1] = sine


def call(kernel, outs, scratch, args, scalars=(), flops=0, nbytes=0, name=None):
    vmem = pl.BlockSpec(memory_space=pltpu.VMEM)
    smem = pl.BlockSpec(memory_space=pltpu.SMEM)
    shapes = [jax.ShapeDtypeStruct(shape, F32) for shape in outs]
    return pl.pallas_call(
        kernel,
        out_shape=shapes,
        in_specs=[smem if i in scalars else vmem for i in range(len(args))],
        out_specs=[vmem] * len(outs),
        scratch_shapes=[pltpu.VMEM(shape, F32) for shape in scratch],
        compiler_params=pltpu.CompilerParams(vmem_limit_bytes=40 * MIB),
        cost_estimate=pl.CostEstimate(
            flops=int(flops), bytes_accessed=int(nbytes), transcendentals=0
        ),
        name=name,
    )(*args)


def local(waves, slab_freq, slowness, ref_slow, inj_freq, wavelet, records, src_pos, rcv_pos):
    ranks, groups = lax.axis_size("row"), lax.axis_size("depth")
    rows, lateral = waves.shape[2], waves.shape[5]
    lay = Layout(ranks, groups, rows, lateral)
    slices, cols, half = lay.slices, lay.cols, lay.half
    x_forward, x_inverse, y_forward, y_inverse = (
        jnp.asarray(table) for table in tables(lateral, slices)
    )
    slow = slowness[0]

    def exchange(value, step):
        return lax.ppermute(value, "row", [(rank, rank ^ step) for rank in range(ranks)])

    def onward(value, step):
        pairs = [
            (group * ranks + rank, (group + 1) % groups * ranks + (rank ^ step))
            for group in range(groups)
            for rank in range(ranks)
        ]
        return lax.ppermute(value, ("depth", "row"), pairs)

    piece = (2, rows, cols)
    pair_piece = (2, 2, rows, cols)
    block = (2, rows, lateral)
    edge = (2, 2, HALF, lateral)
    flat = (2 * rows * 2 * lay.chunks, LANES)

    sent = call(
        functools.partial(first_kernel, lay),
        [piece] * ranks,
        [(4, 2, rows, half)],
        [waves.reshape(flat), y_forward],
        name="rows_to_columns",
    )
    arrived = [sent[0]] + [None] * (ranks - 1)
    for step in reversed(range(1, ranks)):
        arrived[step] = exchange(sent[step], step)

    freq_before = lax.ppermute(slab_freq, "depth", [(i, i + 1) for i in range(groups - 1)])
    ref_next = lax.ppermute(ref_slow, "depth", [(i, (i - 1) % groups) for i in range(groups)])
    phase = (2, 2, half, cols)
    phase_a, phase_b, injected = call(
        functools.partial(prepare_kernel, lay),
        [phase, phase, (2, 2, rows, lateral)],
        [(8 * rows, lateral)],
        [
            slab_freq,
            inj_freq,
            ref_slow,
            ref_next,
            src_pos,
            wavelet[0],
            records.reshape(2, -1),
            rcv_pos.T,
        ],
        scalars=(0, 1, 2, 3, 4, 5),
        flops=4e9,
        name="phases_and_injection",
    )
    (last_lens,) = call(
        functools.partial(last_lens_kernel, lay),
        [block],
        [],
        [freq_before, inj_freq, ref_slow, slow],
        scalars=(0, 1, 2),
        name="last_lens",
    )
    slow_sent, arrived = lax.optimization_barrier((slow, arrived))
    slow_other = exchange(slow_sent, slices)

    sent = call(
        functools.partial(column_kernel, lay, True),
        [pair_piece] * slices,
        [(2, 2, half, cols)] * 2,
        [*arrived, phase_a, x_forward, x_inverse],
        name="columns_first",
    )
    arrived = [sent[0]] + [exchange(sent[step], step) for step in range(1, slices)]
    (lens,) = call(
        functools.partial(lens_kernel, lay),
        [(2, 2, rows, lateral)],
        [],
        [slab_freq, ref_slow, slow, slow_other],
        scalars=(0, 1),
        name="lens",
    )
    own, other, *sent = call(
        functools.partial(middle_kernel, lay),
        [block, block] + [pair_piece] * slices,
        [(2, 2, rows, lateral), (2, 2, 2 * rows, half)],
        [*arrived, lens, injected, y_inverse, y_forward],
        name="columns_to_columns",
    )
    arrived = [sent[0]] + [exchange(sent[step], step) for step in range(1, slices)]
    other = exchange(other, slices)

    sent = call(
        functools.partial(column_kernel, lay, False),
        [piece] * ranks,
        [(2, 2, half, cols)] * 2,
        [*arrived, phase_b, x_forward, x_inverse],
        name="columns_second",
    )
    arrived = [None] * ranks
    for step in reversed(range(ranks)):
        arrived[step] = onward(sent[step], step)

    up = [(rank, rank + 1) for rank in range(ranks - 1)]
    down = [(rank + 1, rank) for rank in range(ranks - 1)]

    def image(own, other, leading, trailing, previous):
        before = lax.ppermute(trailing, "row", up)
        after = lax.ppermute(leading, "row", down)
        args = [own, other, before, after]
        if previous is not None:
            args.append(previous)
        (result,) = call(
            functools.partial(image_kernel, lay, previous is not None),
            [(OFF, rows, lateral)],
            [(2, 2, rows + OFF, lateral)],
            args,
            name="image",
        )
        return result

    previous = image(
        own,
        other,
        jnp.stack([own[:, :HALF], other[:, :HALF]]),
        jnp.stack([own[:, rows - HALF :], other[:, rows - HALF :]]),
        None,
    )
    wave_out, own, other, leading, trailing = call(
        functools.partial(last_kernel, lay),
        [flat, block, block, edge, edge],
        [(2, 2, rows, lateral)],
        [*arrived, last_lens, y_inverse],
        name="columns_to_rows",
    )
    result = image(own, other, leading, trailing, previous)
    return wave_out.reshape(waves.shape), result[None]


def solution(mesh):
    placed = (
        P(("shots", "depth"), None, "row", None, None, None),
        P(("shots", "depth"), None),
        P("depth", "row", None),
        P("depth"),
        P("shots", None),
        P("shots", None, None),
        P("shots", None, None, None),
        P("shots"),
        P("shots", None),
    )
    return jax.shard_map(
        local,
        mesh=mesh,
        in_specs=placed,
        out_specs=(
            P(("shots", "depth"), None, "row", None, None, None),
            P(("shots", "depth"), None, "row", None),
        ),
        check_vma=False,
    )
```

profile of v0, /device:TPU:1, one launch (start us, length us, event | category | flops | bytes accessed | tf_op | source)
XLA Modules:
  0.0 88.1 jit_solution(13570519678515462795)
XLA Ops:
  0.6 4.2 %collective-permute-start.3 = (f32[1]{0:T(128)}, f32[1]{0:T(128)}, u32[]{:S(2)}, u32[]{:S(2)}) collective-permute-start(f32[1]{0:T(128)} %param.16), channel_id=1, source_target_pairs={{0,12},{4,0},{8,4},{12,8},{1,13},{5,1},{9,5},{13,9},{2,14},{6,2},{... | collective-permute-start | bytes 20 | tf_op jit(solution)/shard_map/ppermute | solution.py:462
  9.4 1.2 %collective-permute-start.1 = (f32[2,128,256]{2,1,0:T(8,128)S(1)}, f32[2,128,256]{2,1,0:T(8,128)S(1)}, u32[]{:S(2)}, u32[]{:S(2)}) collective-permute-start(f32[2,128,256]{2,1,0:T(8,128)S(1)} %get-tuple-element.31), channel_id=1, source_target_pairs={{0,2},{1,3},{2,0},{3,1},{4,6},{5,7},{6,4},{7,5},{8,10},{9,11},{10,... | collective-permute-start | bytes 786440 | tf_op jit(solution)/shard_map/ppermute | solution.py:434
  15.9 8.8 %phases_and_injection.1 = (f32[2,2,256,256]{3,2,1,0:T(8,128)S(1)}, f32[2,2,256,256]{3,2,1,0:T(8,128)S(1)}, f32[2,2,128,512]{3,2,1,0:T(8,128)S(1)}) custom-call(f32[1,1]{1,0:T(1,128)S(6)} %copy.16.freq, f32[1,1]{1,0:T(1,128)S(6)} %copy.18.freq_injected, f32[1]{0:T(128)S(6)} %copy.17.ref_own, f32[1]{0:T(128)} %collective-permute-done.3.ref_next, ...), custom_call_target="tpu_custom_call" | custom-call | flops 4000000000 | tf_op jit(solution)/shard_map/phases_and_injection/pallas_call | solution.py:409
  24.8 3.0 %columns_first.1 = (f32[2,2,128,256]{3,2,1,0:T(8,128)S(1)}, f32[2,2,128,256]{3,2,1,0:T(8,128)S(1)}) custom-call(f32[2,128,256]{2,1,0:T(8,128)S(1)} %get-tuple-element.33.refs_0_, f32[2,128,256]{2,1,0:T(8,128)S(1)} %collective-permute-done.refs_1_, f32[2,128,256]{2,1,0:T(8,128)S(1)} %collective-permute-done.1.refs_2_, ...), custom_call_target="tpu_custom_call" | custom-call | tf_op jit(solution)/shard_map/columns_first/pallas_call | solution.py:409
  29.2 6.3 %collective-permute-done.5.slow_other = f32[128,512]{1,0:T(8,128)S(1)} collective-permute-done((f32[128,512]{1,0:T(8,128)S(1)}, f32[128,512]{1,0:T(8,128)S(1)}, u32[]{:S(2)}, u32[]{:S(2)}) %collective-permute-start.5) | collective-permute-done | bytes 262176 | tf_op jit(solution)/shard_map/ppermute | solution.py:434
  36.4 2.3 %columns_to_columns.1 = (f32[2,128,512]{2,1,0:T(8,128)S(1)}, f32[2,128,512]{2,1,0:T(8,128)S(1)}, f32[2,2,128,256]{3,2,1,0:T(8,128)S(1)}, f32[2,2,128,256]{3,2,1,0:T(8,128)S(1)}) custom-call(f32[2,2,128,256]{3,2,1,0:T(8,128)S(1)} %get-tuple-element.38.refs_0_, f32[2,2,128,256]{3,2,1,0:T(8,128)S(1)} %collective-permute-done.4.refs_1_, ...), custom_call_target="tpu_custom_call" | custom-call | tf_op jit(solution)/shard_map/columns_to_columns/pallas_call | solution.py:409
  38.7 1.2 %collective-permute-start.6 = (f32[2,2,128,256]{3,2,1,0:T(8,128)S(1)}, f32[2,2,128,256]{3,2,1,0:T(8,128)S(1)}, u32[]{:S(2)}, u32[]{:S(2)}) collective-permute-start(f32[2,2,128,256]{3,2,1,0:T(8,128)S(1)} %get-tuple-element.43), channel_id=1, source_target_pairs={{0,1},{1,0},{2,3},{3,2},{4,5},{5,4},{6,7},{7,6},{8,9},{9,8},{10,11... | collective-permute-start | bytes 1572872 | tf_op jit(solution)/shard_map/ppermute | solution.py:434
  39.9 1.2 %collective-permute-start.14 = (f32[2,128,512]{2,1,0:T(8,128)S(1)}, f32[2,128,512]{2,1,0:T(8,128)S(1)}, u32[]{:S(2)}, u32[]{:S(2)}) collective-permute-start(f32[2,128,512]{2,1,0:T(8,128)S(1)} %get-tuple-element.55), channel_id=1, source_target_pairs={{0,2},{1,3},{2,0},{3,1},{4,6},{5,7},{6,4},{7,5},{8,10},{9,11},{10,... | collective-permute-start | bytes 1572872 | tf_op jit(solution)/shard_map/ppermute | solution.py:434
  41.1 1.8 %collective-permute-start.11 = (f32[1,1]{1,0:T(1,128)}, f32[1,1]{1,0:T(1,128)}, u32[]{:S(2)}, u32[]{:S(2)}) collective-permute-start(f32[1,1]{1,0:T(1,128)} %param.14), channel_id=1, source_target_pairs={{0,4},{4,8},{8,12},{1,5},{5,9},{9,13},{2,6},{6,10},{10,14},{3,7},{... | collective-permute-start | bytes 20 | tf_op jit(solution)/shard_map/ppermute | solution.py:461
  44.3 2.9 %columns_second.1 = (f32[2,128,256]{2,1,0:T(8,128)S(1)}, f32[2,128,256]{2,1,0:T(8,128)S(1)}, f32[2,128,256]{2,1,0:T(8,128)S(1)}, f32[2,128,256]{2,1,0:T(8,128)S(1)}) custom-call(f32[2,2,128,256]{3,2,1,0:T(8,128)S(1)} %get-tuple-element.42.refs_0_, f32[2,2,128,256]{3,2,1,0:T(8,128)S(1)} %collective-permute-done.6.refs_1_, ...), custom_call_target="tpu_custom_call" | custom-call | tf_op jit(solution)/shard_map/columns_second/pallas_call | solution.py:409
  47.2 2.0 %collective-permute-start.7 = (f32[2,128,256]{2,1,0:T(8,128)S(1)}, f32[2,128,256]{2,1,0:T(8,128)S(1)}, u32[]{:S(2)}, u32[]{:S(2)}) collective-permute-start(f32[2,128,256]{2,1,0:T(8,128)S(1)} %get-tuple-element.45), channel_id=1, source_target_pairs={{0,4},{1,5},{2,6},{3,7},{4,8},{5,9},{6,10},{7,11},{8,12},{9,13},{1... | collective-permute-start | bytes 786440 | tf_op jit(solution)/shard_map/ppermute | solution.py:442
  49.2 1.5 %collective-permute-start.8 = (f32[2,128,256]{2,1,0:T(8,128)S(1)}, f32[2,128,256]{2,1,0:T(8,128)S(1)}, u32[]{:S(2)}, u32[]{:S(2)}) collective-permute-start(f32[2,128,256]{2,1,0:T(8,128)S(1)} %get-tuple-element.46), channel_id=1, source_target_pairs={{0,5},{1,4},{2,7},{3,6},{4,9},{5,8},{6,11},{7,10},{8,13},{9,12},{1... | collective-permute-start | bytes 786440 | tf_op jit(solution)/shard_map/ppermute | solution.py:442
  50.7 1.3 %collective-permute-start.9 = (f32[2,128,256]{2,1,0:T(8,128)S(1)}, f32[2,128,256]{2,1,0:T(8,128)S(1)}, u32[]{:S(2)}, u32[]{:S(2)}) collective-permute-start(f32[2,128,256]{2,1,0:T(8,128)S(1)} %get-tuple-element.47), channel_id=1, source_target_pairs={{0,6},{1,7},{2,4},{3,5},{4,10},{5,11},{6,8},{7,9},{8,14},{9,15},{1... | collective-permute-start | bytes 786440 | tf_op jit(solution)/shard_map/ppermute | solution.py:442
  53.4 3.9 %collective-permute-start.15 = (f32[2,2,8,512]{3,2,1,0:T(8,128)S(1)}, f32[2,2,8,512]{3,2,1,0:T(8,128)S(1)}, u32[]{:S(2)}, u32[]{:S(2)}) collective-permute-start(f32[2,2,8,512]{3,2,1,0:T(8,128)S(1)} %pad_maximum_fusion), channel_id=1, source_target_pairs={{0,1},{1,2},{2,3},{4,5},{5,6},{6,7},{8,9},{9,10},{10,11},{12,13},{... | collective-permute-start | bytes 196616 | tf_op jit(solution)/shard_map/ppermute | solution.py:534
  57.3 3.7 %collective-permute-start.16 = (f32[2,2,8,512]{3,2,1,0:T(8,128)S(1)}, f32[2,2,8,512]{3,2,1,0:T(8,128)S(1)}, u32[]{:S(2)}, u32[]{:S(2)}) collective-permute-start(f32[2,2,8,512]{3,2,1,0:T(8,128)S(1)} %pad_maximum_fusion.1), channel_id=1, source_target_pairs={{1,0},{2,1},{3,2},{5,4},{6,5},{7,6},{9,8},{10,9},{11,10},{13,12},{... | collective-permute-start | bytes 196616 | tf_op jit(solution)/shard_map/ppermute | solution.py:535
  61.1 3.3 %collective-permute-done.8.refs_1_ = f32[2,128,256]{2,1,0:T(8,128)S(1)} collective-permute-done((f32[2,128,256]{2,1,0:T(8,128)S(1)}, f32[2,128,256]{2,1,0:T(8,128)S(1)}, u32[]{:S(2)}, u32[]{:S(2)}) %collective-permute-start.8) | collective-permute-done | bytes 262176 | tf_op jit(solution)/shard_map/ppermute | solution.py:442
  64.4 2.7 %collective-permute-done.9.refs_2_ = f32[2,128,256]{2,1,0:T(8,128)S(1)} collective-permute-done((f32[2,128,256]{2,1,0:T(8,128)S(1)}, f32[2,128,256]{2,1,0:T(8,128)S(1)}, u32[]{:S(2)}, u32[]{:S(2)}) %collective-permute-start.9) | collective-permute-done | bytes 262176 | tf_op jit(solution)/shard_map/ppermute | solution.py:442
  67.1 6.8 %collective-permute-done.10.refs_3_ = f32[2,128,256]{2,1,0:T(8,128)S(1)} collective-permute-done((f32[2,128,256]{2,1,0:T(8,128)S(1)}, f32[2,128,256]{2,1,0:T(8,128)S(1)}, u32[]{:S(2)}, u32[]{:S(2)}) %collective-permute-start.10) | collective-permute-done | bytes 262176 | tf_op jit(solution)/shard_map/ppermute | solution.py:442
  73.9 2.4 %columns_to_rows.1 = (f32[2048,128]{1,0:T(8,128)}, f32[2,128,512]{2,1,0:T(8,128)S(1)}, f32[2,128,512]{2,1,0:T(8,128)S(1)}, f32[2,2,8,512]{3,2,1,0:T(8,128)S(1)}, f32[2,2,8,512]{3,2,1,0:T(8,128)S(1)}) custom-call(f32[2,128,256]{2,1,0:T(8,128)S(1)} %collective-permute-done.7.refs_0_, f32[2,128,256]{2,1,0:T(8,128)S(1)} %collective-permute-done.8.refs_1_, ...), custom_call_target="tpu_custom_call" | custom-call | tf_op jit(solution)/shard_map/columns_to_rows/pallas_call | solution.py:409
  76.3 2.3 %collective-permute-start.12 = (f32[2,2,8,512]{3,2,1,0:T(8,128)S(1)}, f32[2,2,8,512]{3,2,1,0:T(8,128)S(1)}, u32[]{:S(2)}, u32[]{:S(2)}) collective-permute-start(f32[2,2,8,512]{3,2,1,0:T(8,128)S(1)} %get-tuple-element.52), channel_id=1, source_target_pairs={{0,1},{1,2},{2,3},{4,5},{5,6},{6,7},{8,9},{9,10},{10,11},{12,13},{... | collective-permute-start | bytes 196616 | tf_op jit(solution)/shard_map/ppermute | solution.py:534
  78.5 2.1 %collective-permute-start.13 = (f32[2,2,8,512]{3,2,1,0:T(8,128)S(1)}, f32[2,2,8,512]{3,2,1,0:T(8,128)S(1)}, u32[]{:S(2)}, u32[]{:S(2)}) collective-permute-start(f32[2,2,8,512]{3,2,1,0:T(8,128)S(1)} %get-tuple-element.53), channel_id=1, source_target_pairs={{1,0},{2,1},{3,2},{5,4},{6,5},{7,6},{9,8},{10,9},{11,10},{13,12},{... | collective-permute-start | bytes 196616 | tf_op jit(solution)/shard_map/ppermute | solution.py:535
  80.6 1.7 %image.2.refs_4_ = f32[16,128,512]{2,1,0:T(8,128)S(1)} custom-call(f32[2,128,512]{2,1,0:T(8,128)S(1)} %get-tuple-element.54.refs_0_, f32[2,128,512]{2,1,0:T(8,128)S(1)} %collective-permute-done.14.refs_1_, f32[2,2,8,512]{3,2,1,0:T(8,128)S(1)} %collective-permute-done.15.refs_2_, f32[2,2,8,512]{3,2,1,0:T(8,128)S(1)} %collective-permute-done.16.refs_3_), custom_call_target="tpu_custom_call" | custom-call | tf_op jit(solution)/shard_map/image/pallas_call | solution.py:409
  82.3 1.8 %collective-permute-done.13.refs_3_ = f32[2,2,8,512]{3,2,1,0:T(8,128)S(1)} collective-permute-done((f32[2,2,8,512]{3,2,1,0:T(8,128)S(1)}, f32[2,2,8,512]{3,2,1,0:T(8,128)S(1)}, u32[]{:S(2)}, u32[]{:S(2)}) %collective-permute-start.13) | collective-permute-done | bytes 65568 | tf_op jit(solution)/shard_map/ppermute | solution.py:535
  84.1 4.0 %image.3 = f32[16,128,512]{2,1,0:T(8,128)} custom-call(f32[2,128,512]{2,1,0:T(8,128)S(1)} %get-tuple-element.50.refs_0_, f32[2,128,512]{2,1,0:T(8,128)S(1)} %get-tuple-element.51.refs_1_, f32[2,2,8,512]{3,2,1,0:T(8,128)S(1)} %collective-permute-done.12.refs_2_, f32[2,2,8,512]{3,2,1,0:T(8,128)S(1)} %collective-permute-done.13.refs_3_, ...), custom_call_target="tpu_custom_call" | custom-call | tf_op jit(solution)/shard_map/image/pallas_call | solution.py:409
  (46 shorter events, 13.0 us)
Async XLA Ops:
  0.6 12.5 %collective-permute-start.3 = (f32[1]{0:T(128)}, f32[1]{0:T(128)}, u32[]{:S(2)}, u32[]{:S(2)}) collective-permute-start(f32[1]{0:T(128)} %param.16), channel_id=1, source_target_pairs={{0,12},{4,0},{8,4},{12,8},{1,13},{5,1},{9,5},{13,9},{2,14},{6,2},{... | collective-permute-start | bytes 20 | tf_op jit(solution)/shard_map/ppermute | solution.py:462
  4.8 1.2 %copy-start.1 = (bf16[2,2,2,256,256]{4,3,2,1,0:T(8,128)(2,1)S(1)}, bf16[2,2,2,256,256]{4,3,2,1,0:T(8,128)(2,1)}, u32[]{:S(2)}) copy-start(bf16[2,2,2,256,256]{4,3,2,1,0:T(8,128)(2,1)} %constant.10.clone.refs_1_.refs_5_) | copy-start | bytes 3145732
  6.1 1.2 %copy-start.5 = (f32[1,2,128,2,1,512]{5,4,3,2,1,0:T(1,128)S(1)}, f32[1,2,128,2,1,512]{5,4,3,2,1,0:T(1,128)}, u32[]{:S(2)}) copy-start(f32[1,2,128,2,1,512]{5,4,3,2,1,0:T(1,128)} %param.13) | copy-start | bytes 3145732
  8.4 16.4 %collective-permute-start = (f32[2,128,256]{2,1,0:T(8,128)S(1)}, f32[2,128,256]{2,1,0:T(8,128)S(1)}, u32[]{:S(2)}, u32[]{:S(2)}) collective-permute-start(f32[2,128,256]{2,1,0:T(8,128)S(1)} %get-tuple-element.30), channel_id=1, source_target_pairs={{0,1},{1,0},{2,3},{3,2},{4,5},{5,4},{6,7},{7,6},{8,9},{9,8},{10,11... | collective-permute-start | bytes 786440 | tf_op jit(solution)/shard_map/ppermute | solution.py:434
  9.4 15.3 %collective-permute-start.1 = (f32[2,128,256]{2,1,0:T(8,128)S(1)}, f32[2,128,256]{2,1,0:T(8,128)S(1)}, u32[]{:S(2)}, u32[]{:S(2)}) collective-permute-start(f32[2,128,256]{2,1,0:T(8,128)S(1)} %get-tuple-element.31), channel_id=1, source_target_pairs={{0,2},{1,3},{2,0},{3,1},{4,6},{5,7},{6,4},{7,5},{8,10},{9,11},{10,... | collective-permute-start | bytes 786440 | tf_op jit(solution)/shard_map/ppermute | solution.py:434
  10.7 14.1 %collective-permute-start.2 = (f32[2,128,256]{2,1,0:T(8,128)S(1)}, f32[2,128,256]{2,1,0:T(8,128)S(1)}, u32[]{:S(2)}, u32[]{:S(2)}) collective-permute-start(f32[2,128,256]{2,1,0:T(8,128)S(1)} %get-tuple-element.32), channel_id=1, source_target_pairs={{0,3},{1,2},{2,1},{3,0},{4,7},{5,6},{6,5},{7,4},{8,11},{9,10},{10,... | collective-permute-start | bytes 786440 | tf_op jit(solution)/shard_map/ppermute | solution.py:434
  15.9 8.9 %copy-start.3 = (bf16[2,2,512,256]{3,2,1,0:T(8,128)(2,1)S(1)}, bf16[2,2,512,256]{3,2,1,0:T(8,128)(2,1)}, u32[]{:S(2)}) copy-start(bf16[2,2,512,256]{3,2,1,0:T(8,128)(2,1)} %constant.9.clone.refs_6_.refs_4_) | copy-start | bytes 3145732
  15.9 8.9 %copy-start.4 = (bf16[2,2,512,256]{3,2,1,0:T(8,128)(2,1)S(1)}, bf16[2,2,512,256]{3,2,1,0:T(8,128)(2,1)}, u32[]{:S(2)}) copy-start(bf16[2,2,512,256]{3,2,1,0:T(8,128)(2,1)} %constant.8.clone.refs_5_.refs_3_) | copy-start | bytes 3145732
  24.7 3.3 %copy-start.6 = (f32[1,128,512]{2,1,0:T(8,128)S(1)}, f32[1,128,512]{2,1,0:T(8,128)}, u32[]{:S(2)}) copy-start(f32[1,128,512]{2,1,0:T(8,128)} %param.15) | copy-start | bytes 786436
  24.7 11.6 %copy-start = (bf16[2,2,2,256,256]{4,3,2,1,0:T(8,128)(2,1)S(1)}, bf16[2,2,2,256,256]{4,3,2,1,0:T(8,128)(2,1)}, u32[]{:S(2)}) copy-start(bf16[2,2,2,256,256]{4,3,2,1,0:T(8,128)(2,1)} %constant.11.clone.refs_4_.refs_5_) | copy-start | bytes 3145732
  24.8 11.6 %copy-start.2 = (bf16[2,2,2,256,256]{4,3,2,1,0:T(8,128)(2,1)S(1)}, bf16[2,2,2,256,256]{4,3,2,1,0:T(8,128)(2,1)}, u32[]{:S(2)}) copy-start(bf16[2,2,2,256,256]{4,3,2,1,0:T(8,128)(2,1)} %constant.10.clone.refs_1_.refs_5_) | copy-start | bytes 3145732
  27.8 8.6 %collective-permute-start.4 = (f32[2,2,128,256]{3,2,1,0:T(8,128)S(1)}, f32[2,2,128,256]{3,2,1,0:T(8,128)S(1)}, u32[]{:S(2)}, u32[]{:S(2)}) collective-permute-start(f32[2,2,128,256]{3,2,1,0:T(8,128)S(1)} %get-tuple-element.39), channel_id=1, source_target_pairs={{0,1},{1,0},{2,3},{3,2},{4,5},{5,4},{6,7},{7,6},{8,9},{9,8},{10,11... | collective-permute-start | bytes 1572872 | tf_op jit(solution)/shard_map/ppermute | solution.py:434
  28.0 7.5 %collective-permute-start.5 = (f32[128,512]{1,0:T(8,128)S(1)}, f32[128,512]{1,0:T(8,128)S(1)}, u32[]{:S(2)}, u32[]{:S(2)}) collective-permute-start(f32[128,512]{1,0:T(8,128)S(1)} %bitcast.16), channel_id=1, source_target_pairs={{0,2},{1,3},{2,0},{3,1},{4,6},{5,7},{6,4},{7,5},{8,10},{9,11},{10,... | collective-permute-start | bytes 786440 | tf_op jit(solution)/shard_map/ppermute | solution.py:434
  38.7 5.6 %collective-permute-start.6 = (f32[2,2,128,256]{3,2,1,0:T(8,128)S(1)}, f32[2,2,128,256]{3,2,1,0:T(8,128)S(1)}, u32[]{:S(2)}, u32[]{:S(2)}) collective-permute-start(f32[2,2,128,256]{3,2,1,0:T(8,128)S(1)} %get-tuple-element.43), channel_id=1, source_target_pairs={{0,1},{1,0},{2,3},{3,2},{4,5},{5,4},{6,7},{7,6},{8,9},{9,8},{10,11... | collective-permute-start | bytes 1572872 | tf_op jit(solution)/shard_map/ppermute | solution.py:434
  39.9 13.5 %collective-permute-start.14 = (f32[2,128,512]{2,1,0:T(8,128)S(1)}, f32[2,128,512]{2,1,0:T(8,128)S(1)}, u32[]{:S(2)}, u32[]{:S(2)}) collective-permute-start(f32[2,128,512]{2,1,0:T(8,128)S(1)} %get-tuple-element.55), channel_id=1, source_target_pairs={{0,2},{1,3},{2,0},{3,1},{4,6},{5,7},{6,4},{7,5},{8,10},{9,11},{10,... | collective-permute-start | bytes 1572872 | tf_op jit(solution)/shard_map/ppermute | solution.py:434
  41.1 2.1 %collective-permute-start.11 = (f32[1,1]{1,0:T(1,128)}, f32[1,1]{1,0:T(1,128)}, u32[]{:S(2)}, u32[]{:S(2)}) collective-permute-start(f32[1,1]{1,0:T(1,128)} %param.14), channel_id=1, source_target_pairs={{0,4},{4,8},{8,12},{1,5},{5,9},{9,13},{2,6},{6,10},{10,14},{3,7},{... | collective-permute-start | bytes 20 | tf_op jit(solution)/shard_map/ppermute | solution.py:461
  47.2 10.2 %collective-permute-start.7 = (f32[2,128,256]{2,1,0:T(8,128)S(1)}, f32[2,128,256]{2,1,0:T(8,128)S(1)}, u32[]{:S(2)}, u32[]{:S(2)}) collective-permute-start(f32[2,128,256]{2,1,0:T(8,128)S(1)} %get-tuple-element.45), channel_id=1, source_target_pairs={{0,4},{1,5},{2,6},{3,7},{4,8},{5,9},{6,10},{7,11},{8,12},{9,13},{1... | collective-permute-start | bytes 786440 | tf_op jit(solution)/shard_map/ppermute | solution.py:442
  49.2 15.2 %collective-permute-start.8 = (f32[2,128,256]{2,1,0:T(8,128)S(1)}, f32[2,128,256]{2,1,0:T(8,128)S(1)}, u32[]{:S(2)}, u32[]{:S(2)}) collective-permute-start(f32[2,128,256]{2,1,0:T(8,128)S(1)} %get-tuple-element.46), channel_id=1, source_target_pairs={{0,5},{1,4},{2,7},{3,6},{4,9},{5,8},{6,11},{7,10},{8,13},{9,12},{1... | collective-permute-start | bytes 786440 | tf_op jit(solution)/shard_map/ppermute | solution.py:442
  50.7 16.4 %collective-permute-start.9 = (f32[2,128,256]{2,1,0:T(8,128)S(1)}, f32[2,128,256]{2,1,0:T(8,128)S(1)}, u32[]{:S(2)}, u32[]{:S(2)}) collective-permute-start(f32[2,128,256]{2,1,0:T(8,128)S(1)} %get-tuple-element.47), channel_id=1, source_target_pairs={{0,6},{1,7},{2,4},{3,5},{4,10},{5,11},{6,8},{7,9},{8,14},{9,15},{1... | collective-permute-start | bytes 786440 | tf_op jit(solution)/shard_map/ppermute | solution.py:442
  52.0 21.9 %collective-permute-start.10 = (f32[2,128,256]{2,1,0:T(8,128)S(1)}, f32[2,128,256]{2,1,0:T(8,128)S(1)}, u32[]{:S(2)}, u32[]{:S(2)}) collective-permute-start(f32[2,128,256]{2,1,0:T(8,128)S(1)} %get-tuple-element.48), channel_id=1, source_target_pairs={{0,7},{1,6},{2,5},{3,4},{4,11},{5,10},{6,9},{7,8},{8,15},{9,14},{1... | collective-permute-start | bytes 786440 | tf_op jit(solution)/shard_map/ppermute | solution.py:442
  53.4 27.1 %collective-permute-start.15 = (f32[2,2,8,512]{3,2,1,0:T(8,128)S(1)}, f32[2,2,8,512]{3,2,1,0:T(8,128)S(1)}, u32[]{:S(2)}, u32[]{:S(2)}) collective-permute-start(f32[2,2,8,512]{3,2,1,0:T(8,128)S(1)} %pad_maximum_fusion), channel_id=1, source_target_pairs={{0,1},{1,2},{2,3},{4,5},{5,6},{6,7},{8,9},{9,10},{10,11},{12,13},{... | collective-permute-start | bytes 196616 | tf_op jit(solution)/shard_map/ppermute | solution.py:534
  57.3 23.3 %collective-permute-start.16 = (f32[2,2,8,512]{3,2,1,0:T(8,128)S(1)}, f32[2,2,8,512]{3,2,1,0:T(8,128)S(1)}, u32[]{:S(2)}, u32[]{:S(2)}) collective-permute-start(f32[2,2,8,512]{3,2,1,0:T(8,128)S(1)} %pad_maximum_fusion.1), channel_id=1, source_target_pairs={{1,0},{2,1},{3,2},{5,4},{6,5},{7,6},{9,8},{10,9},{11,10},{13,12},{... | collective-permute-start | bytes 196616 | tf_op jit(solution)/shard_map/ppermute | solution.py:535
  76.3 6.1 %collective-permute-start.12 = (f32[2,2,8,512]{3,2,1,0:T(8,128)S(1)}, f32[2,2,8,512]{3,2,1,0:T(8,128)S(1)}, u32[]{:S(2)}, u32[]{:S(2)}) collective-permute-start(f32[2,2,8,512]{3,2,1,0:T(8,128)S(1)} %get-tuple-element.52), channel_id=1, source_target_pairs={{0,1},{1,2},{2,3},{4,5},{5,6},{6,7},{8,9},{9,10},{10,11},{12,13},{... | collective-permute-start | bytes 196616 | tf_op jit(solution)/shard_map/ppermute | solution.py:534
  78.5 5.6 %collective-permute-start.13 = (f32[2,2,8,512]{3,2,1,0:T(8,128)S(1)}, f32[2,2,8,512]{3,2,1,0:T(8,128)S(1)}, u32[]{:S(2)}, u32[]{:S(2)}) collective-permute-start(f32[2,2,8,512]{3,2,1,0:T(8,128)S(1)} %get-tuple-element.53), channel_id=1, source_target_pairs={{1,0},{2,1},{3,2},{5,4},{6,5},{7,6},{9,8},{10,9},{11,10},{13,12},{... | collective-permute-start | bytes 196616 | tf_op jit(solution)/shard_map/ppermute | solution.py:535
  (4 other events, 2.8 us)
where the time goes:
time: 88.6 us; the launch traced here: 88.1 us
  starting transfers between devices  30.6 us (35%)
  Pallas kernels  27.9 us (31%)
  waiting for transfers between devices  21.5 us (24%)
  local copies, waits for them, and re-layouts  5.31 us (6%)
  between operations  2.84 us (3%)
    pallas_call x10, Pallas kernels, call(): pl.pallas_call(kernel, out_shape=shapes, in_specs=[smem if i in scalars e...  27.9 us
    ppermute x4, waiting for transfers between devices, onward(): return lax.ppermute(value, ('depth', 'row'), pairs)  12.8 us
    ppermute x7, starting transfers between devices, exchange(): lax.ppermute(value, 'row', [(rank, rank ^ step) for rank in range(ranks)])  6.65 us
    ppermute x7, waiting for transfers between devices, exchange(): lax.ppermute(value, 'row', [(rank, rank ^ step) for rank in range(ranks)])  6.58 us
    ppermute x2, starting transfers between devices, image(): before = lax.ppermute(trailing, 'row', up)  6.12 us
    ppermute x4, starting transfers between devices, onward(): return lax.ppermute(value, ('depth', 'row'), pairs)  6.01 us
    ppermute x2, starting transfers between devices, image(): after = lax.ppermute(leading, 'row', down)  5.79 us
    unnamed x22, local copies, waits for them, and re-layouts  5.3 us
  transfers between devices with their start and end apart: 17, of which 7 were waited for; matrix products, arithmetic and copies ran while one was open for 0% of the time, Pallas kernels for 21%

commit v1 on v0

--- a/solution.py
+++ b/solution.py
@@ -116,6 +116,7 @@
         self.half = lateral // 2
         self.cols = lateral // self.slices
         self.chunks = lateral // LANES
+        self.wide = rows + OFF
 
     def place(self):
         rank = lax.axis_index("row")
@@ -123,11 +124,17 @@
 
 
 def first_kernel(lay, *refs):
-    waves, y_forward = refs[:2]
-    pieces = refs[2 : 2 + lay.ranks]
-    parity_parts = refs[-1]
+    far, pieces = refs[:2], refs[2 : 2 + lay.ranks]
+    parity_parts, waves, y_forward, arrivals = refs[2 + lay.ranks :]
     index, side = lay.place()
     middle = lay.chunks // 2
+    copies = [
+        pltpu.make_async_copy(source, target, arrivals.at[i])
+        for i, (source, target) in enumerate(zip(far, (waves, y_forward)))
+    ]
+    for copy in copies:
+        copy.start()
+    copies[0].wait()
     for field in range(2):
         for part in range(2):
             chunks = [
@@ -145,6 +152,7 @@
             high = jnp.concatenate(chunks[middle:], axis=1)
             parity_parts[2 * field, part] = low + high
             parity_parts[2 * field + 1, part] = low - high
+    copies[1].wait()
     for step in reversed(range(lay.ranks)):
         piece_slice = index ^ (step % lay.slices)
         field = side ^ (step // lay.slices)
@@ -160,9 +168,11 @@
     count_in = lay.ranks if first else lay.slices
     count_out = lay.slices if first else lay.ranks
     pieces = refs[:count_in]
-    phase, x_forward, x_inverse = refs[count_in : count_in + 3]
-    results = refs[count_in + 3 : count_in + 3 + count_out]
-    parity_parts, halves = refs[-2:]
+    phase, x_forward, x_inverse_far = refs[count_in : count_in + 3]
+    results = refs[-4 - count_out : -4]
+    parity_parts, whole, x_inverse, x_inverse_here = refs[-4:]
+    x_inverse_copy = pltpu.make_async_copy(x_inverse_far, x_inverse, x_inverse_here)
+    x_inverse_copy.start()
     index, side = lay.place()
     sign = (1 - 2 * side).astype(F32)
     for step in range(lay.slices):
@@ -182,6 +192,8 @@
             parity_parts[parity, 0], parity_parts[parity, 1], x_forward, parity, False
         )
         phase_real, phase_imag = phase[0, parity], phase[1, parity]
+        if parity == 0:
+            x_inverse_copy.wait()
         sums.append(
             along_x(
                 real * phase_real - imag * phase_imag,
@@ -192,17 +204,24 @@
             )
         )
     for part in range(2):
-        halves[0, part] = sums[0][part] + sums[1][part]
-        halves[1, part] = sums[0][part] - sums[1][part]
-    for step in range(count_out):
-        block = (index ^ (step % lay.slices)) * lay.rows
-        at = pl.ds(pl.multiple_of(block, lay.rows), lay.rows)
+        whole[part, :HALF] = jnp.zeros((HALF, lay.cols), F32)
+        whole[part, HALF : HALF + lay.half] = sums[0][part] + sums[1][part]
+        whole[part, HALF + lay.half : HALF + lay.lateral] = sums[0][part] - sums[1][part]
+        whole[part, HALF + lay.lateral :] = jnp.zeros((HALF, lay.cols), F32)
+    if first:
+        for step in range(lay.slices):
+            for upper in range(2):
+                place = ((index ^ step) + upper * lay.slices) * lay.rows
+                at = pl.ds(pl.multiple_of(place + HALF, 8), lay.rows)
+                for part in range(2):
+                    results[step][upper, part] = whole[part, at, :]
+        return
+    results[0][0, lay.wide :] = refs[count_in + 3][...]
+    for step in range(lay.ranks):
+        place = ((index + side * lay.slices) ^ step) * lay.rows
+        at = pl.ds(pl.multiple_of(place, 8), lay.wide)
         for part in range(2):
-            if first:
-                for upper in range(2):
-                    results[step][upper, part] = halves[upper, part, at, :]
-            else:
-                results[step][part] = halves[side ^ (step // lay.slices), part, at, :]
+            results[step][part, : lay.wide] = whole[part, at, :]
 
 
 def rows_from(lay, pieces, y_inverse, index):
@@ -260,68 +279,82 @@
 
 def last_kernel(lay, *refs):
     pieces = refs[: lay.ranks]
-    lens, y_inverse = refs[lay.ranks : lay.ranks + 2]
-    wave_out, own, other, leading, trailing = refs[lay.ranks + 2 : lay.ranks + 7]
-    fields = refs[-1]
+    slow, ref_own, before, behind, y_inverse, previous = refs[lay.ranks : lay.ranks + 6]
+    wave_out, image = refs[lay.ranks + 6 : lay.ranks + 8]
+    lens, fields, wave_buffer, image_buffer, wave_sent, image_sent = refs[lay.ranks + 8 :]
     index, side = lay.place()
-    for turn, result in enumerate((own, other)):
+    freq = pieces[0][0, lay.wide : lay.wide + 1, 0:1]
+    end = HALF + lay.rows
+    for start, values in ((0, before[4]), (HALF, slow[...]), (end, behind[4])):
+        sine, cosine = sin_cos(freq * (values - ref_own[0]) * DZ)
+        lens[0, start : start + values.shape[0]] = cosine
+        lens[1, start : start + values.shape[0]] = sine
+    for turn in range(2):
         field = side ^ turn
-        low, high = rows_from(
+        sign = (1 - 2 * field).astype(F32)
+        ends = rows_from(
             lay,
             [
-                [piece[0], piece[1]]
+                [piece[part, : lay.wide] for part in range(2)]
                 for piece in pieces[turn * lay.slices : (turn + 1) * lay.slices]
             ],
             y_inverse,
             index,
         )
-        sign = (1 - 2 * field).astype(F32)
-        for end, (real, imag) in enumerate((low, high)):
+        for end, (real, imag) in enumerate(ends):
             lanes = pl.ds(end * lay.half, lay.half)
             cosine, sine = lens[0, :, lanes], lens[1, :, lanes] * sign
-            result[0, :, lanes] = real * cosine - imag * sine
-            result[1, :, lanes] = real * sine + imag * cosine
-        for part in range(2):
-            fields[field, part] = result[part]
-            leading[turn, part] = result[part, :HALF]
-            trailing[turn, part] = result[part, lay.rows - HALF :]
+            fields[field, 0, :, lanes] = real * cosine - imag * sine
+            fields[field, 1, :, lanes] = real * sine + imag * cosine
     for field in range(2):
         for part in range(2):
             for chunk in range(lay.chunks):
                 start = (part * lay.rows * 2 + field) * lay.chunks + chunk
-                wave_out[pl.ds(start, lay.rows, stride=2 * lay.chunks), :] = fields[
-                    field, part, :, pl.ds(chunk * LANES, LANES)
+                wave_buffer[pl.ds(start, lay.rows, stride=2 * lay.chunks), :] = fields[
+                    field, part, HALF : HALF + lay.rows, pl.ds(chunk * LANES, LANES)
                 ]
-
-
-def image_kernel(lay, adds, *refs):
-    own, other, before, after = refs[:4]
-    result, padded = refs[-2:]
+    copies = [pltpu.make_async_copy(wave_buffer, wave_out, wave_sent)]
+    copies[0].start()
+    for offset in range(OFF):
+        image_buffer[offset] = previous[offset] + correlation(lay, fields, offset)
+        copies.append(
+            pltpu.make_async_copy(
+                image_buffer.at[offset], image.at[offset], image_sent.at[offset]
+            )
+        )
+        copies[-1].start()
+    for copy in copies:
+        copy.wait()
+
+
+def correlation(lay, fields, offset):
+    lag = offset - HALF
+    source = pl.ds(HALF - lag, lay.rows)
+    receiver = pl.ds(HALF + lag, lay.rows)
+    return (
+        fields[0, 0, source] * fields[1, 0, receiver]
+        + fields[0, 1, source] * fields[1, 1, receiver]
+    )
+
+
+def image_kernel(lay, own, other, before, after, result, fields):
     rank = lax.axis_index("row")
     side = rank // lay.slices
     side_before = (rank + lay.ranks - 1) % lay.ranks // lay.slices
     side_after = (rank + 1) % lay.ranks // lay.slices
     end = HALF + lay.rows
     for part in range(2):
-        padded[side, part, HALF:end] = own[part]
-        padded[1 - side, part, HALF:end] = other[part]
+        fields[side, part, HALF:end] = own[part]
+        fields[1 - side, part, HALF:end] = other[part]
         for field in range(2):
-            padded[field, part, :HALF] = before[field ^ side_before, part]
-            padded[field, part, end:] = after[field ^ side_after, part]
+            fields[field, part, :HALF] = before[2 * (field ^ side_before) + part]
+            fields[field, part, end:] = after[2 * (field ^ side_after) + part]
     for offset in range(OFF):
-        lag = offset - HALF
-        source = pl.ds(HALF - lag, lay.rows)
-        receiver = pl.ds(HALF + lag, lay.rows)
-        value = (
-            padded[0, 0, source] * padded[1, 0, receiver]
-            + padded[0, 1, source] * padded[1, 1, receiver]
-        )
-        result[offset] = refs[4][offset] + value if adds else value
-
-
-def prepare_kernel(lay, freq, freq_injected, ref_own, ref_next, source_at, wavelet, records, receivers, phase_a, phase_b, injected, sums):
+        result[offset] = correlation(lay, fields, offset)
+
+
+def fill_phase(lay, wave_number, phase):
     index, side = lay.place()
-    last = lax.axis_index("depth") == lay.groups - 1
     shape = (lay.half, lay.cols)
     spacing = 2.0 * math.pi / lay.lateral
 
@@ -330,25 +363,42 @@
         number = signed.astype(F32) * spacing
         return number * number
 
-    place = lax.broadcasted_iota(jnp.int32, shape, 1) + index * lay.cols
+    place = lax.broadcasted_iota(jnp.int32, (1, lay.cols), 1) + index * lay.cols
     y_squares = squares(jnp.where(place < lay.half, 2 * place, 2 * (place - lay.half) + 1))
     scale = 1.0 / (lay.lateral * lay.lateral)
     sign = (1 - 2 * side).astype(F32) * scale
-    wave_numbers = (
-        freq[0, 0] * ref_own[0],
-        jnp.where(last, freq_injected[0, 0], freq[0, 0]) * ref_next[0],
-    )
     for parity in range(2):
         x_squares = squares(2 * lax.broadcasted_iota(jnp.int32, shape, 0) + parity)
-        lateral_squares = x_squares + y_squares
-        for number, phase in zip(wave_numbers, (phase_a, phase_b)):
-            vertical = number * number - lateral_squares
-            argument = jnp.sqrt(jnp.abs(vertical)) * DZ
-            sine, cosine = sin_cos(argument)
-            runs = vertical > 0
-            phase[0, parity] = jnp.where(runs, cosine, jnp.exp(-argument)) * scale
-            phase[1, parity] = jnp.where(runs, sine, 0.0) * sign
-
+        vertical = wave_number * wave_number - (x_squares + y_squares)
+        argument = jnp.sqrt(jnp.abs(vertical)) * DZ
+        sine, cosine = sin_cos(argument)
+        runs = vertical > 0
+        phase[0, parity] = jnp.where(runs, cosine, jnp.exp(-argument)) * scale
+        phase[1, parity] = jnp.where(runs, sine, 0.0) * sign
+
+
+def phase_kernel(lay, freq, ref_own, phase):
+    fill_phase(lay, freq[0, 0] * ref_own[0], phase)
+
+
+def next_phase_kernel(lay, freq, freq_injected, ref_next, phase, freq_rows):
+    last = lax.axis_index("depth") == lay.groups - 1
+    freq_now = jnp.where(last, freq_injected[0, 0], freq[0, 0])
+    fill_phase(lay, freq_now * ref_next[0], phase)
+    freq_rows[...] = jnp.zeros((8, lay.cols), F32) + freq_now
+
+
+def inject_kernel(lay, *refs):
+    far, injected = refs[:4], refs[4]
+    sums, near, arrivals = refs[5], refs[6:10], refs[10]
+    copies = [
+        pltpu.make_async_copy(source, target, arrivals.at[i])
+        for i, (source, target) in enumerate(zip(far, near))
+    ]
+    for copy in copies:
+        copy.start()
+    index, side = lay.place()
+    source_at, wavelet, records, receivers = near
     count = receivers.shape[1]
     width = next((w for w in (1024, 512, 256, 128) if count % w == 0), count)
     both = 2 * lay.rows
@@ -356,17 +406,21 @@
     row = lax.broadcasted_iota(jnp.int32, (both, width), 0)
     row = row + index * lay.rows + jnp.where(row >= lay.rows, (lay.slices - 1) * lay.rows, 0)
     column = lax.broadcasted_iota(jnp.int32, (lay.lateral, width), 0)
+    for copy in copies:
+        copy.wait()
     for start in range(0, count, width):
         lanes = pl.ds(start, width)
         is_first = lax.broadcasted_iota(jnp.int32, (1, width), 1) + start == 0
         at_row = jnp.where(
-            is_source, jnp.where(is_first, source_at[0], -1), receivers[0:1, lanes]
-        )
-        at_column = jnp.where(is_source, source_at[1], receivers[1:2, lanes])
+            is_source, jnp.where(is_first, source_at[:, 0:1], -1), receivers[0:1, lanes]
+        )
+        at_column = jnp.where(is_source, source_at[:, 1:2], receivers[1:2, lanes])
         hit = row == at_row
         stacked = []
         for part in range(2):
-            value = jnp.where(is_source, wavelet[0, part], records[part : part + 1, lanes])
+            value = jnp.where(
+                is_source, wavelet[:, part : part + 1], records[part : part + 1, lanes]
+            )
             high = value.astype(BF16).astype(F32)
             for piece in (high, value - high):
                 stacked.append(jnp.where(hit, piece, 0.0).astype(BF16))
@@ -384,37 +438,51 @@
         injected[part] = value.reshape(2, lay.rows, lay.lateral)
 
 
-def lens_kernel(lay, freq, ref_own, slow_own, slow_other, lens):
-    index, side = lay.place()
+def lens_kernel(lay, freq, ref_own, slow, *refs):
+    lens = refs[-1]
+    _, side = lay.place()
     sign = (1 - 2 * side).astype(F32)
-    for turn, slow in enumerate((slow_own, slow_other)):
-        at = side ^ turn
-        sine, cosine = sin_cos(sign * freq[0, 0] * (slow[...] - ref_own[0]) * DZ)
-        lens[0, at] = cosine
-        lens[1, at] = sine
-
-
-def last_lens_kernel(lay, freq_before, freq_injected, ref_own, slow, lens):
-    top = lax.axis_index("depth") == 0
-    freq = jnp.where(top, freq_injected[0, 0], freq_before[0, 0])
-    sine, cosine = sin_cos(freq * (slow[...] - ref_own[0]) * DZ)
-    lens[0] = cosine
-    lens[1] = sine
-
-
-def call(kernel, outs, scratch, args, scalars=(), flops=0, nbytes=0, name=None):
-    vmem = pl.BlockSpec(memory_space=pltpu.VMEM)
+
+    def store(field, start, values):
+        sine, cosine = sin_cos(sign * freq[0, 0] * (values - ref_own[0]) * DZ)
+        at = pl.ds(pl.multiple_of(start, 8), values.shape[0])
+        lens[0, field, at, :] = cosine
+        lens[1, field, at, :] = sine
+
+    store(side, 0, slow[...])
+    shot = lax.axis_index("shots")
+    for step, part in enumerate(refs[:-1]):
+        start = (shot ^ step) * part.shape[0] if len(refs) > 2 else 0
+        store(1 - side, start, part[...])
+
+
+def after(*values):
+    return lax.optimization_barrier(values)
+
+
+def call(kernel, outs, scratch, args, scalars=(), far=(), outside=False, vmem=40, name=None):
+    inside = pl.BlockSpec(memory_space=pltpu.VMEM)
     smem = pl.BlockSpec(memory_space=pltpu.SMEM)
+    outer = pl.BlockSpec(memory_space=pltpu.HBM)
+    anywhere = pl.BlockSpec(memory_space=pl.ANY)
     shapes = [jax.ShapeDtypeStruct(shape, F32) for shape in outs]
+    args = [
+        pltpu.with_memory_space_constraint(value, pltpu.HBM) if i in far else value
+        for i, value in enumerate(args)
+    ]
     return pl.pallas_call(
         kernel,
         out_shape=shapes,
-        in_specs=[smem if i in scalars else vmem for i in range(len(args))],
-        out_specs=[vmem] * len(outs),
-        scratch_shapes=[pltpu.VMEM(shape, F32) for shape in scratch],
-        compiler_params=pltpu.CompilerParams(vmem_limit_bytes=40 * MIB),
+        in_specs=[
+            smem if i in scalars else outer if i in far else inside for i in range(len(args))
+        ],
+        out_specs=[anywhere if outside else inside] * len(outs),
+        scratch_shapes=[
+            pltpu.VMEM(shape, F32) if isinstance(shape, tuple) else shape for shape in scratch
+        ],
+        compiler_params=pltpu.CompilerParams(vmem_limit_bytes=vmem * MIB),
         cost_estimate=pl.CostEstimate(
-            flops=int(flops), bytes_accessed=int(nbytes), transcendentals=0
+            flops=1, bytes_accessed=1, transcendentals=0
         ),
         name=name,
     )(*args)
@@ -444,65 +512,82 @@
     piece = (2, rows, cols)
     pair_piece = (2, 2, rows, cols)
     block = (2, rows, lateral)
-    edge = (2, 2, HALF, lateral)
+    wide = lay.wide
     flat = (2 * rows * 2 * lay.chunks, LANES)
 
+    shots = lax.axis_size("shots")
+    if shots & (shots - 1) or rows % (8 * shots):
+        shots = 1
+    share = rows // shots
+    shot = lax.axis_index("shots") if shots > 1 else 0
+    slow_parts = [exchange(lax.dynamic_slice_in_dim(slow, shot * share, share), slices)]
+
+    phase = (2, 2, half, cols)
+    column_scratch = [
+        (2, 2, half, cols),
+        (2, lateral + OFF, cols),
+        pltpu.VMEM(x_inverse.shape, BF16),
+        pltpu.SemaphoreType.DMA(()),
+    ]
     sent = call(
         functools.partial(first_kernel, lay),
         [piece] * ranks,
-        [(4, 2, rows, half)],
+        [
+            (4, 2, rows, half),
+            flat,
+            pltpu.VMEM(y_forward.shape, BF16),
+            pltpu.SemaphoreType.DMA((2,)),
+        ],
         [waves.reshape(flat), y_forward],
+        far=(0, 1),
         name="rows_to_columns",
     )
+    sent, slow_parts = after(sent, slow_parts)
     arrived = [sent[0]] + [None] * (ranks - 1)
     for step in reversed(range(1, ranks)):
         arrived[step] = exchange(sent[step], step)
-
-    freq_before = lax.ppermute(slab_freq, "depth", [(i, i + 1) for i in range(groups - 1)])
-    ref_next = lax.ppermute(ref_slow, "depth", [(i, (i - 1) % groups) for i in range(groups)])
-    phase = (2, 2, half, cols)
-    phase_a, phase_b, injected = call(
-        functools.partial(prepare_kernel, lay),
-        [phase, phase, (2, 2, rows, lateral)],
-        [(8 * rows, lateral)],
-        [
-            slab_freq,
-            inj_freq,
-            ref_slow,
-            ref_next,
-            src_pos,
-            wavelet[0],
-            records.reshape(2, -1),
-            rcv_pos.T,
-        ],
-        scalars=(0, 1, 2, 3, 4, 5),
-        flops=4e9,
-        name="phases_and_injection",
-    )
-    (last_lens,) = call(
-        functools.partial(last_lens_kernel, lay),
-        [block],
+    for step in range(1, shots):
+        pairs = [(shot, shot ^ step) for shot in range(shots)]
+        slow_parts.append(lax.ppermute(slow_parts[0], "shots", pairs))
+
+    ref_sent, _ = after(ref_slow, sent[1])
+    ref_next = lax.ppermute(ref_sent, "depth", [(i, (i - 1) % groups) for i in range(groups)])
+    (phase_a,) = call(
+        functools.partial(phase_kernel, lay),
+        [phase],
         [],
-        [freq_before, inj_freq, ref_slow, slow],
-        scalars=(0, 1, 2),
-        name="last_lens",
-    )
-    slow_sent, arrived = lax.optimization_barrier((slow, arrived))
-    slow_other = exchange(slow_sent, slices)
-
+        [slab_freq, ref_slow],
+        scalars=(0, 1),
+        name="phase_first",
+    )
+    receivers = [src_pos[None], wavelet[0], records.reshape(2, -1), rcv_pos.T]
+    receivers[0], ref_next = after(receivers[0], ref_next)
+    (injected,) = call(
+        functools.partial(inject_kernel, lay),
+        [(2, 2, rows, lateral)],
+        [(8 * rows, lateral)]
+        + [pltpu.VMEM(value.shape, value.dtype) for value in receivers]
+        + [pltpu.SemaphoreType.DMA((4,))],
+        receivers,
+        far=(0, 1, 2, 3),
+        name="injection",
+    )
+    phase_a, slow_parts, injected = after(phase_a, slow_parts, injected)
     sent = call(
         functools.partial(column_kernel, lay, True),
         [pair_piece] * slices,
-        [(2, 2, half, cols)] * 2,
+        column_scratch,
         [*arrived, phase_a, x_forward, x_inverse],
+        far=(ranks + 2,),
         name="columns_first",
     )
+    freq_now, sent = after(slab_freq, sent)
     arrived = [sent[0]] + [exchange(sent[step], step) for step in range(1, slices)]
     (lens,) = call(
         functools.partial(lens_kernel, lay),
         [(2, 2, rows, lateral)],
         [],
-        [slab_freq, ref_slow, slow, slow_other],
+        [freq_now, ref_slow, slow, *slow_parts],
         scalars=(0, 1),
         name="lens",
     )
@@ -515,51 +600,54 @@
     )
     arrived = [sent[0]] + [exchange(sent[step], step) for step in range(1, slices)]
     other = exchange(other, slices)
+    phase_b, freq_rows = call(
+        functools.partial(next_phase_kernel, lay),
+        [phase, (8, cols)],
+        [],
+        [slab_freq, inj_freq, ref_next],
+        scalars=(0, 1, 2),
+        name="phase_second",
+    )
 
     sent = call(
         functools.partial(column_kernel, lay, False),
-        [piece] * ranks,
-        [(2, 2, half, cols)] * 2,
-        [*arrived, phase_b, x_forward, x_inverse],
+        [(2, wide + 8, cols)] + [(2, wide, cols)] * (ranks - 1),
+        column_scratch,
+        [*arrived, phase_b, x_forward, x_inverse, freq_rows],
+        far=(slices + 2,),
         name="columns_second",
     )
-    arrived = [None] * ranks
-    for step in reversed(range(ranks)):
-        arrived[step] = onward(sent[step], step)
-
-    up = [(rank, rank + 1) for rank in range(ranks - 1)]
-    down = [(rank + 1, rank) for rank in range(ranks - 1)]
-
-    def image(own, other, leading, trailing, previous):
-        before = lax.ppermute(trailing, "row", up)
-        after = lax.ppermute(leading, "row", down)
-        args = [own, other, before, after]
-        if previous is not None:
-            args.append(previous)
-        (result,) = call(
-            functools.partial(image_kernel, lay, previous is not None),
-            [(OFF, rows, lateral)],
-            [(2, 2, rows + OFF, lateral)],
-            args,
-            name="image",
-        )
-        return result
-
-    previous = image(
-        own,
-        other,
-        jnp.stack([own[:, :HALF], other[:, :HALF]]),
-        jnp.stack([own[:, rows - HALF :], other[:, rows - HALF :]]),
-        None,
-    )
-    wave_out, own, other, leading, trailing = call(
+    arrived = [onward(value, step) for step, value in enumerate(sent)]
+
+    def beside(rows_at, pairs):
+        planes = [own[0], own[1], other[0], other[1], slow]
+        return lax.ppermute(jnp.stack([plane[rows_at] for plane in planes]), "row", pairs)
+
+    before = beside(slice(rows - HALF, rows), [(rank, rank + 1) for rank in range(ranks - 1)])
+    behind = beside(slice(0, HALF), [(rank + 1, rank) for rank in range(ranks - 1)])
+    (previous,) = call(
+        functools.partial(image_kernel, lay),
+        [(OFF, rows, lateral)],
+        [(2, 2, wide, lateral)],
+        [own, other, before, behind],
+        name="image_first",
+    )
+    wave_out, result = call(
         functools.partial(last_kernel, lay),
-        [flat, block, block, edge, edge],
-        [(2, 2, rows, lateral)],
-        [*arrived, last_lens, y_inverse],
-        name="columns_to_rows",
-    )
-    result = image(own, other, leading, trailing, previous)
+        [flat, (OFF, rows, lateral)],
+        [
+            (2, wide, lateral),
+            (2, 2, wide, lateral),
+            flat,
+            (OFF, rows, lateral),
+            pltpu.SemaphoreType.DMA(()),
+            pltpu.SemaphoreType.DMA((OFF,)),
+        ],
+        [*arrived, slow, ref_slow, before, behind, y_inverse, previous],
+        scalars=(ranks + 1,),
+        outside=True,
+        name="last_rows_and_image",
+    )
     return wave_out.reshape(waves.shape), result[None]
 
 

time: 88.6 us -> 77.9 us (0.88)
  starting transfers between devices: 30.6 us -> 25.3 us
  local copies, waits for them, and re-layouts: 5.31 us -> 1.04 us
    ppermute x6 -> x4, waiting for transfers between devices: 2.13 us -> 19 us  [the longest x2 18.1 us: beside(): lax.ppermute(jnp.stack([plane[rows_at] for plane in planes]), 'row', pairs)]
    ppermute x4, waiting for transfers between devices: 12.8 us -> 0.01 us  [onward(): return lax.ppermute(value, ('depth', 'row'), pairs)]
    ppermute x6 -> x4, starting transfers between devices: 17.9 us -> 11 us  [the longest x2 6.09 us: beside(): lax.ppermute(jnp.stack([plane[rows_at] for plane in planes]), 'row', pairs)]
    unnamed x22 -> x8, local copies, waits for them, and re-layouts: 5.3 us -> 0.02 us
    ppermute x7, waiting for transfers between devices: 6.58 us -> 1.78 us  [exchange(): lax.ppermute(value, 'row', [(rank, rank ^ step) for rank in range(ranks)])]
    ppermute x7, starting transfers between devices: 6.65 us -> 8.42 us  [exchange(): lax.ppermute(value, 'row', [(rank, rank ^ step) for rank in range(ranks)])]
    dynamic_slice x0 -> x1, local copies, waits for them, and re-layouts: none -> 1 us  [local(): lax.dynamic_slice_in_dim(slow, shot * share, share)]
  transfers between devices with their start and end apart: 17 -> 15, of which waited for: 7 -> 6; matrix products, arithmetic and copies ran while one was open for 0% -> 0% of each run, Pallas kernels for 21% -> 22%
where the time goes in v1:
time: 77.9 us; the launch traced here: 77.5 us
  Pallas kernels  27.3 us (35%)
  starting transfers between devices  25.3 us (32%)
  waiting for transfers between devices  20.8 us (27%)
  between operations  2.98 us (4%)
  local copies, waits for them, and re-layouts  1.04 us (1%)
    pallas_call x10, Pallas kernels, call(): pl.pallas_call(kernel, out_shape=shapes, in_specs=[smem if i in scalars e...  27.3 us
    ppermute x2, waiting for transfers between devices, beside(): lax.ppermute(jnp.stack([plane[rows_at] for plane in planes]), 'row', pairs)  18.1 us
    ppermute x7, starting transfers between devices, exchange(): lax.ppermute(value, 'row', [(rank, rank ^ step) for rank in range(ranks)])  8.42 us
    ppermute x2, starting transfers between devices, beside(): lax.ppermute(jnp.stack([plane[rows_at] for plane in planes]), 'row', pairs)  6.09 us
    ppermute x4, starting transfers between devices, onward(): return lax.ppermute(value, ('depth', 'row'), pairs)  5.89 us
    ppermute x1, starting transfers between devices, local(): lax.ppermute(ref_sent, 'depth', [(i, (i - 1) % groups) for i in range(gro...  3.55 us
    ppermute x7, waiting for transfers between devices, exchange(): lax.ppermute(value, 'row', [(rank, rank ^ step) for rank in range(ranks)])  1.78 us
  transfers between devices with their start and end apart: 15, of which 6 were waited for; matrix products, arithmetic and copies ran while one was open for 0% of the time, Pallas kernels for 22%

profile of v1, /device:TPU:1, one launch (start us, length us, event | category | flops | bytes accessed | tf_op | source)
XLA Modules:
  0.0 77.5 jit_solution(1381522813358619197)
XLA Ops:
  0.6 1.0 %dynamic-slice_bitcast_fusion = f32[64,512]{1,0:T(8,128)S(1)} fusion(f32[1,128,512]{2,1,0:T(8,128)} %param.15, s32[]{:T(128)S(6)} %select_n.3), kind=kLoop, calls=%fused_computation | loop fusion | bytes 262148 | tf_op jit(solution)/shard_map/dynamic_slice | solution.py:523
  1.7 2.1 %collective-permute-start = (f32[64,512]{1,0:T(8,128)S(1)}, f32[64,512]{1,0:T(8,128)S(1)}, u32[]{:S(2)}, u32[]{:S(2)}) collective-permute-start(f32[64,512]{1,0:T(8,128)S(1)} %dynamic-slice_bitcast_fusion), channel_id=1, source_target_pairs={{0,2},{1,3},{2,0},{3,1},{4,6},{5,7},{6,4},{7,5},{8,10},{9,11},{10,... | collective-permute-start | bytes 393224 | tf_op jit(solution)/shard_map/ppermute | solution.py:502
  3.8 2.6 %rows_to_columns.1 = (f32[2,128,256]{2,1,0:T(8,128)S(1)}, f32[2,128,256]{2,1,0:T(8,128)S(1)}, f32[2,128,256]{2,1,0:T(8,128)S(1)}, f32[2,128,256]{2,1,0:T(8,128)S(1)}) custom-call(f32[2048,128]{1,0:T(8,128)} %bitcast.12, bf16[2,2,2,256,256]{4,3,2,1,0:T(8,128)(2,1)} %constant.23.clone.refs_1_.refs_5_), custom_call_target="tpu_custom_call" | custom-call | flops 1 | bytes 1 | tf_op jit(solution)/shard_map/rows_to_columns/pallas_call | solution.py:473
  7.0 1.1 %collective-permute-start.2 = (f32[2,128,256]{2,1,0:T(8,128)S(1)}, f32[2,128,256]{2,1,0:T(8,128)S(1)}, u32[]{:S(2)}, u32[]{:S(2)}) collective-permute-start(f32[2,128,256]{2,1,0:T(8,128)S(1)} %get-tuple-element.41), channel_id=1, source_target_pairs={{0,2},{1,3},{2,0},{3,1},{4,6},{5,7},{6,4},{7,5},{8,10},{9,11},{10,... | collective-permute-start | bytes 786440 | tf_op jit(solution)/shard_map/ppermute | solution.py:502
  8.1 1.7 %collective-permute-start.3 = (f32[2,128,256]{2,1,0:T(8,128)S(1)}, f32[2,128,256]{2,1,0:T(8,128)S(1)}, u32[]{:S(2)}, u32[]{:S(2)}) collective-permute-start(f32[2,128,256]{2,1,0:T(8,128)S(1)} %get-tuple-element.42), channel_id=1, source_target_pairs={{0,3},{1,2},{2,1},{3,0},{4,7},{5,6},{6,5},{7,4},{8,11},{9,10},{10,... | collective-permute-start | bytes 786440 | tf_op jit(solution)/shard_map/ppermute | solution.py:502
  10.0 1.4 %collective-permute-start.4 = (f32[64,512]{1,0:T(8,128)S(1)}, f32[64,512]{1,0:T(8,128)S(1)}, u32[]{:S(2)}, u32[]{:S(2)}) collective-permute-start(f32[64,512]{1,0:T(8,128)S(1)} %collective-permute-done.refs_0_), channel_id=1, source_target_pairs={{0,16},{16,0},{1,17},{17,1},{2,18},{18,2},{3,19},{19,3},{4,20},{20... | collective-permute-start | bytes 393224 | tf_op jit(solution)/shard_map/ppermute | solution.py:551
  12.6 1.2 %phase_first.1.refs_4_ = f32[2,2,256,256]{3,2,1,0:T(8,128)S(1)} custom-call(f32[1,1]{1,0:T(1,128)S(6)} %copy.16.freq, f32[1]{0:T(128)S(6)} %copy.17.ref_own.refs_5_), custom_call_target="tpu_custom_call" | custom-call | flops 1 | bytes 1 | tf_op jit(solution)/shard_map/phase_first/pallas_call | solution.py:473
  13.8 3.6 %collective-permute-start.5 = (f32[1]{0:T(128)}, f32[1]{0:T(128)}, u32[]{:S(2)}, u32[]{:S(2)}) collective-permute-start(f32[1]{0:T(128)} %param.16), channel_id=1, source_target_pairs={{0,12},{4,0},{8,4},{12,8},{1,13},{5,1},{9,5},{13,9},{2,14},{6,2},{... | collective-permute-start | bytes 20 | tf_op jit(solution)/shard_map/ppermute | solution.py:554
  17.4 0.9 %collective-permute-done.5.ref_next = f32[1]{0:T(128)} collective-permute-done((f32[1]{0:T(128)}, f32[1]{0:T(128)}, u32[]{:S(2)}, u32[]{:S(2)}) %collective-permute-start.5) | collective-permute-done | bytes 36 | tf_op jit(solution)/shard_map/ppermute | solution.py:554
  18.2 5.4 %injection.1.refs_3_ = f32[2,2,128,512]{3,2,1,0:T(8,128)S(1)} custom-call(s32[1,2]{1,0:T(1,128)} %bitcast.15, f32[1,2]{1,0:T(1,128)} %bitcast.16, f32[2,4096]{1,0:T(2,128)} %bitcast.13, s32[2,4096]{1,0:T(2,128)} %bitcast.14), custom_call_target="tpu_custom_call" | custom-call | flops 1 | bytes 1 | tf_op jit(solution)/shard_map/injection/pallas_call | solution.py:473
  23.7 3.4 %columns_first.1 = (f32[2,2,128,256]{3,2,1,0:T(8,128)S(1)}, f32[2,2,128,256]{3,2,1,0:T(8,128)S(1)}) custom-call(f32[2,128,256]{2,1,0:T(8,128)S(1)} %get-tuple-element.39.refs_0_, f32[2,128,256]{2,1,0:T(8,128)S(1)} %collective-permute-done.1.refs_1_, f32[2,128,256]{2,1,0:T(8,128)S(1)} %collective-permute-done.2.refs_2_, ...), custom_call_target="tpu_custom_call" | custom-call | flops 1 | bytes 1 | tf_op jit(solution)/shard_map/columns_first/pallas_call | solution.py:473
  27.1 1.7 %collective-permute-start.6 = (f32[2,2,128,256]{3,2,1,0:T(8,128)S(1)}, f32[2,2,128,256]{3,2,1,0:T(8,128)S(1)}, u32[]{:S(2)}, u32[]{:S(2)}) collective-permute-start(f32[2,2,128,256]{3,2,1,0:T(8,128)S(1)} %get-tuple-element.50), channel_id=1, source_target_pairs={{0,1},{1,0},{2,3},{3,2},{4,5},{5,4},{6,7},{7,6},{8,9},{9,8},{10,11... | collective-permute-start | bytes 1572872 | tf_op jit(solution)/shard_map/ppermute | solution.py:502
  30.3 2.3 %columns_to_columns.1 = (f32[2,128,512]{2,1,0:T(8,128)S(1)}, f32[2,128,512]{2,1,0:T(8,128)S(1)}, f32[2,2,128,256]{3,2,1,0:T(8,128)S(1)}, f32[2,2,128,256]{3,2,1,0:T(8,128)S(1)}) custom-call(f32[2,2,128,256]{3,2,1,0:T(8,128)S(1)} %get-tuple-element.49.refs_0_, f32[2,2,128,256]{3,2,1,0:T(8,128)S(1)} %collective-permute-done.6.refs_1_, ...), custom_call_target="tpu_custom_call" | custom-call | flops 1 | bytes 1 | tf_op jit(solution)/shard_map/columns_to_columns/pallas_call | solution.py:473
  33.0 1.2 %collective-permute-start.12 = (f32[2,128,512]{2,1,0:T(8,128)S(1)}, f32[2,128,512]{2,1,0:T(8,128)S(1)}, u32[]{:S(2)}, u32[]{:S(2)}) collective-permute-start(f32[2,128,512]{2,1,0:T(8,128)S(1)} %get-tuple-element.65), channel_id=1, source_target_pairs={{0,2},{1,3},{2,0},{3,1},{4,6},{5,7},{6,4},{7,5},{8,10},{9,11},{10,... | collective-permute-start | bytes 1572872 | tf_op jit(solution)/shard_map/ppermute | solution.py:502
  34.9 1.8 %phase_second.1 = (f32[2,2,256,256]{3,2,1,0:T(8,128)S(1)}, f32[8,256]{1,0:T(8,128)S(1)}) custom-call(f32[1,1]{1,0:T(1,128)S(6)} %copy.16.freq, f32[1,1]{1,0:T(1,128)S(6)} %copy.18.freq_injected, f32[1]{0:T(128)} %collective-permute-done.5.ref_next), custom_call_target="tpu_custom_call" | custom-call | flops 1 | bytes 1 | tf_op jit(solution)/shard_map/phase_second/pallas_call | solution.py:473
  36.8 3.3 %columns_second.1 = (f32[2,152,256]{2,1,0:T(8,128)S(1)}, f32[2,144,256]{2,1,0:T(8,128)S(1)}, f32[2,144,256]{2,1,0:T(8,128)S(1)}, f32[2,144,256]{2,1,0:T(8,128)S(1)}) custom-call(f32[2,2,128,256]{3,2,1,0:T(8,128)S(1)} %get-tuple-element.55.refs_0_, f32[2,2,128,256]{3,2,1,0:T(8,128)S(1)} %collective-permute-done.7.refs_1_, ...), custom_call_target="tpu_custom_call" | custom-call | flops 1 | bytes 1 | tf_op jit(solution)/shard_map/columns_second/pallas_call | solution.py:473
  40.3 1.3 %collective-permute-start.10 = (f32[2,144,256]{2,1,0:T(8,128)S(1)}, f32[2,144,256]{2,1,0:T(8,128)S(1)}, u32[]{:S(2)}, u32[]{:S(2)}) collective-permute-start(f32[2,144,256]{2,1,0:T(8,128)S(1)} %get-tuple-element.62), channel_id=1, source_target_pairs={{0,6},{1,7},{2,4},{3,5},{4,10},{5,11},{6,8},{7,9},{8,14},{9,15},{1... | collective-permute-start | bytes 884744 | tf_op jit(solution)/shard_map/ppermute | solution.py:510
  41.6 4.3 %collective-permute-start.11 = (f32[2,144,256]{2,1,0:T(8,128)S(1)}, f32[2,144,256]{2,1,0:T(8,128)S(1)}, u32[]{:S(2)}, u32[]{:S(2)}) collective-permute-start(f32[2,144,256]{2,1,0:T(8,128)S(1)} %get-tuple-element.63), channel_id=1, source_target_pairs={{0,7},{1,6},{2,5},{3,4},{4,11},{5,10},{6,9},{7,8},{8,15},{9,14},{1... | collective-permute-start | bytes 884744 | tf_op jit(solution)/shard_map/ppermute | solution.py:510
  46.4 4.0 %collective-permute-start.13 = (f32[5,8,512]{2,1,0:T(8,128)S(1)}, f32[5,8,512]{2,1,0:T(8,128)S(1)}, u32[]{:S(2)}, u32[]{:S(2)}) collective-permute-start(f32[5,8,512]{2,1,0:T(8,128)S(1)} %pad_maximum_fusion), channel_id=1, source_target_pairs={{0,1},{1,2},{2,3},{4,5},{5,6},{6,7},{8,9},{9,10},{10,11},{12,13},{... | collective-permute-start | bytes 245768 | tf_op jit(solution)/shard_map/ppermute | solution.py:624
  50.4 13.5 %collective-permute-done.13.before.refs_6_ = f32[5,8,512]{2,1,0:T(8,128)S(1)} collective-permute-done((f32[5,8,512]{2,1,0:T(8,128)S(1)}, f32[5,8,512]{2,1,0:T(8,128)S(1)}, u32[]{:S(2)}, u32[]{:S(2)}) %collective-permute-start.13) | collective-permute-done | bytes 81952 | tf_op jit(solution)/shard_map/ppermute | solution.py:624
  63.9 2.1 %collective-permute-start.14 = (f32[5,8,512]{2,1,0:T(8,128)S(1)}, f32[5,8,512]{2,1,0:T(8,128)S(1)}, u32[]{:S(2)}, u32[]{:S(2)}) collective-permute-start(f32[5,8,512]{2,1,0:T(8,128)S(1)} %pad_maximum_fusion.1), channel_id=1, source_target_pairs={{1,0},{2,1},{3,2},{5,4},{6,5},{7,6},{9,8},{10,9},{11,10},{13,12},{... | collective-permute-start | bytes 245768 | tf_op jit(solution)/shard_map/ppermute | solution.py:624
  66.0 4.7 %collective-permute-done.14.after.refs_7_ = f32[5,8,512]{2,1,0:T(8,128)S(1)} collective-permute-done((f32[5,8,512]{2,1,0:T(8,128)S(1)}, f32[5,8,512]{2,1,0:T(8,128)S(1)}, u32[]{:S(2)}, u32[]{:S(2)}) %collective-permute-start.14) | collective-permute-done | bytes 81952 | tf_op jit(solution)/shard_map/ppermute | solution.py:624
  70.7 1.7 %image_first.1.refs_9_ = f32[16,128,512]{2,1,0:T(8,128)S(1)} custom-call(f32[2,128,512]{2,1,0:T(8,128)S(1)} %get-tuple-element.64.own, f32[2,128,512]{2,1,0:T(8,128)S(1)} %collective-permute-done.12.other, f32[5,8,512]{2,1,0:T(8,128)S(1)} %collective-permute-done.13.before.refs_6_, f32[5,8,512]{2,1,0:T(8,128)S(1)} %collective-permute-done.14.after.refs_7_), custom_call_target="tpu_custom_call" | custom-call | flops 1 | bytes 1 | tf_op jit(solution)/shard_map/image_first/pallas_call | solution.py:473
  72.4 4.9 %last_rows_and_image.1 = (f32[2048,128]{1,0:T(8,128)}, f32[16,128,512]{2,1,0:T(8,128)}) custom-call(f32[2,152,256]{2,1,0:T(8,128)S(1)} %collective-permute-done.8.refs_0_, f32[2,144,256]{2,1,0:T(8,128)S(1)} %collective-permute-done.9.refs_1_, f32[2,144,256]{2,1,0:T(8,128)S(1)} %collective-permute-done.10.refs_2_, ...), custom_call_target="tpu_custom_call" | custom-call | flops 1 | bytes 1 | tf_op jit(solution)/shard_map/last_rows_and_image/pallas_call | solution.py:473
  (30 shorter events, 3.5 us)
Async XLA Ops:
  0.6 23.1 %copy-start.2 = (bf16[2,2,512,256]{3,2,1,0:T(8,128)(2,1)S(1)}, bf16[2,2,512,256]{3,2,1,0:T(8,128)(2,1)}, u32[]{:S(2)}) copy-start(bf16[2,2,512,256]{3,2,1,0:T(8,128)(2,1)} %constant.21.clone.refs_5_.refs_3_) | copy-start | bytes 3145732
  1.7 5.3 %collective-permute-start = (f32[64,512]{1,0:T(8,128)S(1)}, f32[64,512]{1,0:T(8,128)S(1)}, u32[]{:S(2)}, u32[]{:S(2)}) collective-permute-start(f32[64,512]{1,0:T(8,128)S(1)} %dynamic-slice_bitcast_fusion), channel_id=1, source_target_pairs={{0,2},{1,3},{2,0},{3,1},{4,6},{5,7},{6,4},{7,5},{8,10},{9,11},{10,... | collective-permute-start | bytes 393224 | tf_op jit(solution)/shard_map/ppermute | solution.py:502
  3.8 25.0 %copy-start.3 = (f32[1,128,512]{2,1,0:T(8,128)S(1)}, f32[1,128,512]{2,1,0:T(8,128)}, u32[]{:S(2)}) copy-start(f32[1,128,512]{2,1,0:T(8,128)} %param.15) | copy-start | bytes 786436
  6.4 24.0 %copy-start = (bf16[2,2,2,256,256]{4,3,2,1,0:T(8,128)(2,1)S(1)}, bf16[2,2,2,256,256]{4,3,2,1,0:T(8,128)(2,1)}, u32[]{:S(2)}) copy-start(bf16[2,2,2,256,256]{4,3,2,1,0:T(8,128)(2,1)} %constant.23.clone.refs_1_.refs_5_) | copy-start | bytes 3145732
  6.4 23.9 %copy-start.1 = (bf16[2,2,2,256,256]{4,3,2,1,0:T(8,128)(2,1)S(1)}, bf16[2,2,2,256,256]{4,3,2,1,0:T(8,128)(2,1)}, u32[]{:S(2)}) copy-start(bf16[2,2,2,256,256]{4,3,2,1,0:T(8,128)(2,1)} %constant.24.clone.refs_4_.refs_8_) | copy-start | bytes 3145732
  7.0 16.7 %collective-permute-start.2 = (f32[2,128,256]{2,1,0:T(8,128)S(1)}, f32[2,128,256]{2,1,0:T(8,128)S(1)}, u32[]{:S(2)}, u32[]{:S(2)}) collective-permute-start(f32[2,128,256]{2,1,0:T(8,128)S(1)} %get-tuple-element.41), channel_id=1, source_target_pairs={{0,2},{1,3},{2,0},{3,1},{4,6},{5,7},{6,4},{7,5},{8,10},{9,11},{10,... | collective-permute-start | bytes 786440 | tf_op jit(solution)/shard_map/ppermute | solution.py:502
  8.1 15.6 %collective-permute-start.3 = (f32[2,128,256]{2,1,0:T(8,128)S(1)}, f32[2,128,256]{2,1,0:T(8,128)S(1)}, u32[]{:S(2)}, u32[]{:S(2)}) collective-permute-start(f32[2,128,256]{2,1,0:T(8,128)S(1)} %get-tuple-element.42), channel_id=1, source_target_pairs={{0,3},{1,2},{2,1},{3,0},{4,7},{5,6},{6,5},{7,4},{8,11},{9,10},{10,... | collective-permute-start | bytes 786440 | tf_op jit(solution)/shard_map/ppermute | solution.py:502
  9.8 13.8 %collective-permute-start.1 = (f32[2,128,256]{2,1,0:T(8,128)S(1)}, f32[2,128,256]{2,1,0:T(8,128)S(1)}, u32[]{:S(2)}, u32[]{:S(2)}) collective-permute-start(f32[2,128,256]{2,1,0:T(8,128)S(1)} %get-tuple-element.40), channel_id=1, source_target_pairs={{0,1},{1,0},{2,3},{3,2},{4,5},{5,4},{6,7},{7,6},{8,9},{9,8},{10,11... | collective-permute-start | bytes 786440 | tf_op jit(solution)/shard_map/ppermute | solution.py:502
  10.0 13.7 %collective-permute-start.4 = (f32[64,512]{1,0:T(8,128)S(1)}, f32[64,512]{1,0:T(8,128)S(1)}, u32[]{:S(2)}, u32[]{:S(2)}) collective-permute-start(f32[64,512]{1,0:T(8,128)S(1)} %collective-permute-done.refs_0_), channel_id=1, source_target_pairs={{0,16},{16,0},{1,17},{17,1},{2,18},{18,2},{3,19},{19,3},{4,20},{20... | collective-permute-start | bytes 393224 | tf_op jit(solution)/shard_map/ppermute | solution.py:551
  13.8 4.4 %collective-permute-start.5 = (f32[1]{0:T(128)}, f32[1]{0:T(128)}, u32[]{:S(2)}, u32[]{:S(2)}) collective-permute-start(f32[1]{0:T(128)} %param.16), channel_id=1, source_target_pairs={{0,12},{4,0},{8,4},{12,8},{1,13},{5,1},{9,5},{13,9},{2,14},{6,2},{... | collective-permute-start | bytes 20 | tf_op jit(solution)/shard_map/ppermute | solution.py:554
  27.1 3.2 %collective-permute-start.6 = (f32[2,2,128,256]{3,2,1,0:T(8,128)S(1)}, f32[2,2,128,256]{3,2,1,0:T(8,128)S(1)}, u32[]{:S(2)}, u32[]{:S(2)}) collective-permute-start(f32[2,2,128,256]{3,2,1,0:T(8,128)S(1)} %get-tuple-element.50), channel_id=1, source_target_pairs={{0,1},{1,0},{2,3},{3,2},{4,5},{5,4},{6,7},{7,6},{8,9},{9,8},{10,11... | collective-permute-start | bytes 1572872 | tf_op jit(solution)/shard_map/ppermute | solution.py:502
  32.6 4.2 %collective-permute-start.7 = (f32[2,2,128,256]{3,2,1,0:T(8,128)S(1)}, f32[2,2,128,256]{3,2,1,0:T(8,128)S(1)}, u32[]{:S(2)}, u32[]{:S(2)}) collective-permute-start(f32[2,2,128,256]{3,2,1,0:T(8,128)S(1)} %get-tuple-element.56), channel_id=1, source_target_pairs={{0,1},{1,0},{2,3},{3,2},{4,5},{5,4},{6,7},{7,6},{8,9},{9,8},{10,11... | collective-permute-start | bytes 1572872 | tf_op jit(solution)/shard_map/ppermute | solution.py:502
  33.0 13.4 %collective-permute-start.12 = (f32[2,128,512]{2,1,0:T(8,128)S(1)}, f32[2,128,512]{2,1,0:T(8,128)S(1)}, u32[]{:S(2)}, u32[]{:S(2)}) collective-permute-start(f32[2,128,512]{2,1,0:T(8,128)S(1)} %get-tuple-element.65), channel_id=1, source_target_pairs={{0,2},{1,3},{2,0},{3,1},{4,6},{5,7},{6,4},{7,5},{8,10},{9,11},{10,... | collective-permute-start | bytes 1572872 | tf_op jit(solution)/shard_map/ppermute | solution.py:502
  40.1 32.3 %collective-permute-start.9 = (f32[2,144,256]{2,1,0:T(8,128)S(1)}, f32[2,144,256]{2,1,0:T(8,128)S(1)}, u32[]{:S(2)}, u32[]{:S(2)}) collective-permute-start(f32[2,144,256]{2,1,0:T(8,128)S(1)} %get-tuple-element.61), channel_id=1, source_target_pairs={{0,5},{1,4},{2,7},{3,6},{4,9},{5,8},{6,11},{7,10},{8,13},{9,12},{1... | collective-permute-start | bytes 884744 | tf_op jit(solution)/shard_map/ppermute | solution.py:510
  40.3 32.0 %collective-permute-start.10 = (f32[2,144,256]{2,1,0:T(8,128)S(1)}, f32[2,144,256]{2,1,0:T(8,128)S(1)}, u32[]{:S(2)}, u32[]{:S(2)}) collective-permute-start(f32[2,144,256]{2,1,0:T(8,128)S(1)} %get-tuple-element.62), channel_id=1, source_target_pairs={{0,6},{1,7},{2,4},{3,5},{4,10},{5,11},{6,8},{7,9},{8,14},{9,15},{1... | collective-permute-start | bytes 884744 | tf_op jit(solution)/shard_map/ppermute | solution.py:510
  41.6 30.8 %collective-permute-start.11 = (f32[2,144,256]{2,1,0:T(8,128)S(1)}, f32[2,144,256]{2,1,0:T(8,128)S(1)}, u32[]{:S(2)}, u32[]{:S(2)}) collective-permute-start(f32[2,144,256]{2,1,0:T(8,128)S(1)} %get-tuple-element.63), channel_id=1, source_target_pairs={{0,7},{1,6},{2,5},{3,4},{4,11},{5,10},{6,9},{7,8},{8,15},{9,14},{1... | collective-permute-start | bytes 884744 | tf_op jit(solution)/shard_map/ppermute | solution.py:510
  45.9 26.5 %collective-permute-start.8 = (f32[2,152,256]{2,1,0:T(8,128)S(1)}, f32[2,152,256]{2,1,0:T(8,128)S(1)}, u32[]{:S(2)}, u32[]{:S(2)}) collective-permute-start(f32[2,152,256]{2,1,0:T(8,128)S(1)} %get-tuple-element.60), channel_id=1, source_target_pairs={{0,4},{1,5},{2,6},{3,7},{4,8},{5,9},{6,10},{7,11},{8,12},{9,13},{1... | collective-permute-start | bytes 933896 | tf_op jit(solution)/shard_map/ppermute | solution.py:510
  46.4 17.5 %collective-permute-start.13 = (f32[5,8,512]{2,1,0:T(8,128)S(1)}, f32[5,8,512]{2,1,0:T(8,128)S(1)}, u32[]{:S(2)}, u32[]{:S(2)}) collective-permute-start(f32[5,8,512]{2,1,0:T(8,128)S(1)} %pad_maximum_fusion), channel_id=1, source_target_pairs={{0,1},{1,2},{2,3},{4,5},{5,6},{6,7},{8,9},{9,10},{10,11},{12,13},{... | collective-permute-start | bytes 245768 | tf_op jit(solution)/shard_map/ppermute | solution.py:624
  63.9 6.8 %collective-permute-start.14 = (f32[5,8,512]{2,1,0:T(8,128)S(1)}, f32[5,8,512]{2,1,0:T(8,128)S(1)}, u32[]{:S(2)}, u32[]{:S(2)}) collective-permute-start(f32[5,8,512]{2,1,0:T(8,128)S(1)} %pad_maximum_fusion.1), channel_id=1, source_target_pairs={{1,0},{2,1},{3,2},{5,4},{6,5},{7,6},{9,8},{10,9},{11,10},{13,12},{... | collective-permute-start | bytes 245768 | tf_op jit(solution)/shard_map/ppermute | solution.py:624

commit v2 on v1

--- a/solution.py
+++ b/solution.py
@@ -186,23 +186,17 @@
                 difference = low - high
             parity_parts[0, part, at, :] = low + high
             parity_parts[1, part, at, :] = difference
-    sums = []
+    shifted = []
     for parity in range(2):
         real, imag = along_x(
             parity_parts[parity, 0], parity_parts[parity, 1], x_forward, parity, False
         )
         phase_real, phase_imag = phase[0, parity], phase[1, parity]
-        if parity == 0:
-            x_inverse_copy.wait()
-        sums.append(
-            along_x(
-                real * phase_real - imag * phase_imag,
-                real * phase_imag + imag * phase_real,
-                x_inverse,
-                parity,
-                True,
-            )
-        )
+        shifted.append(
+            (real * phase_real - imag * phase_imag, real * phase_imag + imag * phase_real)
+        )
+    x_inverse_copy.wait()
+    sums = [along_x(*shifted[parity], x_inverse, parity, True) for parity in range(2)]
     for part in range(2):
         whole[part, :HALF] = jnp.zeros((HALF, lay.cols), F32)
         whole[part, HALF : HALF + lay.half] = sums[0][part] + sums[1][part]
@@ -279,14 +273,15 @@
 
 def last_kernel(lay, *refs):
     pieces = refs[: lay.ranks]
-    slow, ref_own, before, behind, y_inverse, previous = refs[lay.ranks : lay.ranks + 6]
-    wave_out, image = refs[lay.ranks + 6 : lay.ranks + 8]
-    lens, fields, wave_buffer, image_buffer, wave_sent, image_sent = refs[lay.ranks + 8 :]
+    slow, scalars, inner, outer, y_inverse, previous = refs[lay.ranks : lay.ranks + 6]
+    image_top, image_bottom, wave_out, image = refs[lay.ranks + 6 : lay.ranks + 10]
+    lens, fields, wave_buffer, image_buffer, wave_sent, image_sent = refs[-6:]
     index, side = lay.place()
     freq = pieces[0][0, lay.wide : lay.wide + 1, 0:1]
     end = HALF + lay.rows
-    for start, values in ((0, before[4]), (HALF, slow[...]), (end, behind[4])):
-        sine, cosine = sin_cos(freq * (values - ref_own[0]) * DZ)
+    before, behind = beside(inner, outer, 4)
+    for start, values in ((0, before), (HALF, slow[...]), (end, behind)):
+        sine, cosine = sin_cos(freq * (values - scalars[1:2, 0:1]) * DZ)
         lens[0, start : start + values.shape[0]] = cosine
         lens[1, start : start + values.shape[0]] = sine
     for turn in range(2):
@@ -315,8 +310,12 @@
                 ]
     copies = [pltpu.make_async_copy(wave_buffer, wave_out, wave_sent)]
     copies[0].start()
+    stop = lay.rows - HALF
     for offset in range(OFF):
-        image_buffer[offset] = previous[offset] + correlation(lay, fields, offset)
+        value = correlation(fields, offset, lay.rows)
+        image_buffer[offset, :HALF] = image_top[offset] + value[:HALF]
+        image_buffer[offset, HALF:stop] = previous[offset, HALF:stop] + value[HALF:stop]
+        image_buffer[offset, stop:] = image_bottom[offset] + value[stop:]
         copies.append(
             pltpu.make_async_copy(
                 image_buffer.at[offset], image.at[offset], image_sent.at[offset]
@@ -327,30 +326,58 @@
         copy.wait()
 
 
-def correlation(lay, fields, offset):
+def correlation(fields, offset, rows):
     lag = offset - HALF
-    source = pl.ds(HALF - lag, lay.rows)
-    receiver = pl.ds(HALF + lag, lay.rows)
+    source = pl.ds(HALF - lag, rows)
+    receiver = pl.ds(HALF + lag, rows)
     return (
         fields[0, 0, source] * fields[1, 0, receiver]
         + fields[0, 1, source] * fields[1, 1, receiver]
     )
 
 
-def image_kernel(lay, own, other, before, after, result, fields):
+def beside(inner, outer, plane):
+    is_odd = lax.axis_index("row") % 2 == 1
+    one, two = inner[plane], outer[plane]
+    return jnp.where(is_odd, one, two), jnp.where(is_odd, two, one)
+
+
+def ends_kernel(lay, own, other, inner, outer, image_top, image_bottom, top, bottom):
     rank = lax.axis_index("row")
     side = rank // lay.slices
     side_before = (rank + lay.ranks - 1) % lay.ranks // lay.slices
-    side_after = (rank + 1) % lay.ranks // lay.slices
+    side_behind = (rank + 1) % lay.ranks // lay.slices
+    start = lay.rows - 2 * HALF
+    for part in range(2):
+        for field, block in ((side, own), (1 - side, other)):
+            top[field, part, HALF:] = block[part, : 2 * HALF]
+            bottom[field, part, : 2 * HALF] = block[part, start:]
+        for field in range(2):
+            before, _ = beside(inner, outer, 2 * (field ^ side_before) + part)
+            _, behind = beside(inner, outer, 2 * (field ^ side_behind) + part)
+            top[field, part, :HALF] = before
+            bottom[field, part, 2 * HALF :] = behind
+    for offset in range(OFF):
+        image_top[offset] = correlation(top, offset, HALF)
+        image_bottom[offset] = correlation(bottom, offset, HALF)
+
+
+def image_kernel(lay, own, other, slow, result, inner, outer, fields):
+    _, side = lay.place()
     end = HALF + lay.rows
-    for part in range(2):
-        fields[side, part, HALF:end] = own[part]
-        fields[1 - side, part, HALF:end] = other[part]
-        for field in range(2):
-            fields[field, part, :HALF] = before[2 * (field ^ side_before) + part]
-            fields[field, part, end:] = after[2 * (field ^ side_after) + part]
+    nothing = jnp.zeros((2, HALF, lay.lateral), F32)
+    for field, block in ((side, own), (1 - side, other)):
+        fields[field, :, :HALF] = nothing
+        fields[field, :, HALF:end] = block[...]
+        fields[field, :, end:] = nothing
     for offset in range(OFF):
-        result[offset] = correlation(lay, fields, offset)
+        result[offset] = correlation(fields, offset, lay.rows)
+    is_odd = lax.axis_index("row") % 2 == 1
+    planes = [own.at[0], own.at[1], other.at[0], other.at[1], slow]
+    for at, plane in enumerate(planes):
+        first, last = plane[:HALF], plane[lay.rows - HALF :]
+        inner[at] = jnp.where(is_odd, first, last)
+        outer[at] = jnp.where(is_odd, last, first)
 
 
 def fill_phase(lay, wave_number, phase):
@@ -377,14 +404,14 @@
         phase[1, parity] = jnp.where(runs, sine, 0.0) * sign
 
 
-def phase_kernel(lay, freq, ref_own, phase):
-    fill_phase(lay, freq[0, 0] * ref_own[0], phase)
-
-
-def next_phase_kernel(lay, freq, freq_injected, ref_next, phase, freq_rows):
+def phase_kernel(lay, scalars, phase):
+    fill_phase(lay, scalars[0:1, 0:1] * scalars[1:2, 0:1], phase)
+
+
+def next_phase_kernel(lay, scalars, scalars_next, phase, freq_rows):
     last = lax.axis_index("depth") == lay.groups - 1
-    freq_now = jnp.where(last, freq_injected[0, 0], freq[0, 0])
-    fill_phase(lay, freq_now * ref_next[0], phase)
+    freq_now = jnp.where(last, scalars[2:3, 0:1], scalars[0:1, 0:1])
+    fill_phase(lay, freq_now * scalars_next[1:2, 0:1], phase)
     freq_rows[...] = jnp.zeros((8, lay.cols), F32) + freq_now
 
 
@@ -438,13 +465,14 @@
         injected[part] = value.reshape(2, lay.rows, lay.lateral)
 
 
-def lens_kernel(lay, freq, ref_own, slow, *refs):
+def lens_kernel(lay, scalars, slow, *refs):
     lens = refs[-1]
     _, side = lay.place()
     sign = (1 - 2 * side).astype(F32)
+    freq, ref_own = scalars[0:1, 0:1], scalars[1:2, 0:1]
 
     def store(field, start, values):
-        sine, cosine = sin_cos(sign * freq[0, 0] * (values - ref_own[0]) * DZ)
+        sine, cosine = sin_cos(sign * freq * (values - ref_own) * DZ)
         at = pl.ds(pl.multiple_of(start, 8), values.shape[0])
         lens[0, field, at, :] = cosine
         lens[1, field, at, :] = sine
@@ -460,9 +488,8 @@
     return lax.optimization_barrier(values)
 
 
-def call(kernel, outs, scratch, args, scalars=(), far=(), outside=False, vmem=40, name=None):
+def call(kernel, outs, scratch, args, far=(), outside=False, vmem=40, name=None):
     inside = pl.BlockSpec(memory_space=pltpu.VMEM)
-    smem = pl.BlockSpec(memory_space=pltpu.SMEM)
     outer = pl.BlockSpec(memory_space=pltpu.HBM)
     anywhere = pl.BlockSpec(memory_space=pl.ANY)
     shapes = [jax.ShapeDtypeStruct(shape, F32) for shape in outs]
@@ -473,9 +500,7 @@
     return pl.pallas_call(
         kernel,
         out_shape=shapes,
-        in_specs=[
-            smem if i in scalars else outer if i in far else inside for i in range(len(args))
-        ],
+        in_specs=[outer if i in far else inside for i in range(len(args))],
         out_specs=[anywhere if outside else inside] * len(outs),
         scratch_shapes=[
             pltpu.VMEM(shape, F32) if isinstance(shape, tuple) else shape for shape in scratch
@@ -550,18 +575,22 @@
         pairs = [(shot, shot ^ step) for shot in range(shots)]
         slow_parts.append(lax.ppermute(slow_parts[0], "shots", pairs))
 
-    ref_sent, _ = after(ref_slow, sent[1])
-    ref_next = lax.ppermute(ref_sent, "depth", [(i, (i - 1) % groups) for i in range(groups)])
+    values, _ = after((slab_freq[0, 0], ref_slow[0], inj_freq[0, 0]), sent[1])
+    scalars = jnp.broadcast_to(
+        jnp.pad(jnp.stack(values), (0, 5))[:, None], (8, LANES)
+    )
+    scalars_next = lax.ppermute(
+        scalars, "depth", [(i, (i - 1) % groups) for i in range(groups)]
+    )
     (phase_a,) = call(
         functools.partial(phase_kernel, lay),
         [phase],
         [],
-        [slab_freq, ref_slow],
-        scalars=(0, 1),
+        [scalars],
         name="phase_first",
     )
     receivers = [src_pos[None], wavelet[0], records.reshape(2, -1), rcv_pos.T]
-    receivers[0], ref_next = after(receivers[0], ref_next)
+    receivers[0], scalars_next = after(receivers[0], scalars_next)
     (injected,) = call(
         functools.partial(inject_kernel, lay),
         [(2, 2, rows, lateral)],
@@ -581,16 +610,23 @@
         far=(ranks + 2,),
         name="columns_first",
     )
-    freq_now, sent = after(slab_freq, sent)
+    scalars, scalars_next, sent = after(scalars, scalars_next, sent)
     arrived = [sent[0]] + [exchange(sent[step], step) for step in range(1, slices)]
+    phase_b, freq_rows = call(
+        functools.partial(next_phase_kernel, lay),
+        [phase, (8, cols)],
+        [],
+        [scalars, scalars_next],
+        name="phase_second",
+    )
     (lens,) = call(
         functools.partial(lens_kernel, lay),
         [(2, 2, rows, lateral)],
         [],
-        [freq_now, ref_slow, slow, *slow_parts],
-        scalars=(0, 1),
+        [scalars, slow, *slow_parts],
         name="lens",
     )
+    lens, phase_b = after(lens, phase_b)
     own, other, *sent = call(
         functools.partial(middle_kernel, lay),
         [block, block] + [pair_piece] * slices,
@@ -600,15 +636,6 @@
     )
     arrived = [sent[0]] + [exchange(sent[step], step) for step in range(1, slices)]
     other = exchange(other, slices)
-    phase_b, freq_rows = call(
-        functools.partial(next_phase_kernel, lay),
-        [phase, (8, cols)],
-        [],
-        [slab_freq, inj_freq, ref_next],
-        scalars=(0, 1, 2),
-        name="phase_second",
-    )
-
     sent = call(
         functools.partial(column_kernel, lay, False),
         [(2, wide + 8, cols)] + [(2, wide, cols)] * (ranks - 1),
@@ -619,18 +646,24 @@
     )
     arrived = [onward(value, step) for step, value in enumerate(sent)]
 
-    def beside(rows_at, pairs):
-        planes = [own[0], own[1], other[0], other[1], slow]
-        return lax.ppermute(jnp.stack([plane[rows_at] for plane in planes]), "row", pairs)
-
-    before = beside(slice(rows - HALF, rows), [(rank, rank + 1) for rank in range(ranks - 1)])
-    behind = beside(slice(0, HALF), [(rank + 1, rank) for rank in range(ranks - 1)])
-    (previous,) = call(
+    previous, inner, outer = call(
         functools.partial(image_kernel, lay),
-        [(OFF, rows, lateral)],
+        [(OFF, rows, lateral)] + [(5, HALF, lateral)] * 2,
         [(2, 2, wide, lateral)],
-        [own, other, before, behind],
+        [own, other, slow],
         name="image_first",
+    )
+    inner = exchange(inner, 1)
+    between = [(rank, rank + 1) for rank in range(1, ranks - 1, 2)]
+    outer = lax.ppermute(
+        outer, "row", between + [(target, source) for source, target in between]
+    )
+    image_top, image_bottom = call(
+        functools.partial(ends_kernel, lay),
+        [(OFF, HALF, lateral)] * 2,
+        [(2, 2, 3 * HALF, lateral)] * 2,
+        [own, other, inner, outer],
+        name="image_ends",
     )
     wave_out, result = call(
         functools.partial(last_kernel, lay),
@@ -643,8 +676,7 @@
             pltpu.SemaphoreType.DMA(()),
             pltpu.SemaphoreType.DMA((OFF,)),
         ],
-        [*arrived, slow, ref_slow, before, behind, y_inverse, previous],
-        scalars=(ranks + 1,),
+        [*arrived, slow, scalars, inner, outer, y_inverse, previous, image_top, image_bottom],
         outside=True,
         name="last_rows_and_image",
     )

time: 77.9 us -> 73.9 us (0.949)
  starting transfers between devices: 25.3 us -> 22.8 us
  Pallas kernels: 27.3 us -> 26.3 us
    ppermute x3 -> x2, waiting for transfers between devices: 19 us -> 15 us  [the longest x1 15 us: local(): lax.ppermute(outer, 'row', between + [(target, source) for source, target...]
    ppermute x7 -> x8, waiting for transfers between devices: 1.78 us -> 5.16 us  [exchange(): lax.ppermute(value, 'row', [(rank, rank ^ step) for rank in range(ranks)])]
    ppermute x3 -> x2, starting transfers between devices: 9.64 us -> 6.66 us  [the longest x1 3.34 us: local(): lax.ppermute(outer, 'row', between + [(target, source) for source, target...]
    pallas_call x10 -> x11, Pallas kernels: 27.3 us -> 26.3 us  [call(): pl.pallas_call(kernel, out_shape=shapes, in_specs=[outer if i in far else...]
    ppermute x7 -> x8, starting transfers between devices: 8.42 us -> 8.88 us  [exchange(): lax.ppermute(value, 'row', [(rank, rank ^ step) for rank in range(ranks)])]
  transfers between devices with their start and end apart: 15 -> 15, of which waited for: 6 -> 5; matrix products, arithmetic and copies ran while one was open for 0% -> 0% of each run, Pallas kernels for 22% -> 23%
where the time goes in v2:
time: 73.9 us; the launch traced here: 73.5 us
  Pallas kernels  26.3 us (36%)
  starting transfers between devices  22.8 us (31%)
  waiting for transfers between devices  20.2 us (27%)
  between operations  2.97 us (4%)
  local copies, waits for them, and re-layouts  1.1 us (1%)
    pallas_call x11, Pallas kernels, call(): pl.pallas_call(kernel, out_shape=shapes, in_specs=[outer if i in far else...  26.3 us
    ppermute x1, waiting for transfers between devices, local(): lax.ppermute(outer, 'row', between + [(target, source) for source, target...  15 us
    ppermute x8, starting transfers between devices, exchange(): lax.ppermute(value, 'row', [(rank, rank ^ step) for rank in range(ranks)])  8.88 us
    ppermute x4, starting transfers between devices, onward(): return lax.ppermute(value, ('depth', 'row'), pairs)  5.86 us
    ppermute x8, waiting for transfers between devices, exchange(): lax.ppermute(value, 'row', [(rank, rank ^ step) for rank in range(ranks)])  5.16 us
    ppermute x1, starting transfers between devices, local(): lax.ppermute(outer, 'row', between + [(target, source) for source, target...  3.34 us
    ppermute x1, starting transfers between devices, local(): lax.ppermute(scalars, 'depth', [(i, (i - 1) % groups) for i in range(grou...  3.32 us
  transfers between devices with their start and end apart: 15, of which 5 were waited for; matrix products, arithmetic and copies ran while one was open for 0% of the time, Pallas kernels for 23%

profile of v2, /device:TPU:1, one launch (start us, length us, event | category | flops | bytes accessed | tf_op | source)
XLA Modules:
  0.0 73.5 jit_solution(15336918167951522972)
XLA Ops:
  0.6 1.0 %dynamic-slice_bitcast_fusion = f32[64,512]{1,0:T(8,128)S(1)} fusion(f32[1,128,512]{2,1,0:T(8,128)} %param.15, s32[]{:T(128)S(6)} %select_n.3), kind=kLoop, calls=%fused_computation | loop fusion | bytes 262148 | tf_op jit(solution)/shard_map/dynamic_slice | solution.py:548
  1.7 2.1 %collective-permute-start = (f32[64,512]{1,0:T(8,128)S(1)}, f32[64,512]{1,0:T(8,128)S(1)}, u32[]{:S(2)}, u32[]{:S(2)}) collective-permute-start(f32[64,512]{1,0:T(8,128)S(1)} %dynamic-slice_bitcast_fusion), channel_id=1, source_target_pairs={{0,2},{1,3},{2,0},{3,1},{4,6},{5,7},{6,4},{7,5},{8,10},{9,11},{10,... | collective-permute-start | bytes 393224 | tf_op jit(solution)/shard_map/ppermute | solution.py:527
  3.8 2.6 %rows_to_columns.1 = (f32[2,128,256]{2,1,0:T(8,128)S(1)}, f32[2,128,256]{2,1,0:T(8,128)S(1)}, f32[2,128,256]{2,1,0:T(8,128)S(1)}, f32[2,128,256]{2,1,0:T(8,128)S(1)}) custom-call(f32[2048,128]{1,0:T(8,128)} %bitcast.21, bf16[2,2,2,256,256]{4,3,2,1,0:T(8,128)(2,1)} %constant.25.clone.refs_1_.refs_5_), custom_call_target="tpu_custom_call" | custom-call | flops 1 | bytes 1 | tf_op jit(solution)/shard_map/rows_to_columns/pallas_call | solution.py:500
  7.0 1.1 %collective-permute-start.3 = (f32[2,128,256]{2,1,0:T(8,128)S(1)}, f32[2,128,256]{2,1,0:T(8,128)S(1)}, u32[]{:S(2)}, u32[]{:S(2)}) collective-permute-start(f32[2,128,256]{2,1,0:T(8,128)S(1)} %get-tuple-element.55), channel_id=1, source_target_pairs={{0,2},{1,3},{2,0},{3,1},{4,6},{5,7},{6,4},{7,5},{8,10},{9,11},{10,... | collective-permute-start | bytes 786440 | tf_op jit(solution)/shard_map/ppermute | solution.py:527
  8.1 1.7 %collective-permute-start.4 = (f32[2,128,256]{2,1,0:T(8,128)S(1)}, f32[2,128,256]{2,1,0:T(8,128)S(1)}, u32[]{:S(2)}, u32[]{:S(2)}) collective-permute-start(f32[2,128,256]{2,1,0:T(8,128)S(1)} %get-tuple-element.56), channel_id=1, source_target_pairs={{0,3},{1,2},{2,1},{3,0},{4,7},{5,6},{6,5},{7,4},{8,11},{9,10},{10,... | collective-permute-start | bytes 786440 | tf_op jit(solution)/shard_map/ppermute | solution.py:527
  10.0 1.4 %collective-permute-start.5 = (f32[64,512]{1,0:T(8,128)S(1)}, f32[64,512]{1,0:T(8,128)S(1)}, u32[]{:S(2)}, u32[]{:S(2)}) collective-permute-start(f32[64,512]{1,0:T(8,128)S(1)} %collective-permute-done.refs_0_), channel_id=1, source_target_pairs={{0,16},{16,0},{1,17},{17,1},{2,18},{18,2},{3,19},{19,3},{4,20},{20... | collective-permute-start | bytes 393224 | tf_op jit(solution)/shard_map/ppermute | solution.py:576
  13.4 3.3 %collective-permute-start.1 = (f32[8,128]{1,0:T(8,128)S(1)}, f32[8,128]{1,0:T(8,128)S(1)}, u32[]{:S(2)}, u32[]{:S(2)}) collective-permute-start(f32[8,128]{1,0:T(8,128)S(1)} %broadcast_in_dim.12.scalars.refs_5_), channel_id=1, source_target_pairs={{0,12},{4,0},{8,4},{12,8},{1,13},{5,1},{9,5},{13,9},{2,14},{6,2},{... | collective-permute-start | bytes 12296 | tf_op jit(solution)/shard_map/ppermute | solution.py:582
  16.8 1.6 %phase_first.1.refs_4_ = f32[2,2,256,256]{3,2,1,0:T(8,128)S(1)} custom-call(f32[8,128]{1,0:T(8,128)S(1)} %broadcast_in_dim.12.scalars.refs_5_), custom_call_target="tpu_custom_call" | custom-call | flops 1 | bytes 1 | tf_op jit(solution)/shard_map/phase_first/pallas_call | solution.py:500
  18.3 5.4 %injection.1.refs_3_ = f32[2,2,128,512]{3,2,1,0:T(8,128)S(1)} custom-call(s32[1,2]{1,0:T(1,128)} %bitcast.24, f32[1,2]{1,0:T(1,128)} %bitcast.25, f32[2,4096]{1,0:T(2,128)} %bitcast.22, s32[2,4096]{1,0:T(2,128)} %bitcast.23), custom_call_target="tpu_custom_call" | custom-call | flops 1 | bytes 1 | tf_op jit(solution)/shard_map/injection/pallas_call | solution.py:500
  23.8 2.5 %columns_first.1 = (f32[2,2,128,256]{3,2,1,0:T(8,128)S(1)}, f32[2,2,128,256]{3,2,1,0:T(8,128)S(1)}) custom-call(f32[2,128,256]{2,1,0:T(8,128)S(1)} %get-tuple-element.54.refs_0_, f32[2,128,256]{2,1,0:T(8,128)S(1)} %collective-permute-done.2.refs_1_, f32[2,128,256]{2,1,0:T(8,128)S(1)} %collective-permute-done.3.refs_2_, ...), custom_call_target="tpu_custom_call" | custom-call | flops 1 | bytes 1 | tf_op jit(solution)/shard_map/columns_first/pallas_call | solution.py:500
  26.3 1.1 %collective-permute-start.6 = (f32[2,2,128,256]{3,2,1,0:T(8,128)S(1)}, f32[2,2,128,256]{3,2,1,0:T(8,128)S(1)}, u32[]{:S(2)}, u32[]{:S(2)}) collective-permute-start(f32[2,2,128,256]{3,2,1,0:T(8,128)S(1)} %get-tuple-element.63), channel_id=1, source_target_pairs={{0,1},{1,0},{2,3},{3,2},{4,5},{5,4},{6,7},{7,6},{8,9},{9,8},{10,11... | collective-permute-start | bytes 1572872 | tf_op jit(solution)/shard_map/ppermute | solution.py:527
  27.4 1.6 %phase_second.1 = (f32[2,2,256,256]{3,2,1,0:T(8,128)S(1)}, f32[8,256]{1,0:T(8,128)S(1)}) custom-call(f32[8,128]{1,0:T(8,128)S(1)} %broadcast_in_dim.12.scalars.refs_5_, f32[8,128]{1,0:T(8,128)S(1)} %collective-permute-done.1.scalars_next), custom_call_target="tpu_custom_call" | custom-call | flops 1 | bytes 1 | tf_op jit(solution)/shard_map/phase_second/pallas_call | solution.py:500
  29.0 1.1 %lens.1.refs_2_ = f32[2,2,128,512]{3,2,1,0:T(8,128)S(1)} custom-call(f32[8,128]{1,0:T(8,128)S(1)} %broadcast_in_dim.12.scalars.refs_5_, f32[128,512]{1,0:T(8,128)S(1)} %bitcast.18, f32[64,512]{1,0:T(8,128)S(1)} %collective-permute-done.refs_0_, f32[64,512]{1,0:T(8,128)S(1)} %collective-permute-done.5.refs_1_), custom_call_target="tpu_custom_call" | custom-call | flops 1 | bytes 1 | tf_op jit(solution)/shard_map/lens/pallas_call | solution.py:500
  30.1 2.3 %columns_to_columns.1 = (f32[2,128,512]{2,1,0:T(8,128)S(1)}, f32[2,128,512]{2,1,0:T(8,128)S(1)}, f32[2,2,128,256]{3,2,1,0:T(8,128)S(1)}, f32[2,2,128,256]{3,2,1,0:T(8,128)S(1)}) custom-call(f32[2,2,128,256]{3,2,1,0:T(8,128)S(1)} %get-tuple-element.62.refs_0_, f32[2,2,128,256]{3,2,1,0:T(8,128)S(1)} %collective-permute-done.6.refs_1_, ...), custom_call_target="tpu_custom_call" | custom-call | flops 1 | bytes 1 | tf_op jit(solution)/shard_map/columns_to_columns/pallas_call | solution.py:500
  32.5 1.3 %collective-permute-start.12 = (f32[2,128,512]{2,1,0:T(8,128)S(1)}, f32[2,128,512]{2,1,0:T(8,128)S(1)}, u32[]{:S(2)}, u32[]{:S(2)}) collective-permute-start(f32[2,128,512]{2,1,0:T(8,128)S(1)} %get-tuple-element.80), channel_id=1, source_target_pairs={{0,2},{1,3},{2,0},{3,1},{4,6},{5,7},{6,4},{7,5},{8,10},{9,11},{10,... | collective-permute-start | bytes 1572872 | tf_op jit(solution)/shard_map/ppermute | solution.py:527
  34.4 2.4 %columns_second.1 = (f32[2,152,256]{2,1,0:T(8,128)S(1)}, f32[2,144,256]{2,1,0:T(8,128)S(1)}, f32[2,144,256]{2,1,0:T(8,128)S(1)}, f32[2,144,256]{2,1,0:T(8,128)S(1)}) custom-call(f32[2,2,128,256]{3,2,1,0:T(8,128)S(1)} %get-tuple-element.71.refs_0_, f32[2,2,128,256]{3,2,1,0:T(8,128)S(1)} %collective-permute-done.7.refs_1_, ...), custom_call_target="tpu_custom_call" | custom-call | flops 1 | bytes 1 | tf_op jit(solution)/shard_map/columns_second/pallas_call | solution.py:500
  36.8 1.3 %collective-permute-start.9 = (f32[2,144,256]{2,1,0:T(8,128)S(1)}, f32[2,144,256]{2,1,0:T(8,128)S(1)}, u32[]{:S(2)}, u32[]{:S(2)}) collective-permute-start(f32[2,144,256]{2,1,0:T(8,128)S(1)} %get-tuple-element.76), channel_id=1, source_target_pairs={{0,5},{1,4},{2,7},{3,6},{4,9},{5,8},{6,11},{7,10},{8,13},{9,12},{1... | collective-permute-start | bytes 884744 | tf_op jit(solution)/shard_map/ppermute | solution.py:535
  38.2 4.0 %collective-permute-start.10 = (f32[2,144,256]{2,1,0:T(8,128)S(1)}, f32[2,144,256]{2,1,0:T(8,128)S(1)}, u32[]{:S(2)}, u32[]{:S(2)}) collective-permute-start(f32[2,144,256]{2,1,0:T(8,128)S(1)} %get-tuple-element.77), channel_id=1, source_target_pairs={{0,6},{1,7},{2,4},{3,5},{4,10},{5,11},{6,8},{7,9},{8,14},{9,15},{1... | collective-permute-start | bytes 884744 | tf_op jit(solution)/shard_map/ppermute | solution.py:535
  42.6 3.0 %collective-permute-done.12.other = f32[2,128,512]{2,1,0:T(8,128)S(1)} collective-permute-done((f32[2,128,512]{2,1,0:T(8,128)S(1)}, f32[2,128,512]{2,1,0:T(8,128)S(1)}, u32[]{:S(2)}, u32[]{:S(2)}) %collective-permute-start.12) | collective-permute-done | bytes 524320 | tf_op jit(solution)/shard_map/ppermute | solution.py:527
  45.6 1.7 %image_first.1 = (f32[16,128,512]{2,1,0:T(8,128)S(1)}, f32[5,8,512]{2,1,0:T(8,128)S(1)}, f32[5,8,512]{2,1,0:T(8,128)S(1)}) custom-call(f32[2,128,512]{2,1,0:T(8,128)S(1)} %get-tuple-element.79.own, f32[2,128,512]{2,1,0:T(8,128)S(1)} %collective-permute-done.12.other, f32[128,512]{1,0:T(8,128)S(1)} %bitcast.19), custom_call_target="tpu_custom_call" | custom-call | flops 1 | bytes 1 | tf_op jit(solution)/shard_map/image_first/pallas_call | solution.py:500
  47.4 1.3 %collective-permute-start.13 = (f32[5,8,512]{2,1,0:T(8,128)S(1)}, f32[5,8,512]{2,1,0:T(8,128)S(1)}, u32[]{:S(2)}, u32[]{:S(2)}) collective-permute-start(f32[5,8,512]{2,1,0:T(8,128)S(1)} %get-tuple-element.81), channel_id=1, source_target_pairs={{0,1},{1,0},{2,3},{3,2},{4,5},{5,4},{6,7},{7,6},{8,9},{9,8},{10,11... | collective-permute-start | bytes 245768 | tf_op jit(solution)/shard_map/ppermute | solution.py:527
  49.6 3.3 %collective-permute-start.14 = (f32[5,8,512]{2,1,0:T(8,128)S(1)}, f32[5,8,512]{2,1,0:T(8,128)S(1)}, u32[]{:S(2)}, u32[]{:S(2)}) collective-permute-start(f32[5,8,512]{2,1,0:T(8,128)S(1)} %get-tuple-element.82), channel_id=1, source_target_pairs={{1,2},{2,1},{5,6},{6,5},{9,10},{10,9},{13,14},{14,13},{17,18},{18,... | collective-permute-start | bytes 245768 | tf_op jit(solution)/shard_map/ppermute | solution.py:658
  53.0 15.0 %collective-permute-done.14.outer.refs_7_ = f32[5,8,512]{2,1,0:T(8,128)S(1)} collective-permute-done((f32[5,8,512]{2,1,0:T(8,128)S(1)}, f32[5,8,512]{2,1,0:T(8,128)S(1)}, u32[]{:S(2)}, u32[]{:S(2)}) %collective-permute-start.14) | collective-permute-done | bytes 81952 | tf_op jit(solution)/shard_map/ppermute | solution.py:658
  68.3 5.0 %last_rows_and_image.1 = (f32[2048,128]{1,0:T(8,128)}, f32[16,128,512]{2,1,0:T(8,128)}) custom-call(f32[2,152,256]{2,1,0:T(8,128)S(1)} %collective-permute-done.8.refs_0_, f32[2,144,256]{2,1,0:T(8,128)S(1)} %collective-permute-done.9.refs_1_, f32[2,144,256]{2,1,0:T(8,128)S(1)} %collective-permute-done.10.refs_2_, ...), custom_call_target="tpu_custom_call" | custom-call | flops 1 | bytes 1 | tf_op jit(solution)/shard_map/last_rows_and_image/pallas_call | solution.py:500
  (28 shorter events, 3.3 us)
Async XLA Ops:
  0.6 23.2 %copy-start.2 = (bf16[2,2,512,256]{3,2,1,0:T(8,128)(2,1)S(1)}, bf16[2,2,512,256]{3,2,1,0:T(8,128)(2,1)}, u32[]{:S(2)}) copy-start(bf16[2,2,512,256]{3,2,1,0:T(8,128)(2,1)} %constant.23.clone.refs_5_.refs_3_) | copy-start | bytes 3145732
  1.7 5.3 %collective-permute-start = (f32[64,512]{1,0:T(8,128)S(1)}, f32[64,512]{1,0:T(8,128)S(1)}, u32[]{:S(2)}, u32[]{:S(2)}) collective-permute-start(f32[64,512]{1,0:T(8,128)S(1)} %dynamic-slice_bitcast_fusion), channel_id=1, source_target_pairs={{0,2},{1,3},{2,0},{3,1},{4,6},{5,7},{6,4},{7,5},{8,10},{9,11},{10,... | collective-permute-start | bytes 393224 | tf_op jit(solution)/shard_map/ppermute | solution.py:527
  3.8 25.2 %copy-start.3 = (f32[1,128,512]{2,1,0:T(8,128)S(1)}, f32[1,128,512]{2,1,0:T(8,128)}, u32[]{:S(2)}) copy-start(f32[1,128,512]{2,1,0:T(8,128)} %param.15) | copy-start | bytes 786436
  6.4 23.7 %copy-start = (bf16[2,2,2,256,256]{4,3,2,1,0:T(8,128)(2,1)S(1)}, bf16[2,2,2,256,256]{4,3,2,1,0:T(8,128)(2,1)}, u32[]{:S(2)}) copy-start(bf16[2,2,2,256,256]{4,3,2,1,0:T(8,128)(2,1)} %constant.26.clone.refs_4_.refs_8_) | copy-start | bytes 3145732
  6.4 23.7 %copy-start.1 = (bf16[2,2,2,256,256]{4,3,2,1,0:T(8,128)(2,1)S(1)}, bf16[2,2,2,256,256]{4,3,2,1,0:T(8,128)(2,1)}, u32[]{:S(2)}) copy-start(bf16[2,2,2,256,256]{4,3,2,1,0:T(8,128)(2,1)} %constant.25.clone.refs_1_.refs_5_) | copy-start | bytes 3145732
  7.0 16.8 %collective-permute-start.3 = (f32[2,128,256]{2,1,0:T(8,128)S(1)}, f32[2,128,256]{2,1,0:T(8,128)S(1)}, u32[]{:S(2)}, u32[]{:S(2)}) collective-permute-start(f32[2,128,256]{2,1,0:T(8,128)S(1)} %get-tuple-element.55), channel_id=1, source_target_pairs={{0,2},{1,3},{2,0},{3,1},{4,6},{5,7},{6,4},{7,5},{8,10},{9,11},{10,... | collective-permute-start | bytes 786440 | tf_op jit(solution)/shard_map/ppermute | solution.py:527
  8.1 15.7 %collective-permute-start.4 = (f32[2,128,256]{2,1,0:T(8,128)S(1)}, f32[2,128,256]{2,1,0:T(8,128)S(1)}, u32[]{:S(2)}, u32[]{:S(2)}) collective-permute-start(f32[2,128,256]{2,1,0:T(8,128)S(1)} %get-tuple-element.56), channel_id=1, source_target_pairs={{0,3},{1,2},{2,1},{3,0},{4,7},{5,6},{6,5},{7,4},{8,11},{9,10},{10,... | collective-permute-start | bytes 786440 | tf_op jit(solution)/shard_map/ppermute | solution.py:527
  9.8 14.0 %collective-permute-start.2 = (f32[2,128,256]{2,1,0:T(8,128)S(1)}, f32[2,128,256]{2,1,0:T(8,128)S(1)}, u32[]{:S(2)}, u32[]{:S(2)}) collective-permute-start(f32[2,128,256]{2,1,0:T(8,128)S(1)} %get-tuple-element.49), channel_id=1, source_target_pairs={{0,1},{1,0},{2,3},{3,2},{4,5},{5,4},{6,7},{7,6},{8,9},{9,8},{10,11... | collective-permute-start | bytes 786440 | tf_op jit(solution)/shard_map/ppermute | solution.py:527
  10.0 13.8 %collective-permute-start.5 = (f32[64,512]{1,0:T(8,128)S(1)}, f32[64,512]{1,0:T(8,128)S(1)}, u32[]{:S(2)}, u32[]{:S(2)}) collective-permute-start(f32[64,512]{1,0:T(8,128)S(1)} %collective-permute-done.refs_0_), channel_id=1, source_target_pairs={{0,16},{16,0},{1,17},{17,1},{2,18},{18,2},{3,19},{19,3},{4,20},{20... | collective-permute-start | bytes 393224 | tf_op jit(solution)/shard_map/ppermute | solution.py:576
  13.4 4.9 %collective-permute-start.1 = (f32[8,128]{1,0:T(8,128)S(1)}, f32[8,128]{1,0:T(8,128)S(1)}, u32[]{:S(2)}, u32[]{:S(2)}) collective-permute-start(f32[8,128]{1,0:T(8,128)S(1)} %broadcast_in_dim.12.scalars.refs_5_), channel_id=1, source_target_pairs={{0,12},{4,0},{8,4},{12,8},{1,13},{5,1},{9,5},{13,9},{2,14},{6,2},{... | collective-permute-start | bytes 12296 | tf_op jit(solution)/shard_map/ppermute | solution.py:582
  26.3 3.8 %collective-permute-start.6 = (f32[2,2,128,256]{3,2,1,0:T(8,128)S(1)}, f32[2,2,128,256]{3,2,1,0:T(8,128)S(1)}, u32[]{:S(2)}, u32[]{:S(2)}) collective-permute-start(f32[2,2,128,256]{3,2,1,0:T(8,128)S(1)} %get-tuple-element.63), channel_id=1, source_target_pairs={{0,1},{1,0},{2,3},{3,2},{4,5},{5,4},{6,7},{7,6},{8,9},{9,8},{10,11... | collective-permute-start | bytes 1572872 | tf_op jit(solution)/shard_map/ppermute | solution.py:527
  32.4 2.0 %collective-permute-start.7 = (f32[2,2,128,256]{3,2,1,0:T(8,128)S(1)}, f32[2,2,128,256]{3,2,1,0:T(8,128)S(1)}, u32[]{:S(2)}, u32[]{:S(2)}) collective-permute-start(f32[2,2,128,256]{3,2,1,0:T(8,128)S(1)} %get-tuple-element.72), channel_id=1, source_target_pairs={{0,1},{1,0},{2,3},{3,2},{4,5},{5,4},{6,7},{7,6},{8,9},{9,8},{10,11... | collective-permute-start | bytes 1572872 | tf_op jit(solution)/shard_map/ppermute | solution.py:527
  32.5 13.1 %collective-permute-start.12 = (f32[2,128,512]{2,1,0:T(8,128)S(1)}, f32[2,128,512]{2,1,0:T(8,128)S(1)}, u32[]{:S(2)}, u32[]{:S(2)}) collective-permute-start(f32[2,128,512]{2,1,0:T(8,128)S(1)} %get-tuple-element.80), channel_id=1, source_target_pairs={{0,2},{1,3},{2,0},{3,1},{4,6},{5,7},{6,4},{7,5},{8,10},{9,11},{10,... | collective-permute-start | bytes 1572872 | tf_op jit(solution)/shard_map/ppermute | solution.py:527
  36.8 31.6 %collective-permute-start.8 = (f32[2,152,256]{2,1,0:T(8,128)S(1)}, f32[2,152,256]{2,1,0:T(8,128)S(1)}, u32[]{:S(2)}, u32[]{:S(2)}) collective-permute-start(f32[2,152,256]{2,1,0:T(8,128)S(1)} %get-tuple-element.75), channel_id=1, source_target_pairs={{0,4},{1,5},{2,6},{3,7},{4,8},{5,9},{6,10},{7,11},{8,12},{9,13},{1... | collective-permute-start | bytes 933896 | tf_op jit(solution)/shard_map/ppermute | solution.py:535
  36.8 31.5 %collective-permute-start.9 = (f32[2,144,256]{2,1,0:T(8,128)S(1)}, f32[2,144,256]{2,1,0:T(8,128)S(1)}, u32[]{:S(2)}, u32[]{:S(2)}) collective-permute-start(f32[2,144,256]{2,1,0:T(8,128)S(1)} %get-tuple-element.76), channel_id=1, source_target_pairs={{0,5},{1,4},{2,7},{3,6},{4,9},{5,8},{6,11},{7,10},{8,13},{9,12},{1... | collective-permute-start | bytes 884744 | tf_op jit(solution)/shard_map/ppermute | solution.py:535
  38.2 30.1 %collective-permute-start.10 = (f32[2,144,256]{2,1,0:T(8,128)S(1)}, f32[2,144,256]{2,1,0:T(8,128)S(1)}, u32[]{:S(2)}, u32[]{:S(2)}) collective-permute-start(f32[2,144,256]{2,1,0:T(8,128)S(1)} %get-tuple-element.77), channel_id=1, source_target_pairs={{0,6},{1,7},{2,4},{3,5},{4,10},{5,11},{6,8},{7,9},{8,14},{9,15},{1... | collective-permute-start | bytes 884744 | tf_op jit(solution)/shard_map/ppermute | solution.py:535
  42.2 26.1 %collective-permute-start.11 = (f32[2,144,256]{2,1,0:T(8,128)S(1)}, f32[2,144,256]{2,1,0:T(8,128)S(1)}, u32[]{:S(2)}, u32[]{:S(2)}) collective-permute-start(f32[2,144,256]{2,1,0:T(8,128)S(1)} %get-tuple-element.78), channel_id=1, source_target_pairs={{0,7},{1,6},{2,5},{3,4},{4,11},{5,10},{6,9},{7,8},{8,15},{9,14},{1... | collective-permute-start | bytes 884744 | tf_op jit(solution)/shard_map/ppermute | solution.py:535
  47.4 2.3 %collective-permute-start.13 = (f32[5,8,512]{2,1,0:T(8,128)S(1)}, f32[5,8,512]{2,1,0:T(8,128)S(1)}, u32[]{:S(2)}, u32[]{:S(2)}) collective-permute-start(f32[5,8,512]{2,1,0:T(8,128)S(1)} %get-tuple-element.81), channel_id=1, source_target_pairs={{0,1},{1,0},{2,3},{3,2},{4,5},{5,4},{6,7},{7,6},{8,9},{9,8},{10,11... | collective-permute-start | bytes 245768 | tf_op jit(solution)/shard_map/ppermute | solution.py:527
  49.6 18.4 %collective-permute-start.14 = (f32[5,8,512]{2,1,0:T(8,128)S(1)}, f32[5,8,512]{2,1,0:T(8,128)S(1)}, u32[]{:S(2)}, u32[]{:S(2)}) collective-permute-start(f32[5,8,512]{2,1,0:T(8,128)S(1)} %get-tuple-element.82), channel_id=1, source_target_pairs={{1,2},{2,1},{5,6},{6,5},{9,10},{10,9},{13,14},{14,13},{17,18},{18,... | collective-permute-start | bytes 245768 | tf_op jit(solution)/shard_map/ppermute | solution.py:658

commit v3 on v2

--- a/solution.py
+++ b/solution.py
@@ -271,13 +271,30 @@
             results[step][:, part] = pair[part].reshape(2, lay.rows, lay.cols)
 
 
+def rows_of_pieces(lay, pieces, y_inverse):
+    index, _ = lay.place()
+    return rows_from(
+        lay,
+        [[piece[part, : lay.wide] for part in range(2)] for piece in pieces],
+        y_inverse,
+        index,
+    )
+
+
+def own_rows_kernel(lay, *refs):
+    pieces, y_inverse, own = refs[: lay.slices], refs[lay.slices], refs[-1]
+    for end, pair in enumerate(rows_of_pieces(lay, pieces, y_inverse)):
+        for part in range(2):
+            own[part, :, pl.ds(end * lay.half, lay.half)] = pair[part]
+
+
 def last_kernel(lay, *refs):
-    pieces = refs[: lay.ranks]
-    slow, scalars, inner, outer, y_inverse, previous = refs[lay.ranks : lay.ranks + 6]
-    image_top, image_bottom, wave_out, image = refs[lay.ranks + 6 : lay.ranks + 10]
+    near, own, pieces = refs[0], refs[1], refs[2 : 2 + lay.slices]
+    slow, scalars, inner, outer, y_inverse, previous = refs[2 + lay.slices : 8 + lay.slices]
+    image_top, image_bottom, wave_out, image = refs[8 + lay.slices : 12 + lay.slices]
     lens, fields, wave_buffer, image_buffer, wave_sent, image_sent = refs[-6:]
     index, side = lay.place()
-    freq = pieces[0][0, lay.wide : lay.wide + 1, 0:1]
+    freq = near[0, lay.wide : lay.wide + 1, 0:1]
     end = HALF + lay.rows
     before, behind = beside(inner, outer, 4)
     for start, values in ((0, before), (HALF, slow[...]), (end, behind)):
@@ -287,15 +304,13 @@
     for turn in range(2):
         field = side ^ turn
         sign = (1 - 2 * field).astype(F32)
-        ends = rows_from(
-            lay,
-            [
-                [piece[part, : lay.wide] for part in range(2)]
-                for piece in pieces[turn * lay.slices : (turn + 1) * lay.slices]
-            ],
-            y_inverse,
-            index,
-        )
+        if turn == 0:
+            ends = [
+                [own[part, :, pl.ds(end * lay.half, lay.half)] for part in range(2)]
+                for end in range(2)
+            ]
+        else:
+            ends = rows_of_pieces(lay, pieces, y_inverse)
         for end, (real, imag) in enumerate(ends):
             lanes = pl.ds(end * lay.half, lay.half)
             cosine, sine = lens[0, :, lanes], lens[1, :, lanes] * sign
@@ -646,6 +661,14 @@
     )
     arrived = [onward(value, step) for step, value in enumerate(sent)]
 
+    (own_rows,) = call(
+        functools.partial(own_rows_kernel, lay),
+        [(2, wide, lateral)],
+        [],
+        [*arrived[:slices], y_inverse],
+        name="own_rows",
+    )
+
     previous, inner, outer = call(
         functools.partial(image_kernel, lay),
         [(OFF, rows, lateral)] + [(5, HALF, lateral)] * 2,
@@ -654,6 +677,7 @@
         name="image_first",
     )
     inner = exchange(inner, 1)
+    outer, own_rows = after(outer, own_rows)
     between = [(rank, rank + 1) for rank in range(1, ranks - 1, 2)]
     outer = lax.ppermute(
         outer, "row", between + [(target, source) for source, target in between]
@@ -676,7 +700,7 @@
             pltpu.SemaphoreType.DMA(()),
             pltpu.SemaphoreType.DMA((OFF,)),
         ],
-        [*arrived, slow, scalars, inner, outer, y_inverse, previous, image_top, image_bottom],
+        [arrived[0], own_rows, *arrived[slices:], slow, scalars, inner, outer, y_inverse, previous, image_top, image_bottom],
         outside=True,
         name="last_rows_and_image",
     )

time: 73.9 us -> 74.1 us (level)
    ppermute x4, waiting for transfers between devices: 0.01 us -> 5.94 us  [onward(): return lax.ppermute(value, ('depth', 'row'), pairs)]
    ppermute x1, waiting for transfers between devices: 15 us -> 10.4 us  [local(): lax.ppermute(outer, 'row', between + [(target, source) for source, target...]
    ppermute x8, waiting for transfers between devices: 5.16 us -> 4.24 us  [exchange(): lax.ppermute(value, 'row', [(rank, rank ^ step) for rank in range(ranks)])]
    pallas_call x11 -> x12, Pallas kernels: 26.3 us -> 26.5 us  [call(): pl.pallas_call(kernel, out_shape=shapes, in_specs=[outer if i in far else...]
where the time goes in v3:
time: 74.1 us; the launch traced here: 73.7 us
  Pallas kernels  26.5 us (36%)
  starting transfers between devices  22.5 us (30%)
  waiting for transfers between devices  20.6 us (28%)
  between operations  2.97 us (4%)
  local copies, waits for them, and re-layouts  1.1 us (1%)
    pallas_call x12, Pallas kernels, call(): pl.pallas_call(kernel, out_shape=shapes, in_specs=[outer if i in far else...  26.5 us
    ppermute x1, waiting for transfers between devices, local(): lax.ppermute(outer, 'row', between + [(target, source) for source, target...  10.4 us
    ppermute x8, starting transfers between devices, exchange(): lax.ppermute(value, 'row', [(rank, rank ^ step) for rank in range(ranks)])  8.88 us
    ppermute x4, waiting for transfers between devices, onward(): return lax.ppermute(value, ('depth', 'row'), pairs)  5.94 us
    ppermute x4, starting transfers between devices, onward(): return lax.ppermute(value, ('depth', 'row'), pairs)  5.86 us
    ppermute x8, waiting for transfers between devices, exchange(): lax.ppermute(value, 'row', [(rank, rank ^ step) for rank in range(ranks)])  4.24 us
    ppermute x1, starting transfers between devices, local(): lax.ppermute(scalars, 'depth', [(i, (i - 1) % groups) for i in range(grou...  3.32 us
    ppermute x1, starting transfers between devices, local(): lax.ppermute(outer, 'row', between + [(target, source) for source, target...  3.05 us
  transfers between devices with their start and end apart: 15, of which 5 were waited for; matrix products, arithmetic and copies ran while one was open for 0% of the time, Pallas kernels for 23%

profile of v3, /device:TPU:1, one launch (start us, length us, event | category | flops | bytes accessed | tf_op | source)
XLA Modules:
  0.0 73.7 jit_solution(16685633234889513800)
XLA Ops:
  1.7 2.1 %collective-permute-start = (f32[64,512]{1,0:T(8,128)S(1)}, f32[64,512]{1,0:T(8,128)S(1)}, u32[]{:S(2)}, u32[]{:S(2)}) collective-permute-start(f32[64,512]{1,0:T(8,128)S(1)} %dynamic-slice_bitcast_fusion), channel_id=1, source_target_pairs={{0,2},{1,3},{2,0},{3,1},{4,6},{5,7},{6,4},{7,5},{8,10},{9,11},{10,... | collective-permute-start | bytes 393224 | tf_op jit(solution)/shard_map/ppermute | solution.py:542
  3.8 2.6 %rows_to_columns.1 = (f32[2,128,256]{2,1,0:T(8,128)S(1)}, f32[2,128,256]{2,1,0:T(8,128)S(1)}, f32[2,128,256]{2,1,0:T(8,128)S(1)}, f32[2,128,256]{2,1,0:T(8,128)S(1)}) custom-call(f32[2048,128]{1,0:T(8,128)} %bitcast.21, bf16[2,2,2,256,256]{4,3,2,1,0:T(8,128)(2,1)} %constant.25.clone.refs_1_.refs_5_), custom_call_target="tpu_custom_call" | custom-call | flops 1 | bytes 1 | tf_op jit(solution)/shard_map/rows_to_columns/pallas_call | solution.py:515
  7.0 1.1 %collective-permute-start.3 = (f32[2,128,256]{2,1,0:T(8,128)S(1)}, f32[2,128,256]{2,1,0:T(8,128)S(1)}, u32[]{:S(2)}, u32[]{:S(2)}) collective-permute-start(f32[2,128,256]{2,1,0:T(8,128)S(1)} %get-tuple-element.57), channel_id=1, source_target_pairs={{0,2},{1,3},{2,0},{3,1},{4,6},{5,7},{6,4},{7,5},{8,10},{9,11},{10,... | collective-permute-start | bytes 786440 | tf_op jit(solution)/shard_map/ppermute | solution.py:542
  8.1 1.7 %collective-permute-start.4 = (f32[2,128,256]{2,1,0:T(8,128)S(1)}, f32[2,128,256]{2,1,0:T(8,128)S(1)}, u32[]{:S(2)}, u32[]{:S(2)}) collective-permute-start(f32[2,128,256]{2,1,0:T(8,128)S(1)} %get-tuple-element.58), channel_id=1, source_target_pairs={{0,3},{1,2},{2,1},{3,0},{4,7},{5,6},{6,5},{7,4},{8,11},{9,10},{10,... | collective-permute-start | bytes 786440 | tf_op jit(solution)/shard_map/ppermute | solution.py:542
  10.0 1.4 %collective-permute-start.5 = (f32[64,512]{1,0:T(8,128)S(1)}, f32[64,512]{1,0:T(8,128)S(1)}, u32[]{:S(2)}, u32[]{:S(2)}) collective-permute-start(f32[64,512]{1,0:T(8,128)S(1)} %collective-permute-done.refs_0_), channel_id=1, source_target_pairs={{0,16},{16,0},{1,17},{17,1},{2,18},{18,2},{3,19},{19,3},{4,20},{20... | collective-permute-start | bytes 393224 | tf_op jit(solution)/shard_map/ppermute | solution.py:591
  13.4 3.3 %collective-permute-start.1 = (f32[8,128]{1,0:T(8,128)S(1)}, f32[8,128]{1,0:T(8,128)S(1)}, u32[]{:S(2)}, u32[]{:S(2)}) collective-permute-start(f32[8,128]{1,0:T(8,128)S(1)} %broadcast_in_dim.12.scalars.refs_5_), channel_id=1, source_target_pairs={{0,12},{4,0},{8,4},{12,8},{1,13},{5,1},{9,5},{13,9},{2,14},{6,2},{... | collective-permute-start | bytes 12296 | tf_op jit(solution)/shard_map/ppermute | solution.py:597
  16.8 1.6 %phase_first.1.refs_4_ = f32[2,2,256,256]{3,2,1,0:T(8,128)S(1)} custom-call(f32[8,128]{1,0:T(8,128)S(1)} %broadcast_in_dim.12.scalars.refs_5_), custom_call_target="tpu_custom_call" | custom-call | flops 1 | bytes 1 | tf_op jit(solution)/shard_map/phase_first/pallas_call | solution.py:515
  18.3 5.4 %injection.1.refs_3_ = f32[2,2,128,512]{3,2,1,0:T(8,128)S(1)} custom-call(s32[1,2]{1,0:T(1,128)} %bitcast.24, f32[1,2]{1,0:T(1,128)} %bitcast.25, f32[2,4096]{1,0:T(2,128)} %bitcast.22, s32[2,4096]{1,0:T(2,128)} %bitcast.23), custom_call_target="tpu_custom_call" | custom-call | flops 1 | bytes 1 | tf_op jit(solution)/shard_map/injection/pallas_call | solution.py:515
  23.8 2.5 %columns_first.1 = (f32[2,2,128,256]{3,2,1,0:T(8,128)S(1)}, f32[2,2,128,256]{3,2,1,0:T(8,128)S(1)}) custom-call(f32[2,128,256]{2,1,0:T(8,128)S(1)} %get-tuple-element.56.refs_0_, f32[2,128,256]{2,1,0:T(8,128)S(1)} %collective-permute-done.2.refs_1_, f32[2,128,256]{2,1,0:T(8,128)S(1)} %collective-permute-done.3.refs_2_, ...), custom_call_target="tpu_custom_call" | custom-call | flops 1 | bytes 1 | tf_op jit(solution)/shard_map/columns_first/pallas_call | solution.py:515
  26.3 1.1 %collective-permute-start.6 = (f32[2,2,128,256]{3,2,1,0:T(8,128)S(1)}, f32[2,2,128,256]{3,2,1,0:T(8,128)S(1)}, u32[]{:S(2)}, u32[]{:S(2)}) collective-permute-start(f32[2,2,128,256]{3,2,1,0:T(8,128)S(1)} %get-tuple-element.65), channel_id=1, source_target_pairs={{0,1},{1,0},{2,3},{3,2},{4,5},{5,4},{6,7},{7,6},{8,9},{9,8},{10,11... | collective-permute-start | bytes 1572872 | tf_op jit(solution)/shard_map/ppermute | solution.py:542
  27.4 1.6 %phase_second.1 = (f32[2,2,256,256]{3,2,1,0:T(8,128)S(1)}, f32[8,256]{1,0:T(8,128)S(1)}) custom-call(f32[8,128]{1,0:T(8,128)S(1)} %broadcast_in_dim.12.scalars.refs_5_, f32[8,128]{1,0:T(8,128)S(1)} %collective-permute-done.1.scalars_next), custom_call_target="tpu_custom_call" | custom-call | flops 1 | bytes 1 | tf_op jit(solution)/shard_map/phase_second/pallas_call | solution.py:515
  29.0 1.1 %lens.1.refs_2_ = f32[2,2,128,512]{3,2,1,0:T(8,128)S(1)} custom-call(f32[8,128]{1,0:T(8,128)S(1)} %broadcast_in_dim.12.scalars.refs_5_, f32[128,512]{1,0:T(8,128)S(1)} %bitcast.18, f32[64,512]{1,0:T(8,128)S(1)} %collective-permute-done.refs_0_, f32[64,512]{1,0:T(8,128)S(1)} %collective-permute-done.5.refs_1_), custom_call_target="tpu_custom_call" | custom-call | flops 1 | bytes 1 | tf_op jit(solution)/shard_map/lens/pallas_call | solution.py:515
  30.1 2.3 %columns_to_columns.1 = (f32[2,128,512]{2,1,0:T(8,128)S(1)}, f32[2,128,512]{2,1,0:T(8,128)S(1)}, f32[2,2,128,256]{3,2,1,0:T(8,128)S(1)}, f32[2,2,128,256]{3,2,1,0:T(8,128)S(1)}) custom-call(f32[2,2,128,256]{3,2,1,0:T(8,128)S(1)} %get-tuple-element.64.refs_0_, f32[2,2,128,256]{3,2,1,0:T(8,128)S(1)} %collective-permute-done.6.refs_1_, ...), custom_call_target="tpu_custom_call" | custom-call | flops 1 | bytes 1 | tf_op jit(solution)/shard_map/columns_to_columns/pallas_call | solution.py:515
  32.5 1.3 %collective-permute-start.9 = (f32[2,128,512]{2,1,0:T(8,128)S(1)}, f32[2,128,512]{2,1,0:T(8,128)S(1)}, u32[]{:S(2)}, u32[]{:S(2)}) collective-permute-start(f32[2,128,512]{2,1,0:T(8,128)S(1)} %get-tuple-element.79), channel_id=1, source_target_pairs={{0,2},{1,3},{2,0},{3,1},{4,6},{5,7},{6,4},{7,5},{8,10},{9,11},{10,... | collective-permute-start | bytes 1572872 | tf_op jit(solution)/shard_map/ppermute | solution.py:542
  34.4 2.4 %columns_second.1 = (f32[2,152,256]{2,1,0:T(8,128)S(1)}, f32[2,144,256]{2,1,0:T(8,128)S(1)}, f32[2,144,256]{2,1,0:T(8,128)S(1)}, f32[2,144,256]{2,1,0:T(8,128)S(1)}) custom-call(f32[2,2,128,256]{3,2,1,0:T(8,128)S(1)} %get-tuple-element.73.refs_0_, f32[2,2,128,256]{3,2,1,0:T(8,128)S(1)} %collective-permute-done.7.refs_1_, ...), custom_call_target="tpu_custom_call" | custom-call | flops 1 | bytes 1 | tf_op jit(solution)/shard_map/columns_second/pallas_call | solution.py:515
  36.8 1.3 %collective-permute-start.10 = (f32[2,144,256]{2,1,0:T(8,128)S(1)}, f32[2,144,256]{2,1,0:T(8,128)S(1)}, u32[]{:S(2)}, u32[]{:S(2)}) collective-permute-start(f32[2,144,256]{2,1,0:T(8,128)S(1)} %get-tuple-element.81), channel_id=1, source_target_pairs={{0,5},{1,4},{2,7},{3,6},{4,9},{5,8},{6,11},{7,10},{8,13},{9,12},{1... | collective-permute-start | bytes 884744 | tf_op jit(solution)/shard_map/ppermute | solution.py:550
  38.2 4.0 %collective-permute-start.11 = (f32[2,144,256]{2,1,0:T(8,128)S(1)}, f32[2,144,256]{2,1,0:T(8,128)S(1)}, u32[]{:S(2)}, u32[]{:S(2)}) collective-permute-start(f32[2,144,256]{2,1,0:T(8,128)S(1)} %get-tuple-element.83), channel_id=1, source_target_pairs={{0,6},{1,7},{2,4},{3,5},{4,10},{5,11},{6,8},{7,9},{8,14},{9,15},{1... | collective-permute-start | bytes 884744 | tf_op jit(solution)/shard_map/ppermute | solution.py:550
  42.6 3.0 %collective-permute-done.9.other = f32[2,128,512]{2,1,0:T(8,128)S(1)} collective-permute-done((f32[2,128,512]{2,1,0:T(8,128)S(1)}, f32[2,128,512]{2,1,0:T(8,128)S(1)}, u32[]{:S(2)}, u32[]{:S(2)}) %collective-permute-start.9) | collective-permute-done | bytes 524320 | tf_op jit(solution)/shard_map/ppermute | solution.py:542
  45.6 1.7 %image_first.1 = (f32[16,128,512]{2,1,0:T(8,128)S(1)}, f32[5,8,512]{2,1,0:T(8,128)S(1)}, f32[5,8,512]{2,1,0:T(8,128)S(1)}) custom-call(f32[2,128,512]{2,1,0:T(8,128)S(1)} %get-tuple-element.78.own, f32[2,128,512]{2,1,0:T(8,128)S(1)} %collective-permute-done.9.other, f32[128,512]{1,0:T(8,128)S(1)} %bitcast.19), custom_call_target="tpu_custom_call" | custom-call | flops 1 | bytes 1 | tf_op jit(solution)/shard_map/image_first/pallas_call | solution.py:515
  47.4 1.3 %collective-permute-start.13 = (f32[5,8,512]{2,1,0:T(8,128)S(1)}, f32[5,8,512]{2,1,0:T(8,128)S(1)}, u32[]{:S(2)}, u32[]{:S(2)}) collective-permute-start(f32[5,8,512]{2,1,0:T(8,128)S(1)} %get-tuple-element.85), channel_id=1, source_target_pairs={{0,1},{1,0},{2,3},{3,2},{4,5},{5,4},{6,7},{7,6},{8,9},{9,8},{10,11... | collective-permute-start | bytes 245768 | tf_op jit(solution)/shard_map/ppermute | solution.py:542
  48.7 5.9 %collective-permute-done.10.refs_1_ = f32[2,144,256]{2,1,0:T(8,128)S(1)} collective-permute-done((f32[2,144,256]{2,1,0:T(8,128)S(1)}, f32[2,144,256]{2,1,0:T(8,128)S(1)}, u32[]{:S(2)}, u32[]{:S(2)}) %collective-permute-start.10) | collective-permute-done | bytes 294944 | tf_op jit(solution)/shard_map/ppermute | solution.py:550
  55.3 3.1 %collective-permute-start.14 = (f32[5,8,512]{2,1,0:T(8,128)S(1)}, f32[5,8,512]{2,1,0:T(8,128)S(1)}, u32[]{:S(2)}, u32[]{:S(2)}) collective-permute-start(f32[5,8,512]{2,1,0:T(8,128)S(1)} %get-tuple-element.86), channel_id=1, source_target_pairs={{1,2},{2,1},{5,6},{6,5},{9,10},{10,9},{13,14},{14,13},{17,18},{18,... | collective-permute-start | bytes 245768 | tf_op jit(solution)/shard_map/ppermute | solution.py:682
  58.4 10.4 %collective-permute-done.14.outer.refs_7_ = f32[5,8,512]{2,1,0:T(8,128)S(1)} collective-permute-done((f32[5,8,512]{2,1,0:T(8,128)S(1)}, f32[5,8,512]{2,1,0:T(8,128)S(1)}, u32[]{:S(2)}, u32[]{:S(2)}) %collective-permute-start.14) | collective-permute-done | bytes 81952 | tf_op jit(solution)/shard_map/ppermute | solution.py:682
  69.1 4.5 %last_rows_and_image.1 = (f32[2048,128]{1,0:T(8,128)}, f32[16,128,512]{2,1,0:T(8,128)}) custom-call(f32[2,152,256]{2,1,0:T(8,128)S(1)} %collective-permute-done.8.refs_0_, f32[2,144,512]{2,1,0:T(8,128)S(1)} %own_rows.1.refs_1_, f32[2,144,256]{2,1,0:T(8,128)S(1)} %collective-permute-done.11.refs_2_, f32[2,144,256]{2,1,0:T(8,128)S(1)} %collective-permute-done.12.refs_3_, ...), custom_call_target="tpu_custom_call" | custom-call | flops 1 | bytes 1 | tf_op jit(solution)/shard_map/last_rows_and_image/pallas_call | solution.py:515
  (29 shorter events, 4.1 us)
Async XLA Ops:
  0.6 23.2 %copy-start.2 = (bf16[2,2,512,256]{3,2,1,0:T(8,128)(2,1)S(1)}, bf16[2,2,512,256]{3,2,1,0:T(8,128)(2,1)}, u32[]{:S(2)}) copy-start(bf16[2,2,512,256]{3,2,1,0:T(8,128)(2,1)} %constant.23.clone.refs_5_.refs_3_) | copy-start | bytes 3145732
  1.7 5.3 %collective-permute-start = (f32[64,512]{1,0:T(8,128)S(1)}, f32[64,512]{1,0:T(8,128)S(1)}, u32[]{:S(2)}, u32[]{:S(2)}) collective-permute-start(f32[64,512]{1,0:T(8,128)S(1)} %dynamic-slice_bitcast_fusion), channel_id=1, source_target_pairs={{0,2},{1,3},{2,0},{3,1},{4,6},{5,7},{6,4},{7,5},{8,10},{9,11},{10,... | collective-permute-start | bytes 393224 | tf_op jit(solution)/shard_map/ppermute | solution.py:542
  3.8 25.2 %copy-start.3 = (f32[1,128,512]{2,1,0:T(8,128)S(1)}, f32[1,128,512]{2,1,0:T(8,128)}, u32[]{:S(2)}) copy-start(f32[1,128,512]{2,1,0:T(8,128)} %param.15) | copy-start | bytes 786436
  6.4 23.7 %copy-start = (bf16[2,2,2,256,256]{4,3,2,1,0:T(8,128)(2,1)S(1)}, bf16[2,2,2,256,256]{4,3,2,1,0:T(8,128)(2,1)}, u32[]{:S(2)}) copy-start(bf16[2,2,2,256,256]{4,3,2,1,0:T(8,128)(2,1)} %constant.26.clone.refs_4_.refs_2_.refs_8_) | copy-start | bytes 3145732
  6.4 23.7 %copy-start.1 = (bf16[2,2,2,256,256]{4,3,2,1,0:T(8,128)(2,1)S(1)}, bf16[2,2,2,256,256]{4,3,2,1,0:T(8,128)(2,1)}, u32[]{:S(2)}) copy-start(bf16[2,2,2,256,256]{4,3,2,1,0:T(8,128)(2,1)} %constant.25.clone.refs_1_.refs_5_) | copy-start | bytes 3145732
  7.0 16.8 %collective-permute-start.3 = (f32[2,128,256]{2,1,0:T(8,128)S(1)}, f32[2,128,256]{2,1,0:T(8,128)S(1)}, u32[]{:S(2)}, u32[]{:S(2)}) collective-permute-start(f32[2,128,256]{2,1,0:T(8,128)S(1)} %get-tuple-element.57), channel_id=1, source_target_pairs={{0,2},{1,3},{2,0},{3,1},{4,6},{5,7},{6,4},{7,5},{8,10},{9,11},{10,... | collective-permute-start | bytes 786440 | tf_op jit(solution)/shard_map/ppermute | solution.py:542
  8.1 15.7 %collective-permute-start.4 = (f32[2,128,256]{2,1,0:T(8,128)S(1)}, f32[2,128,256]{2,1,0:T(8,128)S(1)}, u32[]{:S(2)}, u32[]{:S(2)}) collective-permute-start(f32[2,128,256]{2,1,0:T(8,128)S(1)} %get-tuple-element.58), channel_id=1, source_target_pairs={{0,3},{1,2},{2,1},{3,0},{4,7},{5,6},{6,5},{7,4},{8,11},{9,10},{10,... | collective-permute-start | bytes 786440 | tf_op jit(solution)/shard_map/ppermute | solution.py:542
  9.8 14.0 %collective-permute-start.2 = (f32[2,128,256]{2,1,0:T(8,128)S(1)}, f32[2,128,256]{2,1,0:T(8,128)S(1)}, u32[]{:S(2)}, u32[]{:S(2)}) collective-permute-start(f32[2,128,256]{2,1,0:T(8,128)S(1)} %get-tuple-element.51), channel_id=1, source_target_pairs={{0,1},{1,0},{2,3},{3,2},{4,5},{5,4},{6,7},{7,6},{8,9},{9,8},{10,11... | collective-permute-start | bytes 786440 | tf_op jit(solution)/shard_map/ppermute | solution.py:542
  10.0 13.8 %collective-permute-start.5 = (f32[64,512]{1,0:T(8,128)S(1)}, f32[64,512]{1,0:T(8,128)S(1)}, u32[]{:S(2)}, u32[]{:S(2)}) collective-permute-start(f32[64,512]{1,0:T(8,128)S(1)} %collective-permute-done.refs_0_), channel_id=1, source_target_pairs={{0,16},{16,0},{1,17},{17,1},{2,18},{18,2},{3,19},{19,3},{4,20},{20... | collective-permute-start | bytes 393224 | tf_op jit(solution)/shard_map/ppermute | solution.py:591
  13.4 4.9 %collective-permute-start.1 = (f32[8,128]{1,0:T(8,128)S(1)}, f32[8,128]{1,0:T(8,128)S(1)}, u32[]{:S(2)}, u32[]{:S(2)}) collective-permute-start(f32[8,128]{1,0:T(8,128)S(1)} %broadcast_in_dim.12.scalars.refs_5_), channel_id=1, source_target_pairs={{0,12},{4,0},{8,4},{12,8},{1,13},{5,1},{9,5},{13,9},{2,14},{6,2},{... | collective-permute-start | bytes 12296 | tf_op jit(solution)/shard_map/ppermute | solution.py:597
  26.3 3.8 %collective-permute-start.6 = (f32[2,2,128,256]{3,2,1,0:T(8,128)S(1)}, f32[2,2,128,256]{3,2,1,0:T(8,128)S(1)}, u32[]{:S(2)}, u32[]{:S(2)}) collective-permute-start(f32[2,2,128,256]{3,2,1,0:T(8,128)S(1)} %get-tuple-element.65), channel_id=1, source_target_pairs={{0,1},{1,0},{2,3},{3,2},{4,5},{5,4},{6,7},{7,6},{8,9},{9,8},{10,11... | collective-permute-start | bytes 1572872 | tf_op jit(solution)/shard_map/ppermute | solution.py:542
  32.4 2.0 %collective-permute-start.7 = (f32[2,2,128,256]{3,2,1,0:T(8,128)S(1)}, f32[2,2,128,256]{3,2,1,0:T(8,128)S(1)}, u32[]{:S(2)}, u32[]{:S(2)}) collective-permute-start(f32[2,2,128,256]{3,2,1,0:T(8,128)S(1)} %get-tuple-element.74), channel_id=1, source_target_pairs={{0,1},{1,0},{2,3},{3,2},{4,5},{5,4},{6,7},{7,6},{8,9},{9,8},{10,11... | collective-permute-start | bytes 1572872 | tf_op jit(solution)/shard_map/ppermute | solution.py:542
  32.5 13.1 %collective-permute-start.9 = (f32[2,128,512]{2,1,0:T(8,128)S(1)}, f32[2,128,512]{2,1,0:T(8,128)S(1)}, u32[]{:S(2)}, u32[]{:S(2)}) collective-permute-start(f32[2,128,512]{2,1,0:T(8,128)S(1)} %get-tuple-element.79), channel_id=1, source_target_pairs={{0,2},{1,3},{2,0},{3,1},{4,6},{5,7},{6,4},{7,5},{8,10},{9,11},{10,... | collective-permute-start | bytes 1572872 | tf_op jit(solution)/shard_map/ppermute | solution.py:542
  36.8 17.9 %collective-permute-start.8 = (f32[2,152,256]{2,1,0:T(8,128)S(1)}, f32[2,152,256]{2,1,0:T(8,128)S(1)}, u32[]{:S(2)}, u32[]{:S(2)}) collective-permute-start(f32[2,152,256]{2,1,0:T(8,128)S(1)} %get-tuple-element.77), channel_id=1, source_target_pairs={{0,4},{1,5},{2,6},{3,7},{4,8},{5,9},{6,10},{7,11},{8,12},{9,13},{1... | collective-permute-start | bytes 933896 | tf_op jit(solution)/shard_map/ppermute | solution.py:550
  36.8 17.8 %collective-permute-start.10 = (f32[2,144,256]{2,1,0:T(8,128)S(1)}, f32[2,144,256]{2,1,0:T(8,128)S(1)}, u32[]{:S(2)}, u32[]{:S(2)}) collective-permute-start(f32[2,144,256]{2,1,0:T(8,128)S(1)} %get-tuple-element.81), channel_id=1, source_target_pairs={{0,5},{1,4},{2,7},{3,6},{4,9},{5,8},{6,11},{7,10},{8,13},{9,12},{1... | collective-permute-start | bytes 884744 | tf_op jit(solution)/shard_map/ppermute | solution.py:550
  38.2 30.9 %collective-permute-start.11 = (f32[2,144,256]{2,1,0:T(8,128)S(1)}, f32[2,144,256]{2,1,0:T(8,128)S(1)}, u32[]{:S(2)}, u32[]{:S(2)}) collective-permute-start(f32[2,144,256]{2,1,0:T(8,128)S(1)} %get-tuple-element.83), channel_id=1, source_target_pairs={{0,6},{1,7},{2,4},{3,5},{4,10},{5,11},{6,8},{7,9},{8,14},{9,15},{1... | collective-permute-start | bytes 884744 | tf_op jit(solution)/shard_map/ppermute | solution.py:550
  42.2 26.9 %collective-permute-start.12 = (f32[2,144,256]{2,1,0:T(8,128)S(1)}, f32[2,144,256]{2,1,0:T(8,128)S(1)}, u32[]{:S(2)}, u32[]{:S(2)}) collective-permute-start(f32[2,144,256]{2,1,0:T(8,128)S(1)} %get-tuple-element.84), channel_id=1, source_target_pairs={{0,7},{1,6},{2,5},{3,4},{4,11},{5,10},{6,9},{7,8},{8,15},{9,14},{1... | collective-permute-start | bytes 884744 | tf_op jit(solution)/shard_map/ppermute | solution.py:550
  47.4 11.0 %collective-permute-start.13 = (f32[5,8,512]{2,1,0:T(8,128)S(1)}, f32[5,8,512]{2,1,0:T(8,128)S(1)}, u32[]{:S(2)}, u32[]{:S(2)}) collective-permute-start(f32[5,8,512]{2,1,0:T(8,128)S(1)} %get-tuple-element.85), channel_id=1, source_target_pairs={{0,1},{1,0},{2,3},{3,2},{4,5},{5,4},{6,7},{7,6},{8,9},{9,8},{10,11... | collective-permute-start | bytes 245768 | tf_op jit(solution)/shard_map/ppermute | solution.py:542
  55.3 13.5 %collective-permute-start.14 = (f32[5,8,512]{2,1,0:T(8,128)S(1)}, f32[5,8,512]{2,1,0:T(8,128)S(1)}, u32[]{:S(2)}, u32[]{:S(2)}) collective-permute-start(f32[5,8,512]{2,1,0:T(8,128)S(1)} %get-tuple-element.86), channel_id=1, source_target_pairs={{1,2},{2,1},{5,6},{6,5},{9,10},{10,9},{13,14},{14,13},{17,18},{18,... | collective-permute-start | bytes 245768 | tf_op jit(solution)/shard_map/ppermute | solution.py:682

commit v4 on v2

--- a/solution.py
+++ b/solution.py
@@ -301,15 +301,7 @@
             cosine, sine = lens[0, :, lanes], lens[1, :, lanes] * sign
             fields[field, 0, :, lanes] = real * cosine - imag * sine
             fields[field, 1, :, lanes] = real * sine + imag * cosine
-    for field in range(2):
-        for part in range(2):
-            for chunk in range(lay.chunks):
-                start = (part * lay.rows * 2 + field) * lay.chunks + chunk
-                wave_buffer[pl.ds(start, lay.rows, stride=2 * lay.chunks), :] = fields[
-                    field, part, HALF : HALF + lay.rows, pl.ds(chunk * LANES, LANES)
-                ]
-    copies = [pltpu.make_async_copy(wave_buffer, wave_out, wave_sent)]
-    copies[0].start()
+    copies = []
     stop = lay.rows - HALF
     for offset in range(OFF):
         value = correlation(fields, offset, lay.rows)
@@ -322,6 +314,16 @@
             )
         )
         copies[-1].start()
+        if offset == OFF // 2:
+            for field in range(2):
+                for part in range(2):
+                    for chunk in range(lay.chunks):
+                        start = (part * lay.rows * 2 + field) * lay.chunks + chunk
+                        wave_buffer[pl.ds(start, lay.rows, stride=2 * lay.chunks), :] = fields[
+                            field, part, HALF : HALF + lay.rows, pl.ds(chunk * LANES, LANES)
+                        ]
+            copies.append(pltpu.make_async_copy(wave_buffer, wave_out, wave_sent))
+            copies[-1].start()
     for copy in copies:
         copy.wait()
 

time: 73.9 us -> 73.9 us (level)
  no operation moved by 1% of the time
where the time goes in v4:
time: 73.9 us; the launch traced here: 73.5 us
  Pallas kernels  26.3 us (36%)
  starting transfers between devices  22.8 us (31%)
  waiting for transfers between devices  20.2 us (27%)
  between operations  2.97 us (4%)
  local copies, waits for them, and re-layouts  1.1 us (1%)
    pallas_call x11, Pallas kernels, call(): pl.pallas_call(kernel, out_shape=shapes, in_specs=[outer if i in far else...  26.3 us
    ppermute x1, waiting for transfers between devices, local(): lax.ppermute(outer, 'row', between + [(target, source) for source, target...  15 us
    ppermute x8, starting transfers between devices, exchange(): lax.ppermute(value, 'row', [(rank, rank ^ step) for rank in range(ranks)])  8.88 us
    ppermute x4, starting transfers between devices, onward(): return lax.ppermute(value, ('depth', 'row'), pairs)  5.86 us
    ppermute x8, waiting for transfers between devices, exchange(): lax.ppermute(value, 'row', [(rank, rank ^ step) for rank in range(ranks)])  5.16 us
    ppermute x1, starting transfers between devices, local(): lax.ppermute(outer, 'row', between + [(target, source) for source, target...  3.34 us
    ppermute x1, starting transfers between devices, local(): lax.ppermute(scalars, 'depth', [(i, (i - 1) % groups) for i in range(grou...  3.32 us
  transfers between devices with their start and end apart: 15, of which 5 were waited for; matrix products, arithmetic and copies ran while one was open for 0% of the time, Pallas kernels for 23%

profile of v4, /device:TPU:1, one launch (start us, length us, event | category | flops | bytes accessed | tf_op | source)
XLA Modules:
  0.0 73.5 jit_solution(9791856171897112670)
XLA Ops:
  0.6 1.0 %dynamic-slice_bitcast_fusion = f32[64,512]{1,0:T(8,128)S(1)} fusion(f32[1,128,512]{2,1,0:T(8,128)} %param.15, s32[]{:T(128)S(6)} %select_n.3), kind=kLoop, calls=%fused_computation | loop fusion | bytes 262148 | tf_op jit(solution)/shard_map/dynamic_slice | solution.py:550
  1.7 2.1 %collective-permute-start = (f32[64,512]{1,0:T(8,128)S(1)}, f32[64,512]{1,0:T(8,128)S(1)}, u32[]{:S(2)}, u32[]{:S(2)}) collective-permute-start(f32[64,512]{1,0:T(8,128)S(1)} %dynamic-slice_bitcast_fusion), channel_id=1, source_target_pairs={{0,2},{1,3},{2,0},{3,1},{4,6},{5,7},{6,4},{7,5},{8,10},{9,11},{10,... | collective-permute-start | bytes 393224 | tf_op jit(solution)/shard_map/ppermute | solution.py:529
  3.8 2.6 %rows_to_columns.1 = (f32[2,128,256]{2,1,0:T(8,128)S(1)}, f32[2,128,256]{2,1,0:T(8,128)S(1)}, f32[2,128,256]{2,1,0:T(8,128)S(1)}, f32[2,128,256]{2,1,0:T(8,128)S(1)}) custom-call(f32[2048,128]{1,0:T(8,128)} %bitcast.21, bf16[2,2,2,256,256]{4,3,2,1,0:T(8,128)(2,1)} %constant.25.clone.refs_1_.refs_5_), custom_call_target="tpu_custom_call" | custom-call | flops 1 | bytes 1 | tf_op jit(solution)/shard_map/rows_to_columns/pallas_call | solution.py:502
  7.0 1.1 %collective-permute-start.3 = (f32[2,128,256]{2,1,0:T(8,128)S(1)}, f32[2,128,256]{2,1,0:T(8,128)S(1)}, u32[]{:S(2)}, u32[]{:S(2)}) collective-permute-start(f32[2,128,256]{2,1,0:T(8,128)S(1)} %get-tuple-element.55), channel_id=1, source_target_pairs={{0,2},{1,3},{2,0},{3,1},{4,6},{5,7},{6,4},{7,5},{8,10},{9,11},{10,... | collective-permute-start | bytes 786440 | tf_op jit(solution)/shard_map/ppermute | solution.py:529
  8.1 1.7 %collective-permute-start.4 = (f32[2,128,256]{2,1,0:T(8,128)S(1)}, f32[2,128,256]{2,1,0:T(8,128)S(1)}, u32[]{:S(2)}, u32[]{:S(2)}) collective-permute-start(f32[2,128,256]{2,1,0:T(8,128)S(1)} %get-tuple-element.56), channel_id=1, source_target_pairs={{0,3},{1,2},{2,1},{3,0},{4,7},{5,6},{6,5},{7,4},{8,11},{9,10},{10,... | collective-permute-start | bytes 786440 | tf_op jit(solution)/shard_map/ppermute | solution.py:529
  10.0 1.4 %collective-permute-start.5 = (f32[64,512]{1,0:T(8,128)S(1)}, f32[64,512]{1,0:T(8,128)S(1)}, u32[]{:S(2)}, u32[]{:S(2)}) collective-permute-start(f32[64,512]{1,0:T(8,128)S(1)} %collective-permute-done.refs_0_), channel_id=1, source_target_pairs={{0,16},{16,0},{1,17},{17,1},{2,18},{18,2},{3,19},{19,3},{4,20},{20... | collective-permute-start | bytes 393224 | tf_op jit(solution)/shard_map/ppermute | solution.py:578
  13.4 3.3 %collective-permute-start.1 = (f32[8,128]{1,0:T(8,128)S(1)}, f32[8,128]{1,0:T(8,128)S(1)}, u32[]{:S(2)}, u32[]{:S(2)}) collective-permute-start(f32[8,128]{1,0:T(8,128)S(1)} %broadcast_in_dim.12.scalars.refs_5_), channel_id=1, source_target_pairs={{0,12},{4,0},{8,4},{12,8},{1,13},{5,1},{9,5},{13,9},{2,14},{6,2},{... | collective-permute-start | bytes 12296 | tf_op jit(solution)/shard_map/ppermute | solution.py:584
  16.8 1.6 %phase_first.1.refs_4_ = f32[2,2,256,256]{3,2,1,0:T(8,128)S(1)} custom-call(f32[8,128]{1,0:T(8,128)S(1)} %broadcast_in_dim.12.scalars.refs_5_), custom_call_target="tpu_custom_call" | custom-call | flops 1 | bytes 1 | tf_op jit(solution)/shard_map/phase_first/pallas_call | solution.py:502
  18.3 5.4 %injection.1.refs_3_ = f32[2,2,128,512]{3,2,1,0:T(8,128)S(1)} custom-call(s32[1,2]{1,0:T(1,128)} %bitcast.24, f32[1,2]{1,0:T(1,128)} %bitcast.25, f32[2,4096]{1,0:T(2,128)} %bitcast.22, s32[2,4096]{1,0:T(2,128)} %bitcast.23), custom_call_target="tpu_custom_call" | custom-call | flops 1 | bytes 1 | tf_op jit(solution)/shard_map/injection/pallas_call | solution.py:502
  23.8 2.5 %columns_first.1 = (f32[2,2,128,256]{3,2,1,0:T(8,128)S(1)}, f32[2,2,128,256]{3,2,1,0:T(8,128)S(1)}) custom-call(f32[2,128,256]{2,1,0:T(8,128)S(1)} %get-tuple-element.54.refs_0_, f32[2,128,256]{2,1,0:T(8,128)S(1)} %collective-permute-done.2.refs_1_, f32[2,128,256]{2,1,0:T(8,128)S(1)} %collective-permute-done.3.refs_2_, ...), custom_call_target="tpu_custom_call" | custom-call | flops 1 | bytes 1 | tf_op jit(solution)/shard_map/columns_first/pallas_call | solution.py:502
  26.3 1.1 %collective-permute-start.6 = (f32[2,2,128,256]{3,2,1,0:T(8,128)S(1)}, f32[2,2,128,256]{3,2,1,0:T(8,128)S(1)}, u32[]{:S(2)}, u32[]{:S(2)}) collective-permute-start(f32[2,2,128,256]{3,2,1,0:T(8,128)S(1)} %get-tuple-element.63), channel_id=1, source_target_pairs={{0,1},{1,0},{2,3},{3,2},{4,5},{5,4},{6,7},{7,6},{8,9},{9,8},{10,11... | collective-permute-start | bytes 1572872 | tf_op jit(solution)/shard_map/ppermute | solution.py:529
  27.4 1.6 %phase_second.1 = (f32[2,2,256,256]{3,2,1,0:T(8,128)S(1)}, f32[8,256]{1,0:T(8,128)S(1)}) custom-call(f32[8,128]{1,0:T(8,128)S(1)} %broadcast_in_dim.12.scalars.refs_5_, f32[8,128]{1,0:T(8,128)S(1)} %collective-permute-done.1.scalars_next), custom_call_target="tpu_custom_call" | custom-call | flops 1 | bytes 1 | tf_op jit(solution)/shard_map/phase_second/pallas_call | solution.py:502
  29.0 1.1 %lens.1.refs_2_ = f32[2,2,128,512]{3,2,1,0:T(8,128)S(1)} custom-call(f32[8,128]{1,0:T(8,128)S(1)} %broadcast_in_dim.12.scalars.refs_5_, f32[128,512]{1,0:T(8,128)S(1)} %bitcast.18, f32[64,512]{1,0:T(8,128)S(1)} %collective-permute-done.refs_0_, f32[64,512]{1,0:T(8,128)S(1)} %collective-permute-done.5.refs_1_), custom_call_target="tpu_custom_call" | custom-call | flops 1 | bytes 1 | tf_op jit(solution)/shard_map/lens/pallas_call | solution.py:502
  30.1 2.3 %columns_to_columns.1 = (f32[2,128,512]{2,1,0:T(8,128)S(1)}, f32[2,128,512]{2,1,0:T(8,128)S(1)}, f32[2,2,128,256]{3,2,1,0:T(8,128)S(1)}, f32[2,2,128,256]{3,2,1,0:T(8,128)S(1)}) custom-call(f32[2,2,128,256]{3,2,1,0:T(8,128)S(1)} %get-tuple-element.62.refs_0_, f32[2,2,128,256]{3,2,1,0:T(8,128)S(1)} %collective-permute-done.6.refs_1_, ...), custom_call_target="tpu_custom_call" | custom-call | flops 1 | bytes 1 | tf_op jit(solution)/shard_map/columns_to_columns/pallas_call | solution.py:502
  32.5 1.3 %collective-permute-start.12 = (f32[2,128,512]{2,1,0:T(8,128)S(1)}, f32[2,128,512]{2,1,0:T(8,128)S(1)}, u32[]{:S(2)}, u32[]{:S(2)}) collective-permute-start(f32[2,128,512]{2,1,0:T(8,128)S(1)} %get-tuple-element.80), channel_id=1, source_target_pairs={{0,2},{1,3},{2,0},{3,1},{4,6},{5,7},{6,4},{7,5},{8,10},{9,11},{10,... | collective-permute-start | bytes 1572872 | tf_op jit(solution)/shard_map/ppermute | solution.py:529
  34.4 2.4 %columns_second.1 = (f32[2,152,256]{2,1,0:T(8,128)S(1)}, f32[2,144,256]{2,1,0:T(8,128)S(1)}, f32[2,144,256]{2,1,0:T(8,128)S(1)}, f32[2,144,256]{2,1,0:T(8,128)S(1)}) custom-call(f32[2,2,128,256]{3,2,1,0:T(8,128)S(1)} %get-tuple-element.71.refs_0_, f32[2,2,128,256]{3,2,1,0:T(8,128)S(1)} %collective-permute-done.7.refs_1_, ...), custom_call_target="tpu_custom_call" | custom-call | flops 1 | bytes 1 | tf_op jit(solution)/shard_map/columns_second/pallas_call | solution.py:502
  36.8 1.3 %collective-permute-start.9 = (f32[2,144,256]{2,1,0:T(8,128)S(1)}, f32[2,144,256]{2,1,0:T(8,128)S(1)}, u32[]{:S(2)}, u32[]{:S(2)}) collective-permute-start(f32[2,144,256]{2,1,0:T(8,128)S(1)} %get-tuple-element.76), channel_id=1, source_target_pairs={{0,5},{1,4},{2,7},{3,6},{4,9},{5,8},{6,11},{7,10},{8,13},{9,12},{1... | collective-permute-start | bytes 884744 | tf_op jit(solution)/shard_map/ppermute | solution.py:537
  38.2 4.0 %collective-permute-start.10 = (f32[2,144,256]{2,1,0:T(8,128)S(1)}, f32[2,144,256]{2,1,0:T(8,128)S(1)}, u32[]{:S(2)}, u32[]{:S(2)}) collective-permute-start(f32[2,144,256]{2,1,0:T(8,128)S(1)} %get-tuple-element.77), channel_id=1, source_target_pairs={{0,6},{1,7},{2,4},{3,5},{4,10},{5,11},{6,8},{7,9},{8,14},{9,15},{1... | collective-permute-start | bytes 884744 | tf_op jit(solution)/shard_map/ppermute | solution.py:537
  42.6 3.0 %collective-permute-done.12.other = f32[2,128,512]{2,1,0:T(8,128)S(1)} collective-permute-done((f32[2,128,512]{2,1,0:T(8,128)S(1)}, f32[2,128,512]{2,1,0:T(8,128)S(1)}, u32[]{:S(2)}, u32[]{:S(2)}) %collective-permute-start.12) | collective-permute-done | bytes 524320 | tf_op jit(solution)/shard_map/ppermute | solution.py:529
  45.6 1.7 %image_first.1 = (f32[16,128,512]{2,1,0:T(8,128)S(1)}, f32[5,8,512]{2,1,0:T(8,128)S(1)}, f32[5,8,512]{2,1,0:T(8,128)S(1)}) custom-call(f32[2,128,512]{2,1,0:T(8,128)S(1)} %get-tuple-element.79.own, f32[2,128,512]{2,1,0:T(8,128)S(1)} %collective-permute-done.12.other, f32[128,512]{1,0:T(8,128)S(1)} %bitcast.19), custom_call_target="tpu_custom_call" | custom-call | flops 1 | bytes 1 | tf_op jit(solution)/shard_map/image_first/pallas_call | solution.py:502
  47.4 1.3 %collective-permute-start.13 = (f32[5,8,512]{2,1,0:T(8,128)S(1)}, f32[5,8,512]{2,1,0:T(8,128)S(1)}, u32[]{:S(2)}, u32[]{:S(2)}) collective-permute-start(f32[5,8,512]{2,1,0:T(8,128)S(1)} %get-tuple-element.81), channel_id=1, source_target_pairs={{0,1},{1,0},{2,3},{3,2},{4,5},{5,4},{6,7},{7,6},{8,9},{9,8},{10,11... | collective-permute-start | bytes 245768 | tf_op jit(solution)/shard_map/ppermute | solution.py:529
  49.6 3.3 %collective-permute-start.14 = (f32[5,8,512]{2,1,0:T(8,128)S(1)}, f32[5,8,512]{2,1,0:T(8,128)S(1)}, u32[]{:S(2)}, u32[]{:S(2)}) collective-permute-start(f32[5,8,512]{2,1,0:T(8,128)S(1)} %get-tuple-element.82), channel_id=1, source_target_pairs={{1,2},{2,1},{5,6},{6,5},{9,10},{10,9},{13,14},{14,13},{17,18},{18,... | collective-permute-start | bytes 245768 | tf_op jit(solution)/shard_map/ppermute | solution.py:660
  53.0 15.0 %collective-permute-done.14.outer.refs_7_ = f32[5,8,512]{2,1,0:T(8,128)S(1)} collective-permute-done((f32[5,8,512]{2,1,0:T(8,128)S(1)}, f32[5,8,512]{2,1,0:T(8,128)S(1)}, u32[]{:S(2)}, u32[]{:S(2)}) %collective-permute-start.14) | collective-permute-done | bytes 81952 | tf_op jit(solution)/shard_map/ppermute | solution.py:660
  68.3 5.0 %last_rows_and_image.1 = (f32[2048,128]{1,0:T(8,128)}, f32[16,128,512]{2,1,0:T(8,128)}) custom-call(f32[2,152,256]{2,1,0:T(8,128)S(1)} %collective-permute-done.8.refs_0_, f32[2,144,256]{2,1,0:T(8,128)S(1)} %collective-permute-done.9.refs_1_, f32[2,144,256]{2,1,0:T(8,128)S(1)} %collective-permute-done.10.refs_2_, ...), custom_call_target="tpu_custom_call" | custom-call | flops 1 | bytes 1 | tf_op jit(solution)/shard_map/last_rows_and_image/pallas_call | solution.py:502
  (28 shorter events, 3.3 us)
Async XLA Ops:
  0.6 23.2 %copy-start.2 = (bf16[2,2,512,256]{3,2,1,0:T(8,128)(2,1)S(1)}, bf16[2,2,512,256]{3,2,1,0:T(8,128)(2,1)}, u32[]{:S(2)}) copy-start(bf16[2,2,512,256]{3,2,1,0:T(8,128)(2,1)} %constant.23.clone.refs_5_.refs_3_) | copy-start | bytes 3145732
  1.7 5.3 %collective-permute-start = (f32[64,512]{1,0:T(8,128)S(1)}, f32[64,512]{1,0:T(8,128)S(1)}, u32[]{:S(2)}, u32[]{:S(2)}) collective-permute-start(f32[64,512]{1,0:T(8,128)S(1)} %dynamic-slice_bitcast_fusion), channel_id=1, source_target_pairs={{0,2},{1,3},{2,0},{3,1},{4,6},{5,7},{6,4},{7,5},{8,10},{9,11},{10,... | collective-permute-start | bytes 393224 | tf_op jit(solution)/shard_map/ppermute | solution.py:529
  3.8 25.2 %copy-start.3 = (f32[1,128,512]{2,1,0:T(8,128)S(1)}, f32[1,128,512]{2,1,0:T(8,128)}, u32[]{:S(2)}) copy-start(f32[1,128,512]{2,1,0:T(8,128)} %param.15) | copy-start | bytes 786436
  6.4 23.7 %copy-start = (bf16[2,2,2,256,256]{4,3,2,1,0:T(8,128)(2,1)S(1)}, bf16[2,2,2,256,256]{4,3,2,1,0:T(8,128)(2,1)}, u32[]{:S(2)}) copy-start(bf16[2,2,2,256,256]{4,3,2,1,0:T(8,128)(2,1)} %constant.26.clone.refs_4_.refs_8_) | copy-start | bytes 3145732
  6.4 23.7 %copy-start.1 = (bf16[2,2,2,256,256]{4,3,2,1,0:T(8,128)(2,1)S(1)}, bf16[2,2,2,256,256]{4,3,2,1,0:T(8,128)(2,1)}, u32[]{:S(2)}) copy-start(bf16[2,2,2,256,256]{4,3,2,1,0:T(8,128)(2,1)} %constant.25.clone.refs_1_.refs_5_) | copy-start | bytes 3145732
  7.0 16.8 %collective-permute-start.3 = (f32[2,128,256]{2,1,0:T(8,128)S(1)}, f32[2,128,256]{2,1,0:T(8,128)S(1)}, u32[]{:S(2)}, u32[]{:S(2)}) collective-permute-start(f32[2,128,256]{2,1,0:T(8,128)S(1)} %get-tuple-element.55), channel_id=1, source_target_pairs={{0,2},{1,3},{2,0},{3,1},{4,6},{5,7},{6,4},{7,5},{8,10},{9,11},{10,... | collective-permute-start | bytes 786440 | tf_op jit(solution)/shard_map/ppermute | solution.py:529
  8.1 15.7 %collective-permute-start.4 = (f32[2,128,256]{2,1,0:T(8,128)S(1)}, f32[2,128,256]{2,1,0:T(8,128)S(1)}, u32[]{:S(2)}, u32[]{:S(2)}) collective-permute-start(f32[2,128,256]{2,1,0:T(8,128)S(1)} %get-tuple-element.56), channel_id=1, source_target_pairs={{0,3},{1,2},{2,1},{3,0},{4,7},{5,6},{6,5},{7,4},{8,11},{9,10},{10,... | collective-permute-start | bytes 786440 | tf_op jit(solution)/shard_map/ppermute | solution.py:529
  9.8 14.0 %collective-permute-start.2 = (f32[2,128,256]{2,1,0:T(8,128)S(1)}, f32[2,128,256]{2,1,0:T(8,128)S(1)}, u32[]{:S(2)}, u32[]{:S(2)}) collective-permute-start(f32[2,128,256]{2,1,0:T(8,128)S(1)} %get-tuple-element.49), channel_id=1, source_target_pairs={{0,1},{1,0},{2,3},{3,2},{4,5},{5,4},{6,7},{7,6},{8,9},{9,8},{10,11... | collective-permute-start | bytes 786440 | tf_op jit(solution)/shard_map/ppermute | solution.py:529
  10.0 13.8 %collective-permute-start.5 = (f32[64,512]{1,0:T(8,128)S(1)}, f32[64,512]{1,0:T(8,128)S(1)}, u32[]{:S(2)}, u32[]{:S(2)}) collective-permute-start(f32[64,512]{1,0:T(8,128)S(1)} %collective-permute-done.refs_0_), channel_id=1, source_target_pairs={{0,16},{16,0},{1,17},{17,1},{2,18},{18,2},{3,19},{19,3},{4,20},{20... | collective-permute-start | bytes 393224 | tf_op jit(solution)/shard_map/ppermute | solution.py:578
  13.4 4.9 %collective-permute-start.1 = (f32[8,128]{1,0:T(8,128)S(1)}, f32[8,128]{1,0:T(8,128)S(1)}, u32[]{:S(2)}, u32[]{:S(2)}) collective-permute-start(f32[8,128]{1,0:T(8,128)S(1)} %broadcast_in_dim.12.scalars.refs_5_), channel_id=1, source_target_pairs={{0,12},{4,0},{8,4},{12,8},{1,13},{5,1},{9,5},{13,9},{2,14},{6,2},{... | collective-permute-start | bytes 12296 | tf_op jit(solution)/shard_map/ppermute | solution.py:584
  26.3 3.8 %collective-permute-start.6 = (f32[2,2,128,256]{3,2,1,0:T(8,128)S(1)}, f32[2,2,128,256]{3,2,1,0:T(8,128)S(1)}, u32[]{:S(2)}, u32[]{:S(2)}) collective-permute-start(f32[2,2,128,256]{3,2,1,0:T(8,128)S(1)} %get-tuple-element.63), channel_id=1, source_target_pairs={{0,1},{1,0},{2,3},{3,2},{4,5},{5,4},{6,7},{7,6},{8,9},{9,8},{10,11... | collective-permute-start | bytes 1572872 | tf_op jit(solution)/shard_map/ppermute | solution.py:529
  32.4 2.0 %collective-permute-start.7 = (f32[2,2,128,256]{3,2,1,0:T(8,128)S(1)}, f32[2,2,128,256]{3,2,1,0:T(8,128)S(1)}, u32[]{:S(2)}, u32[]{:S(2)}) collective-permute-start(f32[2,2,128,256]{3,2,1,0:T(8,128)S(1)} %get-tuple-element.72), channel_id=1, source_target_pairs={{0,1},{1,0},{2,3},{3,2},{4,5},{5,4},{6,7},{7,6},{8,9},{9,8},{10,11... | collective-permute-start | bytes 1572872 | tf_op jit(solution)/shard_map/ppermute | solution.py:529
  32.5 13.1 %collective-permute-start.12 = (f32[2,128,512]{2,1,0:T(8,128)S(1)}, f32[2,128,512]{2,1,0:T(8,128)S(1)}, u32[]{:S(2)}, u32[]{:S(2)}) collective-permute-start(f32[2,128,512]{2,1,0:T(8,128)S(1)} %get-tuple-element.80), channel_id=1, source_target_pairs={{0,2},{1,3},{2,0},{3,1},{4,6},{5,7},{6,4},{7,5},{8,10},{9,11},{10,... | collective-permute-start | bytes 1572872 | tf_op jit(solution)/shard_map/ppermute | solution.py:529
  36.8 31.6 %collective-permute-start.8 = (f32[2,152,256]{2,1,0:T(8,128)S(1)}, f32[2,152,256]{2,1,0:T(8,128)S(1)}, u32[]{:S(2)}, u32[]{:S(2)}) collective-permute-start(f32[2,152,256]{2,1,0:T(8,128)S(1)} %get-tuple-element.75), channel_id=1, source_target_pairs={{0,4},{1,5},{2,6},{3,7},{4,8},{5,9},{6,10},{7,11},{8,12},{9,13},{1... | collective-permute-start | bytes 933896 | tf_op jit(solution)/shard_map/ppermute | solution.py:537
  36.8 31.5 %collective-permute-start.9 = (f32[2,144,256]{2,1,0:T(8,128)S(1)}, f32[2,144,256]{2,1,0:T(8,128)S(1)}, u32[]{:S(2)}, u32[]{:S(2)}) collective-permute-start(f32[2,144,256]{2,1,0:T(8,128)S(1)} %get-tuple-element.76), channel_id=1, source_target_pairs={{0,5},{1,4},{2,7},{3,6},{4,9},{5,8},{6,11},{7,10},{8,13},{9,12},{1... | collective-permute-start | bytes 884744 | tf_op jit(solution)/shard_map/ppermute | solution.py:537
  38.2 30.1 %collective-permute-start.10 = (f32[2,144,256]{2,1,0:T(8,128)S(1)}, f32[2,144,256]{2,1,0:T(8,128)S(1)}, u32[]{:S(2)}, u32[]{:S(2)}) collective-permute-start(f32[2,144,256]{2,1,0:T(8,128)S(1)} %get-tuple-element.77), channel_id=1, source_target_pairs={{0,6},{1,7},{2,4},{3,5},{4,10},{5,11},{6,8},{7,9},{8,14},{9,15},{1... | collective-permute-start | bytes 884744 | tf_op jit(solution)/shard_map/ppermute | solution.py:537
  42.2 26.1 %collective-permute-start.11 = (f32[2,144,256]{2,1,0:T(8,128)S(1)}, f32[2,144,256]{2,1,0:T(8,128)S(1)}, u32[]{:S(2)}, u32[]{:S(2)}) collective-permute-start(f32[2,144,256]{2,1,0:T(8,128)S(1)} %get-tuple-element.78), channel_id=1, source_target_pairs={{0,7},{1,6},{2,5},{3,4},{4,11},{5,10},{6,9},{7,8},{8,15},{9,14},{1... | collective-permute-start | bytes 884744 | tf_op jit(solution)/shard_map/ppermute | solution.py:537
  47.4 2.3 %collective-permute-start.13 = (f32[5,8,512]{2,1,0:T(8,128)S(1)}, f32[5,8,512]{2,1,0:T(8,128)S(1)}, u32[]{:S(2)}, u32[]{:S(2)}) collective-permute-start(f32[5,8,512]{2,1,0:T(8,128)S(1)} %get-tuple-element.81), channel_id=1, source_target_pairs={{0,1},{1,0},{2,3},{3,2},{4,5},{5,4},{6,7},{7,6},{8,9},{9,8},{10,11... | collective-permute-start | bytes 245768 | tf_op jit(solution)/shard_map/ppermute | solution.py:529
  49.6 18.4 %collective-permute-start.14 = (f32[5,8,512]{2,1,0:T(8,128)S(1)}, f32[5,8,512]{2,1,0:T(8,128)S(1)}, u32[]{:S(2)}, u32[]{:S(2)}) collective-permute-start(f32[5,8,512]{2,1,0:T(8,128)S(1)} %get-tuple-element.82), channel_id=1, source_target_pairs={{1,2},{2,1},{5,6},{6,5},{9,10},{10,9},{13,14},{14,13},{17,18},{18,... | collective-permute-start | bytes 245768 | tf_op jit(solution)/shard_map/ppermute | solution.py:660
